TPU v7x, 32 devices: a whole 2x2x4 slice. The times are simulated.
32 devices in a mesh: row: 8 (over z, y), col: 4 (over x, core).
Axes of the slice: x: 2, y: 2, z: 4, core: 2. Of those that a mesh axis runs over, the one named last changes fastest.
Arguments:
- panel_one: bfloat16 [512, 8192], P('col', 'row'), may hold values from -1.1953125 to 1.1953125
- panel_two: bfloat16 [512, 8192], P('col', 'row'), may hold values from -3 to 3
- inverse_one: bfloat16 [512, 512], replicated
- inverse_two: bfloat16 [512, 512], replicated
- column_blocks: int32 [4], replicated, may hold values from 0 to 63, as said below
- row_map: int32 [64], P('row'), may hold values from 0 to 63, as said below
- targets: bfloat16 [8, 4, 128, 128, 128], P('row', 'col'), may hold values from -6 to 6
- rows_one: int32 [8, 4, 128], P('row', 'col'), may hold values from 0 to 63, as said below
- cols_one: int32 [8, 4, 128], P('row', 'col'), may hold values from 0 to 63, as said below
- rows_two: int32 [8, 4, 128], P('row', 'col'), may hold values from 0 to 63, as said below
- cols_two: int32 [8, 4, 128], P('row', 'col'), may hold values from 0 to 63, as said below
Outputs:
- lower_one: bfloat16 [512, 8192], P('col', 'row')
- lower_two: bfloat16 [512, 8192], P('col', 'row')
- trailing: bfloat16 [8, 4, 128, 128, 128], P('row', 'col')
Inputs may be any that keep to these rules, and one draw needn't show every extreme that they name: `column_blocks`: the entries are distinct. row_map[j] // 8 equals j // 8; within each aligned run of 8 entries every value of the run appears once. rows_one[r, c, s] // 8 equals r. cols_one[r, c, s] % 4 equals c. rows_two[r, c, s] // 8 equals r. cols_two[r, c, s] % 4 equals c.
All inputs are finite; a program needn't handle non-finite values.
Results may differ from a plain program's by a relative error of at most 0.006.
Values may be sent and summed in bfloat16 or wider, within the bound.
No kernel may reach another device: no remote copies, remote signals or barrier semaphores. Data moves between devices by JAX's collectives and lax.ppermute only.
A program may use at most 192 MiB of HBM per device.

v0:
```python
import jax
import jax.numpy as jnp
from jax import lax
from jax.sharding import PartitionSpec as P


def factor_panel(panel_part, inverse):
    summed = jnp.dot(
        inverse,
        lax.all_gather(panel_part, "col", axis=0, tiled=True),
        preferred_element_type=jnp.float32,
    )
    return summed.astype(jnp.bfloat16)


def bridge_columns(lower_full, column_blocks, slab_rows, block_size):
    local_count = lower_full.shape[1] // block_size
    begin_col = lax.axis_index("col") * slab_rows
    chosen = column_blocks[begin_col // block_size]
    offset = begin_col % block_size
    column_piece = lax.dynamic_slice_in_dim(
        lower_full, chosen % local_count * block_size + offset, slab_rows, 1
    )
    owner_row = chosen // local_count
    owned_here = owner_row == lax.axis_index("row")
    summed = lax.psum(
        jnp.where(owned_here, column_piece.astype(jnp.float32), 0.0).astype(jnp.bfloat16), "row"
    )
    return summed


def pick_tiles(lower_full, block_size):
    col_count = lax.axis_size("col")
    panel_width, row_count = lower_full.shape
    grouped = lower_full.reshape(
        panel_width, row_count // (block_size * col_count), col_count, block_size
    )
    chosen = lax.dynamic_index_in_dim(grouped, lax.axis_index("col"), 2, keepdims=False)
    return chosen.reshape(panel_width, -1)


def gather_tiles(lower_full, block_size):
    return lax.all_gather(pick_tiles(lower_full, block_size), "row", axis=1, tiled=True)


def schur_terms(lower_full, tiles, slot_rows, slot_cols, block_size):
    panel_width = lower_full.shape[0]
    local_blocks = lower_full.reshape(panel_width, -1, block_size)
    column_set = tiles.reshape(panel_width, -1, block_size)
    local_count = local_blocks.shape[1]
    left_tiles = jnp.take(local_blocks, slot_rows.reshape(-1) % local_count, axis=1)
    right_tiles = jnp.take(column_set, slot_cols.reshape(-1) // lax.axis_size("col"), axis=1)
    return jnp.einsum("wsx,wsy->sxy", left_tiles, right_tiles, preferred_element_type=jnp.float32)


def own_slice(lower_full, slab_rows):
    return lax.dynamic_slice_in_dim(lower_full, lax.axis_index("col") * slab_rows, slab_rows, 0)


def per_device(
    panel_one,
    panel_two,
    inverse_one,
    inverse_two,
    column_blocks,
    row_map,
    targets,
    rows_one,
    cols_one,
    rows_two,
    cols_two,
):
    block_size = targets.shape[-1]
    slab_rows = panel_one.shape[0]
    panel_width = inverse_one.shape[0]
    row_count = panel_one.shape[1]
    local_count = row_count // block_size
    lower_one = factor_panel(panel_one, inverse_one)
    blocks_one = lower_one.reshape(panel_width, local_count, block_size)
    bridge = bridge_columns(lower_one, column_blocks, slab_rows, block_size)
    mapped = jnp.take(blocks_one, row_map % local_count, axis=1).reshape(panel_width, row_count)
    update = lax.dot_general(
        bridge, mapped, (((0,), (0,)), ((), ())), preferred_element_type=jnp.float32
    )
    updated = (panel_two.astype(jnp.float32) - update).astype(jnp.bfloat16)
    lower_two = factor_panel(updated, inverse_two)
    tiles_one = gather_tiles(lower_one, block_size)
    tiles_two = gather_tiles(lower_two, block_size)
    terms = schur_terms(lower_one, tiles_one, rows_one, cols_one, block_size)
    terms = terms + schur_terms(lower_two, tiles_two, rows_two, cols_two, block_size)
    trailing = (
        (targets.astype(jnp.float32).reshape(terms.shape) - terms)
        .astype(jnp.bfloat16)
        .reshape(targets.shape)
    )
    return (own_slice(lower_one, slab_rows), own_slice(lower_two, slab_rows), trailing)


def solution(mesh):
    return jax.shard_map(
        per_device,
        mesh=mesh,
        in_specs=(
            P("col", "row"),
            P("col", "row"),
            P(),
            P(),
            P(),
            P("row"),
            P("row", "col", None, None, None),
            P("row", "col", None),
            P("row", "col", None),
            P("row", "col", None),
            P("row", "col", None),
        ),
        out_specs=(P("col", "row"), P("col", "row"), P("row", "col", None, None, None)),
        check_vma=False,
    )
```

profile of v0, /device:TPU:0, one launch (start us, length us, event | category | flops | bytes accessed | tf_op | source)
XLA Modules:
  0.0 258.9 jit_solution(3657992558839600060)
XLA Ops:
  7.2 0.0 copy-start
  7.2 0.0 copy-start.7
  7.2 0.0 copy-start.3
  7.2 0.0 copy-start.4
  7.2 0.0 copy-start.5
  7.2 0.0 copy-start.6
  7.2 0.0 all-gather.5.cloned.1.call-start
  7.3 0.7 all-gather.5.cloned.1.call-update
  8.0 0.0 all-reduce.2.cloned.1.call-start
  8.0 1.2 dynamic_slice.20
  11.9 0.7 compare_and_fusion.4
  12.6 0.1 broadcast_bitcast_fusion
  12.7 16.4 %all-gather.5.cloned.1.call-done = bf16[512,1024]{1,0:T(8,128)(2,1)} async-done(((bf16[128,1024]{1,0:T(8,128)(2,1)}), bf16[512,1024]{1,0:T(8,128)(2,1)}) %all-gather.5.cloned.1.call-update) | async-done | bytes 1048592 | tf_op jit(solution)/shard_map/all_gather | solution.py:10
  29.1 1.9 convolution_convert_fusion.1
  31.0 0.0 copy-start.2
  31.0 0.2 copy_bitcast_fusion
  31.2 0.8 select_convert_fusion
  32.0 0.0 all-reduce.2.cloned.1.call-update
  32.1 0.0 all-gather.7.cloned.1.call-start
  32.1 1.6 gather_fusion
  33.8 2.3 copy.21
  36.0 2.4 bitcast_select_fusion
  38.4 64.2 %all-reduce.2.cloned.1.call-done = bf16[512,128]{1,0:T(8,128)(2,1)} async-done(((bf16[512,128]{1,0:T(8,128)(2,1)}), bf16[512,128]{1,0:T(8,128)(2,1)}) %all-reduce.2.cloned.1.call-update) | async-done | bytes 131088 | tf_op jit(solution)/shard_map/psum | solution.py:26
  102.6 2.5 fusion.23
  105.1 0.0 all-gather.7.cloned.1.call-update
  105.1 0.0 all-gather.9.cloned.1.call-start
  105.2 1.6 reshape.76
  106.8 1.8 constant_dynamic-slice_fusion.1
  108.5 1.3 copy.29
  109.8 0.0 all-gather.9.cloned.1.call-update
  109.9 0.2 all-gather.11.cloned.1.call-start
  110.1 0.0 copy-done.2
  110.1 11.2 %all-gather.7.cloned.1.call-done = bf16[512,1024]{1,0:T(8,128)(2,1)} async-done(((bf16[128,1024]{1,0:T(8,128)(2,1)}), bf16[512,1024]{1,0:T(8,128)(2,1)}) %all-gather.7.cloned.1.call-update) | async-done | bytes 1048592 | tf_op jit(solution)/shard_map/all_gather | solution.py:10
  121.3 2.0 convolution_convert_fusion
  123.3 0.7 constant_dynamic-slice_fusion
  124.0 0.0 all-gather.11.cloned.1.call-update
  124.2 8.2 %gather_fusion.1 = bf16[128,512,128]{2,1,0:T(8,128)(2,1)} fusion(bf16[512,8,128]{2,0,1:T(8,128)(2,1)S(1)} %copy_bitcast_fusion, s32[1024]{0:T(1024)S(1)} %pad_clamp_fusion.3), kind=kCustom, calls=%fused_computation.clone | custom fusion | bytes 33554944 | tf_op jit(solution)/shard_map/jit(_take)/gather | solution.py:51
  132.4 1.7 constant_dynamic-slice_fusion.2
  134.1 0.8 copy.27
  135.0 8.2 %gather_fusion.3 = bf16[128,512,128]{1,2,0:T(8,128)(2,1)} fusion(bf16[512,8,128]{0,2,1:T(8,128)(2,1)S(1)} %bitcast.78, s32[1024]{0:T(1024)S(1)} %pad_clamp_fusion.1), kind=kCustom, calls=%fused_computation.2.clone | custom fusion | bytes 33554944 | tf_op jit(solution)/shard_map/jit(_take)/gather | solution.py:51
  143.2 29.6 %all-gather.9.cloned.1.call-done = bf16[512,2048]{0,1:T(8,128)(2,1)} async-done(((bf16[512,256]{0,1:T(8,128)(2,1)}), bf16[512,2048]{0,1:T(8,128)(2,1)}) %all-gather.9.cloned.1.call-update) | async-done | bytes 2097168 | tf_op jit(solution)/shard_map/all_gather | solution.py:43
  172.8 3.0 %copy.24 = bf16[512,16,128]{2,0,1:T(8,128)(2,1)S(1)} copy(bf16[512,16,128]{0,2,1:T(8,128)(2,1)} %bitcast.80) | data formatting | bytes 4194304 | tf_op jit(solution)/shard_map/reshape | solution.py:49
  175.9 8.4 %gather_fusion.2 = bf16[128,512,128]{2,1,0:T(8,128)(2,1)} fusion(bf16[512,16,128]{2,0,1:T(8,128)(2,1)S(1)} %copy.24, s32[1024]{0:T(1024)S(1)} %pad_clamp_fusion.2), kind=kCustom, calls=%fused_computation.1.clone | custom fusion | bytes 33554944 | tf_op jit(solution)/shard_map/jit(_take)/gather | solution.py:52
  184.3 16.8 %fusion.3 = f32[128,128,128]{2,1,0:T(8,128)} fusion(bf16[128,512,128]{2,1,0:T(8,128)(2,1)} %gather_fusion.2, bf16[128,512,128]{2,1,0:T(8,128)(2,1)} %gather_fusion.1, pred[128]{0:T(512)(128)(4,1)S(1)} %get-tuple-element.20, pred[128]{0:T(512)(128)(4,1)S(1)} %get-tuple-element.26), kind=kOutput, calls=%fused_computation.8 | convolution fusion | flops 2164260864 | bytes 41943296 | tf_op jit(solution)/shard_map/wsx,wsy->sxy/dot_general | solution.py:53
  201.0 21.8 %all-gather.11.cloned.1.call-done = bf16[512,2048]{0,1:T(8,128)(2,1)} async-done(((bf16[512,256]{0,1:T(8,128)(2,1)}), bf16[512,2048]{0,1:T(8,128)(2,1)}) %all-gather.11.cloned.1.call-update) | async-done | bytes 2097168 | tf_op jit(solution)/shard_map/all_gather | solution.py:43
  222.8 3.0 %copy.26 = bf16[512,16,128]{2,0,1:T(8,128)(2,1)S(1)} copy(bf16[512,16,128]{0,2,1:T(8,128)(2,1)} %bitcast.81) | data formatting | bytes 4194304 | tf_op jit(solution)/shard_map/reshape | solution.py:49
  225.9 8.3 %gather_fusion.4 = bf16[128,512,128]{2,1,0:T(8,128)(2,1)} fusion(bf16[512,16,128]{2,0,1:T(8,128)(2,1)S(1)} %copy.26, s32[1024]{0:T(1024)S(1)} %pad_clamp_fusion), kind=kCustom, calls=%fused_computation.3.clone | custom fusion | bytes 33554944 | tf_op jit(solution)/shard_map/jit(_take)/gather | solution.py:52
  234.2 18.2 %fusion.18 = bf16[1,1,128,128,128]{4,3,2,1,0:T(8,128)(2,1)} fusion(f32[128,128,128]{2,1,0:T(8,128)} %fusion.3, bf16[1,1,128,128,128]{4,3,2,1,0:T(8,128)(2,1)} %param.21, bf16[128,512,128]{2,1,0:T(8,128)(2,1)} %gather_fusion.4, pred[128]{0:T(512)(128)(4,1)S(1)} %get-tuple-element.16, bf16[128,512,128]{1,2,0:T(8,128)(2,1)} %gather_fusion.3, ...), kind=kOutput, calls=%fused_computation.24 | convolution fusion | flops 2172649472 | bytes 50331904 | tf_op jit(solution)/shard_map/wsx,wsy->sxy/dot_general | solution.py:53
  (16 shorter events, 0.1 us)
Async XLA Ops:
  7.2 21.9 %copy-start = (bf16[512,512]{1,0:T(8,128)(2,1)S(1)}, bf16[512,512]{1,0:T(8,128)(2,1)}, u32[]{:S(2)}) copy-start(bf16[512,512]{1,0:T(8,128)(2,1)} %param.17) | copy-start | bytes 1572868
  7.2 114.1 %copy-start.7 = (bf16[512,512]{1,0:T(8,128)(2,1)S(1)}, bf16[512,512]{1,0:T(8,128)(2,1)}, u32[]{:S(2)}) copy-start(bf16[512,512]{1,0:T(8,128)(2,1)} %param.18) | copy-start | bytes 1572868
  7.2 116.8 %copy-start.3 = (s32[1,1,128]{2,1,0:T(1,128)S(1)}, s32[1,1,128]{2,1,0:T(1,128)}, u32[]{:S(2)}) copy-start(s32[1,1,128]{2,1,0:T(1,128)} %param.23) | copy-start | bytes 1540
  7.2 116.8 %copy-start.4 = (s32[1,1,128]{2,1,0:T(1,128)S(1)}, s32[1,1,128]{2,1,0:T(1,128)}, u32[]{:S(2)}) copy-start(s32[1,1,128]{2,1,0:T(1,128)} %param.22) | copy-start | bytes 1540
  7.2 116.9 %copy-start.5 = (s32[1,1,128]{2,1,0:T(1,128)S(1)}, s32[1,1,128]{2,1,0:T(1,128)}, u32[]{:S(2)}) copy-start(s32[1,1,128]{2,1,0:T(1,128)} %param.25) | copy-start | bytes 1540
  7.2 116.9 %copy-start.6 = (s32[1,1,128]{2,1,0:T(1,128)S(1)}, s32[1,1,128]{2,1,0:T(1,128)}, u32[]{:S(2)}) copy-start(s32[1,1,128]{2,1,0:T(1,128)} %param.24) | copy-start | bytes 1540
  7.2 21.8 %all-gather.5.cloned.1.call-start = ((), (), s32[]{:S(2)}) async-start(), calls=%async_computation | async-start | bytes 1310720 | tf_op jit(solution)/shard_map/all_gather | solution.py:10
  8.0 94.7 %all-reduce.2.cloned.1.call-start = ((), (), s32[]{:S(2)}) async-start(), calls=%async_computation.1 | async-start | bytes 262144 | tf_op jit(solution)/shard_map/psum | solution.py:26
  31.0 79.1 %copy-start.2 = (bf16[512,1024]{1,0:T(8,128)(2,1)}, bf16[512,1024]{1,0:T(8,128)(2,1)S(1)}, u32[]{:S(2)}) copy-start(bf16[512,1024]{1,0:T(8,128)(2,1)S(1)} %convolution_convert_fusion.1) | copy-start | bytes 3145732
  32.1 89.2 %all-gather.7.cloned.1.call-start = ((), (), s32[]{:S(2)}) async-start(), calls=%async_computation.2 | async-start | bytes 1310720 | tf_op jit(solution)/shard_map/all_gather | solution.py:10
  105.1 67.7 %all-gather.9.cloned.1.call-start = ((), (), s32[]{:S(2)}) async-start(), calls=%async_computation.3 | async-start | bytes 2359296 | tf_op jit(solution)/shard_map/all_gather | solution.py:43
  109.9 113.0 %all-gather.11.cloned.1.call-start = ((), (), s32[]{:S(2)}) async-start(), calls=%async_computation.4 | async-start | bytes 2359296 | tf_op jit(solution)/shard_map/all_gather | solution.py:43
  234.2 18.2 %copy-start.1 = (bf16[512,512]{1,0:T(8,128)(2,1)S(1)}, bf16[512,512]{1,0:T(8,128)(2,1)}, u32[]{:S(2)}) copy-start(bf16[512,512]{1,0:T(8,128)(2,1)} %param.17) | copy-start | bytes 1572868
Sparse Core Ops, SparseCore 0:
  9.6 19.4 all-gather.4
  33.0 69.5 all-reduce.1
  105.3 15.9 all-gather.6
  123.5 49.2 all-gather.8
  175.0 47.7 all-gather.10
where the time goes:
time: 260 us; the launch traced here: 259 us
  waiting for transfers between devices  144 us (55%)
  local copies, waits for them, and re-layouts  52.6 us (20%)
  matrix products  41.4 us (16%)
  between operations  16.6 us (6%)
  other arithmetic  3.92 us (2%)
    psum x1, waiting for transfers between devices, bridge_columns(): lax.psum(jnp.where(owned_here, column_piece.astype(jnp.float32), 0.0).ast...  64.2 us
    all_gather x2, waiting for transfers between devices, gather_tiles(): lax.all_gather(pick_tiles(lower_full, block_size), 'row', axis=1, tiled=T...  51.4 us
    dot_general x2, matrix products, schur_terms(): jnp.einsum('wsx,wsy->sxy', left_tiles, right_tiles, preferred_element_typ...  35 us
    all_gather x2, waiting for transfers between devices, factor_panel(): lax.all_gather(panel_part, 'col', axis=0, tiled=True)  27.6 us
    gather x2, local copies, waits for them, and re-layouts, schur_terms(): jnp.take(column_set, slot_cols.reshape(-1) // lax.axis_size('col'), axis=1)  16.7 us
    gather x2, local copies, waits for them, and re-layouts, schur_terms(): jnp.take(local_blocks, slot_rows.reshape(-1) % local_count, axis=1)  16.5 us
    reshape x2, local copies, waits for them, and re-layouts, schur_terms(): column_set = tiles.reshape(panel_width, -1, block_size)  6.06 us
  transfers between devices with their start and end apart: 5, of which 5 were waited for; matrix products, arithmetic and copies ran while one was open for 24% of the time, Pallas kernels for 0%

commit v1 on v0

v1 whole, which is shorter than its diff:
```python
import functools

import jax
import jax.numpy as jnp
from jax import lax
from jax.experimental import pallas as pl
from jax.experimental.pallas import tpu as pltpu
from jax.sharding import PartitionSpec as P

VMEM = pl.BlockSpec(memory_space=pltpu.VMEM)
SMEM = pl.BlockSpec(memory_space=pltpu.SMEM)
F32 = jnp.float32
BF16 = jnp.bfloat16
TN = (((0,), (0,)), ((), ()))


def params(mib):
    return pltpu.CompilerParams(vmem_limit_bytes=mib << 20)


def xor_permute(value, axis, mask):
    return lax.ppermute(value, axis, [(i, i ^ mask) for i in range(lax.axis_size(axis))])


def xor_gather(value, axis):
    pieces = {0: value}
    bit = lax.axis_size(axis) // 2
    while bit:
        for m in list(pieces):
            pieces[m | bit] = xor_permute(pieces[m], axis, bit)
        bit //= 2
    return [pieces[m] for m in range(len(pieces))]


def xor_sum(value, axis):
    bit = 1
    while bit < lax.axis_size(axis):
        value = value + xor_permute(value, axis, bit)
        bit *= 2
    return value


def ring_order(count):
    return list(range(0, count, 2)) + list(range(count - 1, 0, -2))


def ring_gather(tile):
    count = lax.axis_size("row")
    order = ring_order(count)
    ahead = [(order[i], order[(i + 1) % count]) for i in range(count)]
    back = [(b, a) for a, b in ahead]
    forward, backward = [], []
    f = b = tile
    for _ in range(count // 2 - 1):
        f = lax.ppermute(f, "row", ahead)
        b = lax.ppermute(b, "row", back)
        forward.append(f)
        backward.append(b)
    half = tile.shape[0] // 2
    top = lax.ppermute(f[:half], "row", ahead)
    bottom = lax.ppermute(b[half:], "row", back)
    return [tile] + forward + [top, bottom] + backward[::-1]


def ring_distance(row):
    count = lax.axis_size("row")
    position = lambda r: jnp.where(r % 2 == 0, r // 2, count - 1 - r // 2)
    return (position(lax.axis_index("row")) - position(row)) % count


def bridge_kernel(block, local, blocks_ref, panel_ref, out_ref):
    row = lax.axis_index("row")
    for k in range(blocks_ref.shape[0]):
        chosen = blocks_ref[k]
        start = pl.multiple_of(chosen % local * block, block)
        piece = panel_ref[:, pl.ds(start, block)]
        keep = jnp.where(chosen // local == row, 1.0, 0.0).astype(BF16)
        out_ref[:, k * block : (k + 1) * block] = piece * keep


def bridge_columns(panel, column_blocks, block):
    slab = panel.shape[0]
    count = column_blocks.shape[0]
    return pl.pallas_call(
        functools.partial(bridge_kernel, block, panel.shape[1] // block),
        out_shape=jax.ShapeDtypeStruct((slab, count * block), BF16),
        in_specs=[SMEM, VMEM],
        out_specs=VMEM,
        name="bridge_columns",
    )(column_blocks, panel)


def assemble(pieces, full_ref):
    col = lax.axis_index("col")
    slab = pieces[0].shape[0]
    for m, piece in enumerate(pieces):
        start = pl.multiple_of((col ^ m) * slab, slab)
        full_ref[pl.ds(start, slab), :] = piece[...]


def store_parts(block, lower_ref, own_ref, tile_ref):
    col = lax.axis_index("col")
    slab = own_ref.shape[0]
    own_ref[...] = lower_ref[pl.ds(pl.multiple_of(col * slab, slab), slab), :]
    for t in range(tile_ref.shape[1] // block):
        start = pl.multiple_of((t * lax.axis_size("col") + col) * block, block)
        tile_ref[:, t * block : (t + 1) * block] = lower_ref[:, pl.ds(start, block)]


def multiply(left, right_ref, out_ref, step=256):
    for n in range(0, right_ref.shape[1], step):
        out_ref[:, n : n + step] = jnp.dot(
            left, right_ref[:, n : n + step], preferred_element_type=F32
        ).astype(out_ref.dtype)


def lower_one_kernel(block, *refs):
    inverse_ref, *pieces, lower_ref, own_ref, tile_ref, full_ref = refs
    assemble(pieces, full_ref)
    multiply(inverse_ref[...], full_ref, lower_ref)
    store_parts(block, lower_ref, own_ref, tile_ref)


def lower_shapes(width, slab, columns, block, cols):
    tiles = columns // block // cols
    return (
        jax.ShapeDtypeStruct((width, columns), BF16),
        jax.ShapeDtypeStruct((slab, columns), BF16),
        jax.ShapeDtypeStruct((width, tiles * block), BF16),
    )


def factor_one(inverse, pieces, block):
    width = inverse.shape[0]
    slab, columns = pieces[0].shape
    return pl.pallas_call(
        functools.partial(lower_one_kernel, block),
        out_shape=lower_shapes(width, slab, columns, block, len(pieces)),
        in_specs=[VMEM] * (1 + len(pieces)),
        out_specs=(VMEM,) * 3,
        scratch_shapes=[pltpu.VMEM((width, columns), BF16)],
        compiler_params=params(24),
        name="factor_one",
    )(inverse, *pieces)


def lower_two_kernel(block, count, *refs):
    map_ref, one_ref, two_ref, lower_one_ref = refs[:4]
    raw = refs[4 : 4 + count]
    pieces = refs[4 + count : 4 + 2 * count]
    lower_ref, own_ref, tile_ref, raw_ref, bridge_ref, mapped_ref, full_ref = refs[4 + 2 * count :]
    local = map_ref.shape[0]
    assemble(raw, raw_ref)
    assemble(pieces, full_ref)
    multiply(one_ref[...], raw_ref, bridge_ref)
    for j in range(local):
        start = pl.multiple_of(map_ref[j] % local * block, block)
        mapped_ref[:, j * block : (j + 1) * block] = lower_one_ref[:, pl.ds(start, block)]
    step = 256
    for n in range(0, full_ref.shape[1], step):
        update = lax.dot_general(
            bridge_ref[...], mapped_ref[:, n : n + step], TN, preferred_element_type=F32
        )
        mapped_ref[:, n : n + step] = (full_ref[:, n : n + step].astype(F32) - update).astype(BF16)
    multiply(two_ref[...], mapped_ref, lower_ref)
    store_parts(block, lower_ref, own_ref, tile_ref)


def factor_two(row_map, inverse_one, inverse_two, lower_one, raw, pieces, block):
    width = inverse_one.shape[0]
    slab, columns = pieces[0].shape
    count = len(pieces)
    return pl.pallas_call(
        functools.partial(lower_two_kernel, block, count),
        out_shape=lower_shapes(width, slab, columns, block, count),
        in_specs=[SMEM] + [VMEM] * (3 + 2 * count),
        out_specs=(VMEM,) * 3,
        scratch_shapes=[
            pltpu.VMEM((width, raw[0].shape[1]), BF16),
            pltpu.VMEM((width, raw[0].shape[1]), BF16),
            pltpu.VMEM((width, columns), BF16),
            pltpu.VMEM((width, columns), BF16),
        ],
        compiler_params=params(24),
        name="factor_two",
    )(row_map, inverse_one, inverse_two, lower_one, *raw, *pieces)


def transpose_kernel(block, in_ref, out_ref):
    for n in range(0, in_ref.shape[1], block):
        out_ref[n : n + block, :] = in_ref[:, n : n + block].T


def transposed(lower, block):
    return pl.pallas_call(
        functools.partial(transpose_kernel, block),
        out_shape=jax.ShapeDtypeStruct(lower.shape[::-1], BF16),
        in_specs=[VMEM],
        out_specs=VMEM,
        name="transposed",
    )(lower)


def schur_kernel(block, count, per_step, index_ref, left_ref, *refs):
    tiles = refs[: count + 1]
    base_ref, out_ref, products_ref = refs[count + 1 :]
    local = left_ref.shape[0] // block
    each = tiles[0].shape[1] // block
    half = left_ref.shape[1] // 2

    def store(distance, product):
        for t in range(each):
            for a in range(local):
                products_ref[(distance * each + t) * local + a] = product[
                    a * block : (a + 1) * block, t * block : (t + 1) * block
                ]

    @pl.when(pl.program_id(0) == 0)
    def _():
        for distance in range(count):
            if distance == count // 2:
                product = jnp.dot(
                    left_ref[:, :half], tiles[distance][...], preferred_element_type=F32
                )
                product = product + jnp.dot(
                    left_ref[:, half:], tiles[distance + 1][...], preferred_element_type=F32
                )
            else:
                tile = tiles[distance + (distance > count // 2)]
                product = jnp.dot(left_ref[...], tile[...], preferred_element_type=F32)
            store(distance, product)

    first = pl.program_id(0) * per_step
    for s in range(per_step):
        term = products_ref[index_ref[first + s]]
        out_ref[s] = (base_ref[s].astype(F32) - term).astype(out_ref.dtype)


def schur(index, left, tiles, base, dtype, per_step=16):
    slots, block, _ = base.shape
    count = len(tiles) - 1
    local = left.shape[0] // block
    each = tiles[0].shape[1] // block
    whole = lambda a: pl.BlockSpec(a.shape, lambda i, idx: (0, 0), pipeline_mode=pl.Buffered(1))
    moving = pl.BlockSpec((per_step, block, block), lambda i, idx: (i, 0, 0))
    return pl.pallas_call(
        functools.partial(schur_kernel, block, count, per_step),
        out_shape=jax.ShapeDtypeStruct(base.shape, dtype),
        grid_spec=pltpu.PrefetchScalarGridSpec(
            num_scalar_prefetch=1,
            grid=(slots // per_step,),
            in_specs=[whole(left)] + [whole(t) for t in tiles] + [moving],
            out_specs=moving,
            scratch_shapes=[pltpu.VMEM((count * each * local, block, block), F32)],
        ),
        compiler_params=params(40),
        name="schur",
    )(index, left, *tiles, base)


def slot_index(rows, cols, local):
    rows, cols = rows.reshape(-1), cols.reshape(-1)
    parts = lax.axis_size("col")
    tile = cols % local // parts
    return (ring_distance(cols // local) * (local // parts) + tile) * local + rows % local


def per_device(
    panel_one,
    panel_two,
    inverse_one,
    inverse_two,
    column_blocks,
    row_map,
    targets,
    rows_one,
    cols_one,
    rows_two,
    cols_two,
):
    block = targets.shape[-1]
    local = panel_one.shape[1] // block
    raw = xor_sum(bridge_columns(panel_one, column_blocks, block), "row")
    pieces_one = xor_gather(panel_one, "col")
    pieces_two = xor_gather(panel_two, "col")
    lower_one, own_one, tile_one = factor_one(inverse_one, pieces_one, block)
    tiles_one = ring_gather(tile_one)
    raw = xor_gather(raw, "col")
    lower_two, own_two, tile_two = factor_two(
        row_map, inverse_one, inverse_two, lower_one, raw, pieces_two, block
    )
    tiles_two = ring_gather(tile_two)
    base = targets.reshape(-1, block, block)
    part = schur(
        slot_index(rows_one, cols_one, local), transposed(lower_one, block), tiles_one, base, F32
    )
    trailing = schur(
        slot_index(rows_two, cols_two, local), transposed(lower_two, block), tiles_two, part, BF16
    )
    return own_one, own_two, trailing.reshape(targets.shape)


def solution(mesh):
    return jax.shard_map(
        per_device,
        mesh=mesh,
        in_specs=(
            P("col", "row"),
            P("col", "row"),
            P(),
            P(),
            P(),
            P("row"),
            P("row", "col", None, None, None),
            P("row", "col", None),
            P("row", "col", None),
            P("row", "col", None),
            P("row", "col", None),
        ),
        out_specs=(P("col", "row"), P("col", "row"), P("row", "col", None, None, None)),
        check_vma=False,
    )
```

time: 260 us -> 104 us (0.40)
  waiting for transfers between devices: 144 us -> 30 us
  matrix products: 41.4 us -> 0 us
  local copies, waits for them, and re-layouts: 52.6 us -> 15.8 us
  Pallas kernels: 0 us -> 28.1 us
  starting transfers between devices: 0.38 us -> 28 us
  between operations: 16.6 us -> 0.77 us
  other arithmetic: 3.92 us -> 1.07 us
    all_gather x4 -> x0, waiting for transfers between devices: 79 us -> none  [the longest x2 51.4 us: gather_tiles(): lax.all_gather(pick_tiles(lower_full, block_size), 'row', axis=1, tiled=T...]
    psum x1 -> x0, waiting for transfers between devices: 64.2 us -> none  [bridge_columns(): lax.psum(jnp.where(owned_here, column_piece.astype(jnp.float32), 0.0).ast...]
    dot_general x5 -> x0, matrix products: 41.4 us -> none  [the longest x2 35 us: schur_terms(): jnp.einsum('wsx,wsy->sxy', left_tiles, right_tiles, preferred_element_typ...]
    gather x6 -> x0, local copies, waits for them, and re-layouts: 37.1 us -> none  [the longest x2 16.7 us: schur_terms(): jnp.take(column_set, slot_cols.reshape(-1) // lax.axis_size('col'), axis=1)]
    ppermute x0 -> x28, waiting for transfers between devices: none -> 30 us  [the longest x6 17.3 us: ring_gather(): b = lax.ppermute(b, 'row', back)]
    pallas_call x0 -> x7, Pallas kernels: none -> 28.1 us  [the longest x2 16.5 us: schur(): pl.pallas_call(functools.partial(schur_kernel, block, count, per_step), o...]
    ppermute x0 -> x28, starting transfers between devices: none -> 28 us  [the longest x12 11.8 us: xor_permute(): lax.ppermute(value, axis, [(i, i ^ mask) for i in range(lax.axis_size(axi...]
    unnamed x18 -> x34, local copies, waits for them, and re-layouts: 2.21 us -> 13.1 us
  transfers between devices with their start and end apart: 5 -> 28, of which waited for: 5 -> 10; matrix products, arithmetic and copies ran while one was open for 24% -> 4% of each run, Pallas kernels for 0% -> 18%
where the time goes in v1:
time: 104 us
  waiting for transfers between devices  30 us (29%)
  Pallas kernels  28.1 us (27%)
  starting transfers between devices  28 us (27%)
  local copies, waits for them, and re-layouts  15.8 us (15%)
  other arithmetic  1.07 us (1%)
    ppermute x6, waiting for transfers between devices, ring_gather(): b = lax.ppermute(b, 'row', back)  17.3 us
    pallas_call x2, Pallas kernels, schur(): pl.pallas_call(functools.partial(schur_kernel, block, count, per_step), o...  16.5 us
    unnamed x34, local copies, waits for them, and re-layouts  13.1 us
    ppermute x12, waiting for transfers between devices, xor_permute(): lax.ppermute(value, axis, [(i, i ^ mask) for i in range(lax.axis_size(axi...  12.6 us
    ppermute x12, starting transfers between devices, xor_permute(): lax.ppermute(value, axis, [(i, i ^ mask) for i in range(lax.axis_size(axi...  11.8 us
    ppermute x6, starting transfers between devices, ring_gather(): b = lax.ppermute(b, 'row', back)  8.89 us
    pallas_call x2, Pallas kernels, transposed(): pl.pallas_call(functools.partial(transpose_kernel, block), out_shape=jax....  5.05 us
    ppermute x6, starting transfers between devices, ring_gather(): f = lax.ppermute(f, 'row', ahead)  3.27 us
  transfers between devices with their start and end apart: 28, of which 10 were waited for; matrix products, arithmetic and copies ran while one was open for 4% of the time, Pallas kernels for 18%

profile of v1, /device:TPU:0, one launch (start us, length us, event | category | flops | bytes accessed | tf_op | source)
XLA Modules:
  0.0 103.7 jit_solution(5762901724500713597)
XLA Ops:
  0.7 1.7 %bridge_columns.1 = bf16[128,512]{1,0:T(8,128)(2,1)} custom-call(s32[4]{0:T(128)} %blocks_ref.1, bf16[128,1024]{1,0:T(8,128)(2,1)} %panel_ref.1), custom_call_target="tpu_custom_call" | custom-call | tf_op jit(solution)/shard_map/bridge_columns/pallas_call | solution.py:84
  2.4 3.0 %collective-permute-start.3 = (bf16[128,512]{1,0:T(8,128)(2,1)}, bf16[128,512]{1,0:T(8,128)(2,1)S(1)}, u32[]{:S(2)}, u32[]{:S(2)}) collective-permute-start(bf16[128,512]{1,0:T(8,128)(2,1)} %bridge_columns.1), channel_id=1, source_target_pairs={{0,4},{4,0},{8,12},{12,8},{16,20},{20,16},{24,28},{28,24},{1,5},{5... | collective-permute-start | bytes 393224 | tf_op jit(solution)/shard_map/ppermute | solution.py:22
  5.3 1.5 %collective-permute-start.1 = (bf16[128,1024]{1,0:T(8,128)(2,1)}, bf16[128,1024]{1,0:T(8,128)(2,1)S(1)}, u32[]{:S(2)}, u32[]{:S(2)}) collective-permute-start(bf16[128,1024]{1,0:T(8,128)(2,1)} %panel_ref.1), channel_id=1, source_target_pairs={{0,2},{1,3},{2,0},{3,1},{4,6},{5,7},{6,4},{7,5},{8,10},{9,11},{10,... | collective-permute-start | bytes 786440 | tf_op jit(solution)/shard_map/ppermute | solution.py:22
  7.4 1.7 %collective-permute-done.3 = bf16[128,512]{1,0:T(8,128)(2,1)S(1)} collective-permute-done((bf16[128,512]{1,0:T(8,128)(2,1)}, bf16[128,512]{1,0:T(8,128)(2,1)S(1)}, u32[]{:S(2)}, u32[]{:S(2)}) %collective-permute-start.3) | collective-permute-done | bytes 131104 | tf_op jit(solution)/shard_map/ppermute | solution.py:22
  9.0 0.9 add.67
  10.0 1.9 %collective-permute-start.4 = (bf16[128,512]{1,0:T(8,128)(2,1)S(1)}, bf16[128,512]{1,0:T(8,128)(2,1)S(1)}, u32[]{:S(2)}, u32[]{:S(2)}) collective-permute-start(bf16[128,512]{1,0:T(8,128)(2,1)S(1)} %add.67), channel_id=1, source_target_pairs={{0,8},{4,12},{8,0},{12,4},{16,24},{20,28},{24,16},{28,20},{1,9},{5... | collective-permute-start | bytes 393224 | tf_op jit(solution)/shard_map/ppermute | solution.py:22
  11.8 3.2 %collective-permute-done.4 = bf16[128,512]{1,0:T(8,128)(2,1)S(1)} collective-permute-done((bf16[128,512]{1,0:T(8,128)(2,1)S(1)}, bf16[128,512]{1,0:T(8,128)(2,1)S(1)}, u32[]{:S(2)}, u32[]{:S(2)}) %collective-permute-start.4) | collective-permute-done | bytes 131104 | tf_op jit(solution)/shard_map/ppermute | solution.py:22
  15.0 2.9 %collective-permute-start.5 = (bf16[128,512]{1,0:T(8,128)(2,1)S(1)}, bf16[128,512]{1,0:T(8,128)(2,1)S(1)}, u32[]{:S(2)}, u32[]{:S(2)}) collective-permute-start(bf16[128,512]{1,0:T(8,128)(2,1)S(1)} %add.68), channel_id=1, source_target_pairs={{0,16},{4,20},{8,24},{12,28},{16,0},{20,4},{24,8},{28,12},{1,17},{... | collective-permute-start | bytes 393224 | tf_op jit(solution)/shard_map/ppermute | solution.py:22
  18.9 3.7 %collective-permute-done.5 = bf16[128,512]{1,0:T(8,128)(2,1)S(1)} collective-permute-done((bf16[128,512]{1,0:T(8,128)(2,1)S(1)}, bf16[128,512]{1,0:T(8,128)(2,1)S(1)}, u32[]{:S(2)}, u32[]{:S(2)}) %collective-permute-start.5) | collective-permute-done | bytes 131104 | tf_op jit(solution)/shard_map/ppermute | solution.py:22
  22.7 1.5 %collective-permute-start.7 = (bf16[128,512]{1,0:T(8,128)(2,1)S(1)}, bf16[128,512]{1,0:T(8,128)(2,1)S(1)}, u32[]{:S(2)}, u32[]{:S(2)}) collective-permute-start(bf16[128,512]{1,0:T(8,128)(2,1)S(1)} %add.69.refs_4_), channel_id=1, source_target_pairs={{0,2},{1,3},{2,0},{3,1},{4,6},{5,7},{6,4},{7,5},{8,10},{9,11},{10,... | collective-permute-start | bytes 393224 | tf_op jit(solution)/shard_map/ppermute | solution.py:22
  24.2 3.5 %collective-permute-done.7.refs_6_ = bf16[128,512]{1,0:T(8,128)(2,1)S(1)} collective-permute-done((bf16[128,512]{1,0:T(8,128)(2,1)S(1)}, bf16[128,512]{1,0:T(8,128)(2,1)S(1)}, u32[]{:S(2)}, u32[]{:S(2)}) %collective-permute-start.7) | collective-permute-done | bytes 131104 | tf_op jit(solution)/shard_map/ppermute | solution.py:22
  27.7 1.0 %copy-done.5 = bf16[512,512]{1,0:T(8,128)(2,1)S(1)} copy-done((bf16[512,512]{1,0:T(8,128)(2,1)S(1)}, bf16[512,512]{1,0:T(8,128)(2,1)}, u32[]{:S(2)}) %copy-start.5) | copy-done | bytes 524312
  28.8 0.9 copy-done.7
  29.7 1.6 %factor_one.1 = (bf16[512,1024]{1,0:T(8,128)(2,1)S(1)}, bf16[128,1024]{1,0:T(8,128)(2,1)}, bf16[512,256]{1,0:T(8,128)(2,1)S(1)}) custom-call(bf16[512,512]{1,0:T(8,128)(2,1)S(1)} %copy-done.5, bf16[128,1024]{1,0:T(8,128)(2,1)S(1)} %copy-done.7, bf16[128,1024]{1,0:T(8,128)(2,1)S(1)} %collective-permute-done.refs_2_, ...), custom_call_target="tpu_custom_call" | custom-call | tf_op jit(solution)/shard_map/factor_one/pallas_call | solution.py:136
  31.3 1.5 %collective-permute-start.24 = (bf16[512,256]{1,0:T(8,128)(2,1)S(1)}, bf16[512,256]{1,0:T(8,128)(2,1)S(1)}, u32[]{:S(2)}, u32[]{:S(2)}) collective-permute-start(bf16[512,256]{1,0:T(8,128)(2,1)S(1)} %get-tuple-element.14.refs_0_), channel_id=1, source_target_pairs={{8,0},{16,8},{24,16},{28,24},{20,28},{12,20},{4,12},{0,4},{9,1},{1... | collective-permute-start | bytes 786440 | tf_op jit(solution)/shard_map/ppermute | solution.py:56
  32.8 0.5 collective-permute-start.20
  33.4 1.0 copy-done.8
  34.4 0.9 copy-done.11
  35.4 0.7 copy-done.12
  36.0 3.2 %factor_two.1 = (bf16[512,1024]{1,0:T(8,128)(2,1)S(1)}, bf16[128,1024]{1,0:T(8,128)(2,1)}, bf16[512,256]{1,0:T(8,128)(2,1)S(1)}) custom-call(s32[8]{0:T(128)S(1)} %copy-done.12, bf16[512,512]{1,0:T(8,128)(2,1)S(1)} %copy-done.5, bf16[512,512]{1,0:T(8,128)(2,1)S(1)} %copy-done.8, bf16[512,1024]{1,0:T(8,128)(2,1)S(1)} %get-tuple-element.10.refs_3_.in_ref, ...), custom_call_target="tpu_custom_call" | custom-call | tf_op jit(solution)/shard_map/factor_two/pallas_call | solution.py:173
  39.2 1.0 copy-done.6
  40.2 1.5 %collective-permute-start.16 = (bf16[512,256]{1,0:T(8,128)(2,1)S(1)}, bf16[512,256]{1,0:T(8,128)(2,1)S(1)}, u32[]{:S(2)}, u32[]{:S(2)}) collective-permute-start(bf16[512,256]{1,0:T(8,128)(2,1)S(1)} %get-tuple-element.13.refs_0_), channel_id=1, source_target_pairs={{8,0},{16,8},{24,16},{28,24},{20,28},{12,20},{4,12},{0,4},{9,1},{1... | collective-permute-start | bytes 786440 | tf_op jit(solution)/shard_map/ppermute | solution.py:56
  41.7 0.5 collective-permute-start.12
  42.2 1.5 %collective-permute-start.25 = (bf16[512,256]{1,0:T(8,128)(2,1)S(1)}, bf16[512,256]{1,0:T(8,128)(2,1)}, u32[]{:S(2)}, u32[]{:S(2)}) collective-permute-start(bf16[512,256]{1,0:T(8,128)(2,1)S(1)} %collective-permute-done.24.refs_8_), channel_id=1, source_target_pairs={{8,0},{16,8},{24,16},{28,24},{20,28},{12,20},{4,12},{0,4},{9,1},{1... | collective-permute-start | bytes 786440 | tf_op jit(solution)/shard_map/ppermute | solution.py:56
  43.7 0.5 collective-permute-start.21
  44.3 5.1 %collective-permute-done.16.refs_8_ = bf16[512,256]{1,0:T(8,128)(2,1)S(1)} collective-permute-done((bf16[512,256]{1,0:T(8,128)(2,1)S(1)}, bf16[512,256]{1,0:T(8,128)(2,1)S(1)}, u32[]{:S(2)}, u32[]{:S(2)}) %collective-permute-start.16) | collective-permute-done | bytes 262176 | tf_op jit(solution)/shard_map/ppermute | solution.py:56
  49.4 1.5 %collective-permute-start.17 = (bf16[512,256]{1,0:T(8,128)(2,1)S(1)}, bf16[512,256]{1,0:T(8,128)(2,1)}, u32[]{:S(2)}, u32[]{:S(2)}) collective-permute-start(bf16[512,256]{1,0:T(8,128)(2,1)S(1)} %collective-permute-done.16.refs_8_), channel_id=1, source_target_pairs={{8,0},{16,8},{24,16},{28,24},{20,28},{12,20},{4,12},{0,4},{9,1},{1... | collective-permute-start | bytes 786440 | tf_op jit(solution)/shard_map/ppermute | solution.py:56
  50.9 0.5 collective-permute-start.13
  51.4 0.7 copy-done.9
  52.2 2.9 %collective-permute-done.25.refs_7_ = bf16[512,256]{1,0:T(8,128)(2,1)} collective-permute-done((bf16[512,256]{1,0:T(8,128)(2,1)S(1)}, bf16[512,256]{1,0:T(8,128)(2,1)}, u32[]{:S(2)}, u32[]{:S(2)}) %collective-permute-start.25) | collective-permute-done | bytes 262176 | tf_op jit(solution)/shard_map/ppermute | solution.py:56
  55.1 1.5 %collective-permute-start.26 = (bf16[512,256]{1,0:T(8,128)(2,1)}, bf16[512,256]{1,0:T(8,128)(2,1)S(1)}, u32[]{:S(2)}, u32[]{:S(2)}) collective-permute-start(bf16[512,256]{1,0:T(8,128)(2,1)} %collective-permute-done.25.refs_7_), channel_id=1, source_target_pairs={{8,0},{16,8},{24,16},{28,24},{20,28},{12,20},{4,12},{0,4},{9,1},{1... | collective-permute-start | bytes 786440 | tf_op jit(solution)/shard_map/ppermute | solution.py:56
  57.2 3.6 %collective-permute-done.17.refs_7_ = bf16[512,256]{1,0:T(8,128)(2,1)} collective-permute-done((bf16[512,256]{1,0:T(8,128)(2,1)S(1)}, bf16[512,256]{1,0:T(8,128)(2,1)}, u32[]{:S(2)}, u32[]{:S(2)}) %collective-permute-start.17) | collective-permute-done | bytes 262176 | tf_op jit(solution)/shard_map/ppermute | solution.py:56
  60.7 1.5 %collective-permute-start.18 = (bf16[512,256]{1,0:T(8,128)(2,1)}, bf16[512,256]{1,0:T(8,128)(2,1)S(1)}, u32[]{:S(2)}, u32[]{:S(2)}) collective-permute-start(bf16[512,256]{1,0:T(8,128)(2,1)} %collective-permute-done.17.refs_7_), channel_id=1, source_target_pairs={{8,0},{16,8},{24,16},{28,24},{20,28},{12,20},{4,12},{0,4},{9,1},{1... | collective-permute-start | bytes 786440 | tf_op jit(solution)/shard_map/ppermute | solution.py:56
  62.8 3.4 %collective-permute-done.26.refs_6_ = bf16[512,256]{1,0:T(8,128)(2,1)S(1)} collective-permute-done((bf16[512,256]{1,0:T(8,128)(2,1)}, bf16[512,256]{1,0:T(8,128)(2,1)S(1)}, u32[]{:S(2)}, u32[]{:S(2)}) %collective-permute-start.26) | collective-permute-done | bytes 262176 | tf_op jit(solution)/shard_map/ppermute | solution.py:56
  66.2 0.7 slice.19
  66.9 1.5 %collective-permute-start.27 = (bf16[256,256]{1,0:T(8,128)(2,1)}, bf16[256,256]{1,0:T(8,128)(2,1)}, u32[]{:S(2)}, u32[]{:S(2)}) collective-permute-start(bf16[256,256]{1,0:T(8,128)(2,1)} %slice.19), channel_id=1, source_target_pairs={{8,0},{16,8},{24,16},{28,24},{20,28},{12,20},{4,12},{0,4},{9,1},{1... | collective-permute-start | bytes 393224 | tf_op jit(solution)/shard_map/ppermute | solution.py:61
  68.4 0.7 slice.18
  69.6 2.3 %collective-permute-done.18.refs_6_ = bf16[512,256]{1,0:T(8,128)(2,1)S(1)} collective-permute-done((bf16[512,256]{1,0:T(8,128)(2,1)}, bf16[512,256]{1,0:T(8,128)(2,1)S(1)}, u32[]{:S(2)}, u32[]{:S(2)}) %collective-permute-start.18) | collective-permute-done | bytes 262176 | tf_op jit(solution)/shard_map/ppermute | solution.py:56
  71.8 0.7 slice.17
  72.5 1.5 %collective-permute-start.19 = (bf16[256,256]{1,0:T(8,128)(2,1)}, bf16[256,256]{1,0:T(8,128)(2,1)S(1)}, u32[]{:S(2)}, u32[]{:S(2)}) collective-permute-start(bf16[256,256]{1,0:T(8,128)(2,1)} %slice.17), channel_id=1, source_target_pairs={{8,0},{16,8},{24,16},{28,24},{20,28},{12,20},{4,12},{0,4},{9,1},{1... | collective-permute-start | bytes 393224 | tf_op jit(solution)/shard_map/ppermute | solution.py:61
  74.0 0.7 slice.16
  75.2 2.5 %transposed.3.left_ref = bf16[1024,512]{1,0:T(8,128)(2,1)} custom-call(bf16[512,1024]{1,0:T(8,128)(2,1)} %copy-done.4), custom_call_target="tpu_custom_call" | custom-call | tf_op jit(solution)/shard_map/transposed/pallas_call | solution.py:195
  77.8 2.5 %transposed.2.left_ref = bf16[1024,512]{1,0:T(8,128)(2,1)} custom-call(bf16[512,1024]{1,0:T(8,128)(2,1)} %copy-done.6), custom_call_target="tpu_custom_call" | custom-call | tf_op jit(solution)/shard_map/transposed/pallas_call | solution.py:195
  80.3 2.2 %copy-done.1 = bf16[1,1,128,128,128]{4,3,2,1,0:T(8,128)(2,1)S(1)} copy-done((bf16[1,1,128,128,128]{4,3,2,1,0:T(8,128)(2,1)S(1)}, bf16[1,1,128,128,128]{4,3,2,1,0:T(8,128)(2,1)}, u32[]{:S(2)}) %copy-start.1) | copy-done | bytes 4194328
  82.5 1.2 %copy-done.3 = bf16[1024,512]{1,0:T(8,128)(2,1)S(1)} copy-done((bf16[1024,512]{1,0:T(8,128)(2,1)S(1)}, bf16[1024,512]{1,0:T(8,128)(2,1)}, u32[]{:S(2)}) %copy-start.3) | copy-done | bytes 1048600
  83.7 8.8 %schur.2.refs_9_ = f32[128,128,128]{2,1,0:T(8,128)} custom-call(s32[128]{0:T(128)S(1)} %fusion.1.index_ref, bf16[1024,512]{1,0:T(8,128)(2,1)S(1)} %copy-done.3, bf16[512,256]{1,0:T(8,128)(2,1)S(1)} %get-tuple-element.14.refs_0_, bf16[512,256]{1,0:T(8,128)(2,1)S(1)} %collective-permute-done.20.refs_1_, bf16[512,256]{1,0:T(8,128)(2,1)} %collective-permute-done.21.refs_2_, ...), custom_call_target="tpu_custom_call" | custom-call | tf_op jit(solution)/shard_map/schur/pallas_call | solution.py:246
  92.6 3.4 %copy-done = f32[128,128,128]{2,1,0:T(8,128)S(1)} copy-done((f32[128,128,128]{2,1,0:T(8,128)S(1)}, f32[128,128,128]{2,1,0:T(8,128)}, u32[]{:S(2)}) %copy-start) | copy-done | bytes 8388632
  95.9 7.7 %schur.3 = bf16[128,128,128]{2,1,0:T(8,128)(2,1)} custom-call(s32[128]{0:T(128)S(1)} %fusion.index_ref, bf16[1024,512]{1,0:T(8,128)(2,1)S(1)} %copy-done.2, bf16[512,256]{1,0:T(8,128)(2,1)S(1)} %get-tuple-element.13.refs_0_, bf16[512,256]{1,0:T(8,128)(2,1)S(1)} %copy-done.10, bf16[512,256]{1,0:T(8,128)(2,1)} %collective-permute-done.13.refs_2_, ...), custom_call_target="tpu_custom_call" | custom-call | tf_op jit(solution)/shard_map/schur/pallas_call | solution.py:246
  (58 shorter events, 4.0 us)
Async XLA Ops:
  0.6 62.1 %copy-start.14 = (s32[1,1,128]{2,1,0:T(1,128)S(1)}, s32[1,1,128]{2,1,0:T(1,128)}, u32[]{:S(2)}) copy-start(s32[1,1,128]{2,1,0:T(1,128)} %param.19) | copy-start | bytes 1540
  0.6 62.1 %copy-start.13 = (s32[1,1,128]{2,1,0:T(1,128)S(1)}, s32[1,1,128]{2,1,0:T(1,128)}, u32[]{:S(2)}) copy-start(s32[1,1,128]{2,1,0:T(1,128)} %param.18) | copy-start | bytes 1540
  0.7 74.5 %copy-start.16 = (s32[1,1,128]{2,1,0:T(1,128)S(1)}, s32[1,1,128]{2,1,0:T(1,128)}, u32[]{:S(2)}) copy-start(s32[1,1,128]{2,1,0:T(1,128)} %param.21) | copy-start | bytes 1540
  0.7 74.5 %copy-start.15 = (s32[1,1,128]{2,1,0:T(1,128)S(1)}, s32[1,1,128]{2,1,0:T(1,128)}, u32[]{:S(2)}) copy-start(s32[1,1,128]{2,1,0:T(1,128)} %param.20) | copy-start | bytes 1540
  2.4 6.7 %collective-permute-start.3 = (bf16[128,512]{1,0:T(8,128)(2,1)}, bf16[128,512]{1,0:T(8,128)(2,1)S(1)}, u32[]{:S(2)}, u32[]{:S(2)}) collective-permute-start(bf16[128,512]{1,0:T(8,128)(2,1)} %bridge_columns.1), channel_id=1, source_target_pairs={{0,4},{4,0},{8,12},{12,8},{16,20},{20,16},{24,28},{28,24},{1,5},{5... | collective-permute-start | bytes 393224 | tf_op jit(solution)/shard_map/ppermute | solution.py:22
  5.3 12.6 %collective-permute-start.1 = (bf16[128,1024]{1,0:T(8,128)(2,1)}, bf16[128,1024]{1,0:T(8,128)(2,1)S(1)}, u32[]{:S(2)}, u32[]{:S(2)}) collective-permute-start(bf16[128,1024]{1,0:T(8,128)(2,1)} %panel_ref.1), channel_id=1, source_target_pairs={{0,2},{1,3},{2,0},{3,1},{4,6},{5,7},{6,4},{7,5},{8,10},{9,11},{10,... | collective-permute-start | bytes 786440 | tf_op jit(solution)/shard_map/ppermute | solution.py:22
  6.8 12.1 %collective-permute-start.10 = (bf16[128,1024]{1,0:T(8,128)(2,1)}, bf16[128,1024]{1,0:T(8,128)(2,1)S(1)}, u32[]{:S(2)}, u32[]{:S(2)}) collective-permute-start(bf16[128,1024]{1,0:T(8,128)(2,1)} %refs_8_.1), channel_id=1, source_target_pairs={{0,2},{1,3},{2,0},{3,1},{4,6},{5,7},{6,4},{7,5},{8,10},{9,11},{10,... | collective-permute-start | bytes 786440 | tf_op jit(solution)/shard_map/ppermute | solution.py:22
  10.0 5.0 %collective-permute-start.4 = (bf16[128,512]{1,0:T(8,128)(2,1)S(1)}, bf16[128,512]{1,0:T(8,128)(2,1)S(1)}, u32[]{:S(2)}, u32[]{:S(2)}) collective-permute-start(bf16[128,512]{1,0:T(8,128)(2,1)S(1)} %add.67), channel_id=1, source_target_pairs={{0,8},{4,12},{8,0},{12,4},{16,24},{20,28},{24,16},{28,20},{1,9},{5... | collective-permute-start | bytes 393224 | tf_op jit(solution)/shard_map/ppermute | solution.py:22
  11.8 12.4 %collective-permute-start = (bf16[128,1024]{1,0:T(8,128)(2,1)}, bf16[128,1024]{1,0:T(8,128)(2,1)S(1)}, u32[]{:S(2)}, u32[]{:S(2)}) collective-permute-start(bf16[128,1024]{1,0:T(8,128)(2,1)} %panel_ref.1), channel_id=1, source_target_pairs={{0,1},{1,0},{2,3},{3,2},{4,5},{5,4},{6,7},{7,6},{8,9},{9,8},{10,11... | collective-permute-start | bytes 786440 | tf_op jit(solution)/shard_map/ppermute | solution.py:22
  15.0 7.6 %collective-permute-start.5 = (bf16[128,512]{1,0:T(8,128)(2,1)S(1)}, bf16[128,512]{1,0:T(8,128)(2,1)S(1)}, u32[]{:S(2)}, u32[]{:S(2)}) collective-permute-start(bf16[128,512]{1,0:T(8,128)(2,1)S(1)} %add.68), channel_id=1, source_target_pairs={{0,16},{4,20},{8,24},{12,28},{16,0},{20,4},{24,8},{28,12},{1,17},{... | collective-permute-start | bytes 393224 | tf_op jit(solution)/shard_map/ppermute | solution.py:22
  17.9 9.8 %collective-permute-start.2 = (bf16[128,1024]{1,0:T(8,128)(2,1)S(1)}, bf16[128,1024]{1,0:T(8,128)(2,1)S(1)}, u32[]{:S(2)}, u32[]{:S(2)}) collective-permute-start(bf16[128,1024]{1,0:T(8,128)(2,1)S(1)} %collective-permute-done.1.refs_3_), channel_id=1, source_target_pairs={{0,1},{1,0},{2,3},{3,2},{4,5},{5,4},{6,7},{7,6},{8,9},{9,8},{10,11... | collective-permute-start | bytes 786440 | tf_op jit(solution)/shard_map/ppermute | solution.py:22
  17.9 14.9 %collective-permute-start.9 = (bf16[128,1024]{1,0:T(8,128)(2,1)}, bf16[128,1024]{1,0:T(8,128)(2,1)S(1)}, u32[]{:S(2)}, u32[]{:S(2)}) collective-permute-start(bf16[128,1024]{1,0:T(8,128)(2,1)} %refs_8_.1), channel_id=1, source_target_pairs={{0,1},{1,0},{2,3},{3,2},{4,5},{5,4},{6,7},{7,6},{8,9},{9,8},{10,11... | collective-permute-start | bytes 786440 | tf_op jit(solution)/shard_map/ppermute | solution.py:22
  18.9 14.4 %collective-permute-start.11 = (bf16[128,1024]{1,0:T(8,128)(2,1)S(1)}, bf16[128,1024]{1,0:T(8,128)(2,1)S(1)}, u32[]{:S(2)}, u32[]{:S(2)}) collective-permute-start(bf16[128,1024]{1,0:T(8,128)(2,1)S(1)} %collective-permute-done.10.refs_10_), channel_id=1, source_target_pairs={{0,1},{1,0},{2,3},{3,2},{4,5},{5,4},{6,7},{7,6},{8,9},{9,8},{10,11... | collective-permute-start | bytes 786440 | tf_op jit(solution)/shard_map/ppermute | solution.py:22
  22.7 5.0 %collective-permute-start.7 = (bf16[128,512]{1,0:T(8,128)(2,1)S(1)}, bf16[128,512]{1,0:T(8,128)(2,1)S(1)}, u32[]{:S(2)}, u32[]{:S(2)}) collective-permute-start(bf16[128,512]{1,0:T(8,128)(2,1)S(1)} %add.69.refs_4_), channel_id=1, source_target_pairs={{0,2},{1,3},{2,0},{3,1},{4,6},{5,7},{6,4},{7,5},{8,10},{9,11},{10,... | collective-permute-start | bytes 393224 | tf_op jit(solution)/shard_map/ppermute | solution.py:22
  24.2 9.1 %collective-permute-start.6 = (bf16[128,512]{1,0:T(8,128)(2,1)S(1)}, bf16[128,512]{1,0:T(8,128)(2,1)S(1)}, u32[]{:S(2)}, u32[]{:S(2)}) collective-permute-start(bf16[128,512]{1,0:T(8,128)(2,1)S(1)} %add.69.refs_4_), channel_id=1, source_target_pairs={{0,1},{1,0},{2,3},{3,2},{4,5},{5,4},{6,7},{7,6},{8,9},{9,8},{10,11... | collective-permute-start | bytes 393224 | tf_op jit(solution)/shard_map/ppermute | solution.py:22
  27.7 5.6 %collective-permute-start.8 = (bf16[128,512]{1,0:T(8,128)(2,1)S(1)}, bf16[128,512]{1,0:T(8,128)(2,1)S(1)}, u32[]{:S(2)}, u32[]{:S(2)}) collective-permute-start(bf16[128,512]{1,0:T(8,128)(2,1)S(1)} %collective-permute-done.7.refs_6_), channel_id=1, source_target_pairs={{0,1},{1,0},{2,3},{3,2},{4,5},{5,4},{6,7},{7,6},{8,9},{9,8},{10,11... | collective-permute-start | bytes 393224 | tf_op jit(solution)/shard_map/ppermute | solution.py:22
  27.7 1.0 %copy-start.5 = (bf16[512,512]{1,0:T(8,128)(2,1)S(1)}, bf16[512,512]{1,0:T(8,128)(2,1)}, u32[]{:S(2)}) copy-start(bf16[512,512]{1,0:T(8,128)(2,1)} %refs_1_.3) | copy-start | bytes 1572868
  28.8 0.9 copy-start.7
  31.3 43.9 %copy-start.4 = (bf16[512,1024]{1,0:T(8,128)(2,1)}, bf16[512,1024]{1,0:T(8,128)(2,1)S(1)}, u32[]{:S(2)}) copy-start(bf16[512,1024]{1,0:T(8,128)(2,1)S(1)} %get-tuple-element.10.refs_3_.in_ref) | copy-start | bytes 3145732
  31.3 10.9 %collective-permute-start.24 = (bf16[512,256]{1,0:T(8,128)(2,1)S(1)}, bf16[512,256]{1,0:T(8,128)(2,1)S(1)}, u32[]{:S(2)}, u32[]{:S(2)}) collective-permute-start(bf16[512,256]{1,0:T(8,128)(2,1)S(1)} %get-tuple-element.14.refs_0_), channel_id=1, source_target_pairs={{8,0},{16,8},{24,16},{28,24},{20,28},{12,20},{4,12},{0,4},{9,1},{1... | collective-permute-start | bytes 786440 | tf_op jit(solution)/shard_map/ppermute | solution.py:56
  32.8 10.9 %collective-permute-start.20 = (bf16[512,256]{1,0:T(8,128)(2,1)S(1)}, bf16[512,256]{1,0:T(8,128)(2,1)S(1)}, u32[]{:S(2)}, u32[]{:S(2)}) collective-permute-start(bf16[512,256]{1,0:T(8,128)(2,1)S(1)} %get-tuple-element.14.refs_0_), channel_id=1, source_target_pairs={{0,8},{8,16},{16,24},{24,28},{28,20},{20,12},{12,4},{4,0},{1,9},{9... | collective-permute-start | bytes 786440 | tf_op jit(solution)/shard_map/ppermute | solution.py:55
  33.4 1.0 %copy-start.8 = (bf16[512,512]{1,0:T(8,128)(2,1)S(1)}, bf16[512,512]{1,0:T(8,128)(2,1)}, u32[]{:S(2)}) copy-start(bf16[512,512]{1,0:T(8,128)(2,1)} %refs_2_.1) | copy-start | bytes 1572868
  34.4 0.9 copy-start.11
  35.4 0.7 copy-start.12
  39.2 1.0 copy-start.6
  40.2 9.2 %collective-permute-start.16 = (bf16[512,256]{1,0:T(8,128)(2,1)S(1)}, bf16[512,256]{1,0:T(8,128)(2,1)S(1)}, u32[]{:S(2)}, u32[]{:S(2)}) collective-permute-start(bf16[512,256]{1,0:T(8,128)(2,1)S(1)} %get-tuple-element.13.refs_0_), channel_id=1, source_target_pairs={{8,0},{16,8},{24,16},{28,24},{20,28},{12,20},{4,12},{0,4},{9,1},{1... | collective-permute-start | bytes 786440 | tf_op jit(solution)/shard_map/ppermute | solution.py:56
  41.7 9.2 %collective-permute-start.12 = (bf16[512,256]{1,0:T(8,128)(2,1)S(1)}, bf16[512,256]{1,0:T(8,128)(2,1)S(1)}, u32[]{:S(2)}, u32[]{:S(2)}) collective-permute-start(bf16[512,256]{1,0:T(8,128)(2,1)S(1)} %get-tuple-element.13.refs_0_), channel_id=1, source_target_pairs={{0,8},{8,16},{16,24},{24,28},{28,20},{20,12},{12,4},{4,0},{1,9},{9... | collective-permute-start | bytes 786440 | tf_op jit(solution)/shard_map/ppermute | solution.py:55
  42.2 12.9 %collective-permute-start.25 = (bf16[512,256]{1,0:T(8,128)(2,1)S(1)}, bf16[512,256]{1,0:T(8,128)(2,1)}, u32[]{:S(2)}, u32[]{:S(2)}) collective-permute-start(bf16[512,256]{1,0:T(8,128)(2,1)S(1)} %collective-permute-done.24.refs_8_), channel_id=1, source_target_pairs={{8,0},{16,8},{24,16},{28,24},{20,28},{12,20},{4,12},{0,4},{9,1},{1... | collective-permute-start | bytes 786440 | tf_op jit(solution)/shard_map/ppermute | solution.py:56
  43.7 12.9 %collective-permute-start.21 = (bf16[512,256]{1,0:T(8,128)(2,1)S(1)}, bf16[512,256]{1,0:T(8,128)(2,1)}, u32[]{:S(2)}, u32[]{:S(2)}) collective-permute-start(bf16[512,256]{1,0:T(8,128)(2,1)S(1)} %collective-permute-done.20.refs_1_), channel_id=1, source_target_pairs={{0,8},{8,16},{16,24},{24,28},{28,20},{20,12},{12,4},{4,0},{1,9},{9... | collective-permute-start | bytes 786440 | tf_op jit(solution)/shard_map/ppermute | solution.py:55
  49.4 11.3 %collective-permute-start.17 = (bf16[512,256]{1,0:T(8,128)(2,1)S(1)}, bf16[512,256]{1,0:T(8,128)(2,1)}, u32[]{:S(2)}, u32[]{:S(2)}) collective-permute-start(bf16[512,256]{1,0:T(8,128)(2,1)S(1)} %collective-permute-done.16.refs_8_), channel_id=1, source_target_pairs={{8,0},{16,8},{24,16},{28,24},{20,28},{12,20},{4,12},{0,4},{9,1},{1... | collective-permute-start | bytes 786440 | tf_op jit(solution)/shard_map/ppermute | solution.py:56
  50.9 11.3 %collective-permute-start.13 = (bf16[512,256]{1,0:T(8,128)(2,1)S(1)}, bf16[512,256]{1,0:T(8,128)(2,1)}, u32[]{:S(2)}, u32[]{:S(2)}) collective-permute-start(bf16[512,256]{1,0:T(8,128)(2,1)S(1)} %collective-permute-done.12.refs_1_), channel_id=1, source_target_pairs={{0,8},{8,16},{16,24},{24,28},{28,20},{20,12},{12,4},{4,0},{1,9},{9... | collective-permute-start | bytes 786440 | tf_op jit(solution)/shard_map/ppermute | solution.py:55
  51.4 0.7 copy-start.9
  55.1 11.1 %collective-permute-start.26 = (bf16[512,256]{1,0:T(8,128)(2,1)}, bf16[512,256]{1,0:T(8,128)(2,1)S(1)}, u32[]{:S(2)}, u32[]{:S(2)}) collective-permute-start(bf16[512,256]{1,0:T(8,128)(2,1)} %collective-permute-done.25.refs_7_), channel_id=1, source_target_pairs={{8,0},{16,8},{24,16},{28,24},{20,28},{12,20},{4,12},{0,4},{9,1},{1... | collective-permute-start | bytes 786440 | tf_op jit(solution)/shard_map/ppermute | solution.py:56
  56.6 11.8 %collective-permute-start.22 = (bf16[512,256]{1,0:T(8,128)(2,1)}, bf16[512,256]{1,0:T(8,128)(2,1)S(1)}, u32[]{:S(2)}, u32[]{:S(2)}) collective-permute-start(bf16[512,256]{1,0:T(8,128)(2,1)} %collective-permute-done.21.refs_2_), channel_id=1, source_target_pairs={{0,8},{8,16},{16,24},{24,28},{28,20},{20,12},{12,4},{4,0},{1,9},{9... | collective-permute-start | bytes 786440 | tf_op jit(solution)/shard_map/ppermute | solution.py:55
  60.7 11.1 %collective-permute-start.18 = (bf16[512,256]{1,0:T(8,128)(2,1)}, bf16[512,256]{1,0:T(8,128)(2,1)S(1)}, u32[]{:S(2)}, u32[]{:S(2)}) collective-permute-start(bf16[512,256]{1,0:T(8,128)(2,1)} %collective-permute-done.17.refs_7_), channel_id=1, source_target_pairs={{8,0},{16,8},{24,16},{28,24},{20,28},{12,20},{4,12},{0,4},{9,1},{1... | collective-permute-start | bytes 786440 | tf_op jit(solution)/shard_map/ppermute | solution.py:56
  62.2 11.8 %collective-permute-start.14 = (bf16[512,256]{1,0:T(8,128)(2,1)}, bf16[512,256]{1,0:T(8,128)(2,1)S(1)}, u32[]{:S(2)}, u32[]{:S(2)}) collective-permute-start(bf16[512,256]{1,0:T(8,128)(2,1)} %collective-permute-done.13.refs_2_), channel_id=1, source_target_pairs={{0,8},{8,16},{16,24},{24,28},{28,20},{20,12},{12,4},{4,0},{1,9},{9... | collective-permute-start | bytes 786440 | tf_op jit(solution)/shard_map/ppermute | solution.py:55
  66.9 13.4 %collective-permute-start.27 = (bf16[256,256]{1,0:T(8,128)(2,1)}, bf16[256,256]{1,0:T(8,128)(2,1)}, u32[]{:S(2)}, u32[]{:S(2)}) collective-permute-start(bf16[256,256]{1,0:T(8,128)(2,1)} %slice.19), channel_id=1, source_target_pairs={{8,0},{16,8},{24,16},{28,24},{20,28},{12,20},{4,12},{0,4},{9,1},{1... | collective-permute-start | bytes 393224 | tf_op jit(solution)/shard_map/ppermute | solution.py:61
  69.0 11.3 %collective-permute-start.23 = (bf16[256,256]{1,0:T(8,128)(2,1)}, bf16[256,256]{1,0:T(8,128)(2,1)}, u32[]{:S(2)}, u32[]{:S(2)}) collective-permute-start(bf16[256,256]{1,0:T(8,128)(2,1)} %slice.18), channel_id=1, source_target_pairs={{0,8},{8,16},{16,24},{24,28},{28,20},{20,12},{12,4},{4,0},{1,9},{9... | collective-permute-start | bytes 393224 | tf_op jit(solution)/shard_map/ppermute | solution.py:60
  72.5 20.0 %collective-permute-start.19 = (bf16[256,256]{1,0:T(8,128)(2,1)}, bf16[256,256]{1,0:T(8,128)(2,1)S(1)}, u32[]{:S(2)}, u32[]{:S(2)}) collective-permute-start(bf16[256,256]{1,0:T(8,128)(2,1)} %slice.17), channel_id=1, source_target_pairs={{8,0},{16,8},{24,16},{28,24},{20,28},{12,20},{4,12},{0,4},{9,1},{1... | collective-permute-start | bytes 393224 | tf_op jit(solution)/shard_map/ppermute | solution.py:61
  74.7 17.9 %collective-permute-start.15 = (bf16[256,256]{1,0:T(8,128)(2,1)}, bf16[256,256]{1,0:T(8,128)(2,1)}, u32[]{:S(2)}, u32[]{:S(2)}) collective-permute-start(bf16[256,256]{1,0:T(8,128)(2,1)} %slice.16), channel_id=1, source_target_pairs={{0,8},{8,16},{16,24},{24,28},{28,20},{20,12},{12,4},{4,0},{1,9},{9... | collective-permute-start | bytes 393224 | tf_op jit(solution)/shard_map/ppermute | solution.py:60
  80.3 2.2 %copy-start.1 = (bf16[1,1,128,128,128]{4,3,2,1,0:T(8,128)(2,1)S(1)}, bf16[1,1,128,128,128]{4,3,2,1,0:T(8,128)(2,1)}, u32[]{:S(2)}) copy-start(bf16[1,1,128,128,128]{4,3,2,1,0:T(8,128)(2,1)} %param.17) | copy-start | bytes 12582916
  82.5 1.2 %copy-start.3 = (bf16[1024,512]{1,0:T(8,128)(2,1)S(1)}, bf16[1024,512]{1,0:T(8,128)(2,1)}, u32[]{:S(2)}) copy-start(bf16[1024,512]{1,0:T(8,128)(2,1)} %transposed.3.left_ref) | copy-start | bytes 3145732
  83.7 8.8 %copy-start.2 = (bf16[1024,512]{1,0:T(8,128)(2,1)S(1)}, bf16[1024,512]{1,0:T(8,128)(2,1)}, u32[]{:S(2)}) copy-start(bf16[1024,512]{1,0:T(8,128)(2,1)} %transposed.2.left_ref) | copy-start | bytes 3145732
  83.7 8.8 %copy-start.10 = (bf16[512,256]{1,0:T(8,128)(2,1)S(1)}, bf16[512,256]{1,0:T(8,128)(2,1)}, u32[]{:S(2)}) copy-start(bf16[512,256]{1,0:T(8,128)(2,1)} %copy-done.9) | copy-start | bytes 786436
  92.6 3.4 %copy-start = (f32[128,128,128]{2,1,0:T(8,128)S(1)}, f32[128,128,128]{2,1,0:T(8,128)}, u32[]{:S(2)}) copy-start(f32[128,128,128]{2,1,0:T(8,128)} %schur.2.refs_9_) | copy-start | bytes 25165828

commit v2 on v0

v2 whole, which is shorter than its diff:
```python
import functools

import jax
import jax.numpy as jnp
from jax import lax
from jax.experimental import pallas as pl
from jax.experimental.pallas import tpu as pltpu
from jax.sharding import PartitionSpec as P

VMEM = pl.BlockSpec(memory_space=pltpu.VMEM)
SMEM = pl.BlockSpec(memory_space=pltpu.SMEM)
HBM = pl.BlockSpec(memory_space=pltpu.HBM)
ANY = pl.BlockSpec(memory_space=pl.ANY)
F32 = jnp.float32
BF16 = jnp.bfloat16
TN = (((0,), (0,)), ((), ()))


def call(kernel, name, mib, micros, **kwargs):
    return pl.pallas_call(
        kernel,
        compiler_params=pltpu.CompilerParams(vmem_limit_bytes=mib and mib << 20),
        cost_estimate=pl.CostEstimate(
            flops=0, bytes_accessed=int(micros * 1e6), transcendentals=0
        ),
        name=name,
        **kwargs,
    )


def after(value, *earlier):
    return lax.optimization_barrier((value,) + earlier)[0]


def xor_permute(value, axis, mask):
    return lax.ppermute(value, axis, [(i, i ^ mask) for i in range(lax.axis_size(axis))])


def far_pieces(value):
    pieces = {0: value}
    bit = lax.axis_size("col") // 2
    while bit > 1:
        for m in list(pieces):
            pieces[m | bit] = xor_permute(pieces[m], "col", bit)
        bit //= 2
    return pieces


def near_pieces(pieces):
    pieces = dict(pieces)
    for m in list(pieces):
        pieces[m ^ 1] = xor_permute(pieces[m], "col", 1)
    return [pieces[m] for m in range(len(pieces))]


def ring_order(count):
    return list(range(0, count, 2)) + list(range(count - 1, 0, -2))


def ring_step(forward, backward):
    count = lax.axis_size("row")
    order = ring_order(count)
    ahead = [(order[i], order[(i + 1) % count]) for i in range(count)]
    back = [(b, a) for a, b in ahead]
    return lax.ppermute(forward, "row", ahead), lax.ppermute(backward, "row", back)


def arrival_rank(row):
    count = lax.axis_size("row")
    position = lambda r: jnp.where(r % 2 == 0, r // 2, count - 1 - r // 2)
    distance = (position(lax.axis_index("row")) - position(row)) % count
    ahead = jnp.maximum(2 * distance - 1, 0)
    return jnp.where(distance <= count // 2, ahead, 2 * (count - distance))


def slot_products(rows, cols, local):
    each = local // lax.axis_size("col")
    tile = cols % local // lax.axis_size("col")
    return (arrival_rank(cols // local) * each + tile) * local + rows % local


def late_slots(products, first):
    slots = products.shape[0]
    places = jnp.arange(slots, dtype=jnp.int32)
    late = products >= first
    place = jnp.sum(late[None, :] & (places[None, :] < places[:, None]), -1, dtype=jnp.int32)
    code = products * slots + places
    here = late[None, :] & (place[None, :] == places[:, None])
    table = jnp.sum(jnp.where(here, code[None, :], 0), -1, dtype=jnp.int32)
    return table, jnp.sum(late, dtype=jnp.int32).reshape(1)


def staged(value):
    return value * lax.optimization_barrier(jnp.ones((), value.dtype))


def bridge_kernel(block, local, blocks_ref, panel_ref, out_ref):
    row = lax.axis_index("row")
    for k in range(blocks_ref.shape[0]):
        piece = panel_ref[:, column(blocks_ref[k] % local, block)]
        keep = jnp.where(blocks_ref[k] // local == row, 1.0, 0.0).astype(BF16)
        out_ref[:, k * block : (k + 1) * block] = piece * keep


def bridge_columns(panel, column_blocks, block):
    slab = panel.shape[0]
    count = column_blocks.shape[0]
    return call(
        functools.partial(bridge_kernel, block, panel.shape[1] // block),
        "bridge_columns",
        None,
        1.3,
        out_shape=jax.ShapeDtypeStruct((slab, count * block), BF16),
        in_specs=[SMEM, VMEM],
        out_specs=VMEM,
    )(column_blocks, panel)


def slab_place(m, slab):
    start = pl.multiple_of((lax.axis_index("col") ^ m) * slab, slab)
    return pl.ds(start, slab)


def transposed_dot(left, right):
    return lax.dot_general(left, right, TN, preferred_element_type=F32)


def multiply(left_ref, right_ref, out_ref, step=256):
    for n in range(0, right_ref.shape[1], step):
        out_ref[:, n : n + step] = jnp.dot(
            left_ref[...], right_ref[:, n : n + step], preferred_element_type=F32
        ).astype(out_ref.dtype)


def column(j, block):
    return pl.ds(pl.multiple_of(j * block, block), block)


def own_blocks(block, width):
    for t in range(width // block):
        j = t * lax.axis_size("col") + lax.axis_index("col")
        yield slice(t * block, (t + 1) * block), j


def factor_one_kernel(block, count, *refs):
    inverse_ref, *pieces = refs[: 1 + count]
    lower_ref, own_ref, tile_ref, full_ref = refs[1 + count :]
    slab = own_ref.shape[0]
    for m, piece in enumerate(pieces):
        full_ref[slab_place(m, slab), :] = piece[...]
    multiply(inverse_ref, full_ref, lower_ref)
    own_ref[...] = lower_ref[slab_place(0, slab), :]
    for part, j in own_blocks(block, tile_ref.shape[1]):
        tile_ref[:, part] = lower_ref[:, column(j, block)]


def factor_one(inverse, pieces, block):
    width = inverse.shape[0]
    slab, columns = pieces[0].shape
    count = len(pieces)
    return call(
        functools.partial(factor_one_kernel, block, count),
        "factor_one",
        12,
        1.6,
        out_shape=(
            jax.ShapeDtypeStruct((width, columns), BF16),
            jax.ShapeDtypeStruct((slab, columns), BF16),
            jax.ShapeDtypeStruct((width, columns // count), BF16),
        ),
        in_specs=[VMEM] * (1 + count),
        out_specs=(VMEM,) * 3,
        scratch_shapes=[pltpu.VMEM((width, columns), BF16)],
    )(inverse, *pieces)


def tile_two_kernel(block, count, *refs):
    map_ref, one_ref, two_ref, lower_one_ref = refs[:4]
    raw = refs[4 : 4 + count]
    pieces = refs[4 + count : 4 + 2 * count]
    tile_ref, bridge_ref, raw_ref, full_ref, mapped_ref = refs[4 + 2 * count :]
    slab = raw[0].shape[0]
    for m, piece in enumerate(raw):
        raw_ref[slab_place(m, slab), :] = piece[...]
    multiply(one_ref, raw_ref, bridge_ref)
    for part, j in own_blocks(block, tile_ref.shape[1]):
        for m, piece in enumerate(pieces):
            full_ref[slab_place(m, slab), part] = piece[:, column(j, block)]
        mapped_ref[:, part] = lower_one_ref[:, column(map_ref[j], block)]
    update = transposed_dot(bridge_ref[...], mapped_ref[...])
    mapped_ref[...] = (full_ref[...].astype(F32) - update).astype(BF16)
    multiply(two_ref, mapped_ref, tile_ref)


def tile_two(row_map, inverse_one, inverse_two, lower_one, raw, pieces, block):
    width = inverse_one.shape[0]
    columns = pieces[0].shape[1]
    count = len(pieces)
    tile = columns // count
    return call(
        functools.partial(tile_two_kernel, block, count),
        "tile_two",
        12,
        1.6,
        out_shape=(
            jax.ShapeDtypeStruct((width, tile), BF16),
            jax.ShapeDtypeStruct((width, raw[0].shape[1]), BF16),
        ),
        in_specs=[SMEM] + [VMEM] * (3 + 2 * count),
        out_specs=(VMEM,) * 2,
        scratch_shapes=[
            pltpu.VMEM((width, raw[0].shape[1]), BF16),
            pltpu.VMEM((width, tile), BF16),
            pltpu.VMEM((width, tile), BF16),
        ],
    )(row_map, inverse_one, inverse_two, lower_one, *raw, *pieces)


def factor_two_kernel(block, count, *refs):
    map_ref, two_ref, lower_one_ref, bridge_ref, *pieces = refs[: 4 + count]
    lower_ref, own_ref, full_ref, mapped_ref = refs[4 + count :]
    slab = own_ref.shape[0]
    for m, piece in enumerate(pieces):
        full_ref[slab_place(m, slab), :] = piece[...]
    for j in range(map_ref.shape[0]):
        mapped_ref[:, j * block : (j + 1) * block] = lower_one_ref[:, column(map_ref[j], block)]
    step = 256
    for n in range(0, full_ref.shape[1], step):
        part = slice(n, n + step)
        update = transposed_dot(bridge_ref[...], mapped_ref[:, part])
        mapped_ref[:, part] = (full_ref[:, part].astype(F32) - update).astype(BF16)
    multiply(two_ref, mapped_ref, lower_ref)
    own_ref[...] = lower_ref[slab_place(0, slab), :]


def factor_two(row_map, inverse_two, lower_one, bridge, pieces, block):
    width = inverse_two.shape[0]
    slab, columns = pieces[0].shape
    count = len(pieces)
    return call(
        functools.partial(factor_two_kernel, block, count),
        "factor_two",
        12,
        2.4,
        out_shape=(
            jax.ShapeDtypeStruct((width, columns), BF16),
            jax.ShapeDtypeStruct((slab, columns), BF16),
        ),
        in_specs=[SMEM] + [VMEM] * (3 + count),
        out_specs=(VMEM,) * 2,
        scratch_shapes=[pltpu.VMEM((width, columns), BF16), pltpu.VMEM((width, columns), BF16)],
    )(row_map, inverse_two, lower_one, bridge, *pieces)


def products_of(left_ref, tiles, products_ref, block):
    local = left_ref.shape[1] // block
    each = tiles[0].shape[1] // block
    half = left_ref.shape[0] // 2
    tiles = list(tiles)
    n = 0
    while tiles:
        tile = tiles.pop(0)
        if tile.shape[0] == half:
            product = transposed_dot(left_ref[:half], tile[...])
            product = product + transposed_dot(left_ref[half:], tiles.pop(0)[...])
        else:
            product = transposed_dot(left_ref[...], tile[...])
        for t in range(each):
            for a in range(local):
                products_ref[(n * each + t) * local + a] = product[
                    a * block : (a + 1) * block, t * block : (t + 1) * block
                ]
        n += 1


def dense_kernel(block, tiles, blank, per_step, table_ref, left_ref, *refs):
    pieces = refs[:tiles]
    base_ref, out_hbm, products_ref, *held = refs[tiles:]
    out_ref = held[0] if held else out_hbm
    last = products_ref.shape[0] - 1
    if blank:
        products_ref[last] = jnp.zeros_like(products_ref[last])
    products_of(left_ref, pieces, products_ref, block)

    def step(i, _):
        for u in range(per_step):
            s = i * per_step + u
            product = products_ref[jnp.minimum(table_ref[s], last)]
            out_ref[s] = (base_ref[s].astype(F32) - product).astype(BF16)
        if held:
            copy(i).start()
        return _

    def copy(i):
        part = pl.ds(i * per_step, per_step)
        return pltpu.make_async_copy(out_ref.at[part], out_hbm.at[part], held[1].at[i])

    steps = table_ref.shape[0] // per_step
    lax.fori_loop(0, steps, step, 0)
    for i in range(steps if held else 0):
        copy(i).wait()


def dense(table, left, pieces, count, blank, base, per_step=16):
    slots, block, _ = base.shape
    local = left.shape[1] // block
    each = pieces[0].shape[1] // block
    return call(
        functools.partial(dense_kernel, block, len(pieces), blank, per_step),
        "dense",
        24,
        5,
        out_shape=jax.ShapeDtypeStruct(base.shape, BF16),
        in_specs=[SMEM] + [VMEM] * (2 + len(pieces)),
        out_specs=HBM if blank else VMEM,
        scratch_shapes=[pltpu.VMEM((count * each * local + blank, block, block), F32)]
        + ([pltpu.VMEM(base.shape, BF16), pltpu.SemaphoreType.DMA((slots // per_step,))] if blank else []),
    )(table, left, *pieces, base)


def last_kernel(block, tiles, first, table_ref, count_ref, left_ref, *refs):
    pieces = refs[:tiles]
    base_ref, _, out_hbm = refs[tiles : tiles + 3]
    products_ref, held_ref, sem = refs[tiles + 3 :]
    slots = table_ref.shape[0]
    products_of(left_ref, pieces, products_ref, block)

    def update(i, _):
        code = table_ref[i]
        s = code % slots
        product = products_ref[code // slots - first]
        held_ref[s] = (base_ref[s].astype(F32) - product).astype(BF16)
        pltpu.make_async_copy(held_ref.at[s], out_hbm.at[s], sem).start()
        return _

    def finish(i, _):
        pltpu.make_async_copy(held_ref.at[0], out_hbm.at[0], sem).wait()
        return _

    lax.fori_loop(0, count_ref[0], update, 0)
    lax.fori_loop(0, count_ref[0], finish, 0)


def last(table, count, left, pieces, base, done):
    slots, block, _ = base.shape
    local = left.shape[1] // block
    each = pieces[0].shape[1] // block
    rank = lax.axis_size("row") - 1
    return call(
        functools.partial(last_kernel, block, len(pieces), rank * each * local),
        "last",
        12,
        3,
        out_shape=jax.ShapeDtypeStruct(base.shape, BF16),
        in_specs=[SMEM] * 2 + [VMEM] * (2 + len(pieces)) + [HBM],
        out_specs=HBM,
        input_output_aliases={4 + len(pieces): 0},
        scratch_shapes=[
            pltpu.VMEM((each * local, block, block), F32),
            pltpu.VMEM((slots, block, block), BF16),
            pltpu.SemaphoreType.DMA,
        ],
    )(table, count, left, *pieces, base, done)


def per_device(
    panel_one,
    panel_two,
    inverse_one,
    inverse_two,
    column_blocks,
    row_map,
    targets,
    rows_one,
    cols_one,
    rows_two,
    cols_two,
):
    block = targets.shape[-1]
    slots = targets.shape[2]
    local = panel_one.shape[1] // block
    base = targets.reshape(slots, block, block)
    steps = lax.axis_size("row") // 2

    def ring(tile, between={}):
        half = tile.shape[0] // 2
        f = b = tile
        arrived = [tile]
        for k in range(1, steps + 1):
            if k == steps:
                f, b = f[:half], b[half:]
            f, b = ring_step(f, b)
            if between.get(k):
                earlier = between[k](arrived)
                f, b = after(f, *earlier), after(b, *earlier)
            arrived += [f, b]
        return arrived

    far_one = far_pieces(panel_one)
    raw = bridge_columns(panel_one, column_blocks, block)
    inverse_one_here = staged(inverse_one)
    own_one_here = staged(panel_one)
    masks = [1 << i for i in range(lax.axis_size("row").bit_length() - 1)][::-1]
    for mask in masks:
        other = xor_permute(raw, "row", mask)
        if mask == masks[0]:
            pieces_one = near_pieces(far_one)
            lower_one, own_one, tile_one = factor_one(
                inverse_one_here, [own_one_here] + pieces_one[1:], block
            )
            ring_one = ring(tile_one)
            other = after(other, tile_one)
        if mask == masks[-1]:
            far_two = far_pieces(after(panel_two, raw))
            inverse_two_here = staged(after(inverse_two, raw))
            own_two_here = staged(after(panel_two, raw))
            first = after(rows_one, raw).reshape(-1), cols_one.reshape(-1)
            second = after(rows_two, raw).reshape(-1), cols_two.reshape(-1)
            slots_one = slot_products(*first, local)
            slots_two = slot_products(*second, local)
            late, late_count = late_slots(
                slots_two, (lax.axis_size("row") - 1) * (local // lax.axis_size("col")) * local
            )
            row_map = after(row_map, raw) % local
            tables = (slots_one, slots_two, late, late_count, row_map)
            other = after(other, inverse_two_here, own_two_here, *tables, *ring_one[1:3])
        raw = raw + other
    base = staged(base)
    pieces_two = [own_two_here] + near_pieces(far_two)[1:]

    far_raw = far_pieces(raw)
    far_raw = {m: after(p, base) for m, p in far_raw.items()}
    tile, bridge = tile_two(
        row_map,
        inverse_one_here,
        inverse_two_here,
        lower_one,
        near_pieces(far_raw),
        pieces_two,
        block,
    )
    tile = after(tile, *ring_one[3:5])
    lower_two, own_two = factor_two(row_map, inverse_two_here, lower_one, bridge, pieces_two, block)
    part = dense(slots_one, lower_one, ring_one, 2 * steps, 0, base)
    result = []

    def most(arrived):
        result.append(dense(slots_two, lower_two, arrived, 2 * steps - 1, 1, part))
        return result

    ring_two = ring(tile, {1: lambda _: (own_two,) + tuple(ring_one[7:]), steps - 1: lambda _: (part,), steps: most})
    done = last(late, late_count, lower_two, ring_two[-2:], part, result[0])
    return own_one, own_two, done.reshape(targets.shape)


def solution(mesh):
    return jax.shard_map(
        per_device,
        mesh=mesh,
        in_specs=(
            P("col", "row"),
            P("col", "row"),
            P(),
            P(),
            P(),
            P("row"),
            P("row", "col", None, None, None),
            P("row", "col", None),
            P("row", "col", None),
            P("row", "col", None),
            P("row", "col", None),
        ),
        out_specs=(P("col", "row"), P("col", "row"), P("row", "col", None, None, None)),
        check_vma=False,
    )
```

time: 260 us -> 76.9 us (0.30)
  waiting for transfers between devices: 144 us -> 23.6 us
  local copies, waits for them, and re-layouts: 52.6 us -> 0.07 us
  matrix products: 41.4 us -> 0 us
  starting transfers between devices: 0.38 us -> 26.4 us
  Pallas kernels: 0 us -> 19.1 us
  between operations: 16.6 us -> 0.87 us
    all_gather x4 -> x0, waiting for transfers between devices: 79 us -> none  [the longest x2 51.4 us: gather_tiles(): lax.all_gather(pick_tiles(lower_full, block_size), 'row', axis=1, tiled=T...]
    psum x1 -> x0, waiting for transfers between devices: 64.2 us -> none  [bridge_columns(): lax.psum(jnp.where(owned_here, column_piece.astype(jnp.float32), 0.0).ast...]
    dot_general x5 -> x0, matrix products: 41.4 us -> none  [the longest x2 35 us: schur_terms(): jnp.einsum('wsx,wsy->sxy', left_tiles, right_tiles, preferred_element_typ...]
    gather x6 -> x0, local copies, waits for them, and re-layouts: 37.1 us -> none  [the longest x2 16.7 us: schur_terms(): jnp.take(column_set, slot_cols.reshape(-1) // lax.axis_size('col'), axis=1)]
    ppermute x0 -> x28, starting transfers between devices: none -> 26.4 us  [the longest x12 10.5 us: xor_permute(): lax.ppermute(value, axis, [(i, i ^ mask) for i in range(lax.axis_size(axi...]
    ppermute x0 -> x28, waiting for transfers between devices: none -> 23.6 us  [the longest x8 14.1 us: ring_step(): lax.ppermute(backward, 'row', back)]
    pallas_call x0 -> x7, Pallas kernels: none -> 19.1 us  [the longest x2 8.65 us: dense(): call(functools.partial(dense_kernel, block, len(pieces), blank, per_step)...]
    reshape x4 -> x0, local copies, waits for them, and re-layouts: 7.81 us -> none  [the longest x2 6.06 us: schur_terms(): column_set = tiles.reshape(panel_width, -1, block_size)]
  transfers between devices with their start and end apart: 5 -> 28, of which waited for: 5 -> 14; matrix products, arithmetic and copies ran while one was open for 24% -> 7% of each run, Pallas kernels for 0% -> 22%
where the time goes in v2:
time: 76.9 us; the launch traced here: 76.6 us
  starting transfers between devices  26.4 us (34%)
  waiting for transfers between devices  23.6 us (31%)
  Pallas kernels  19.1 us (25%)
  other arithmetic  6.51 us (8%)
  between operations  0.87 us (1%)
    ppermute x8, waiting for transfers between devices, ring_step(): lax.ppermute(backward, 'row', back)  14.1 us
    ppermute x12, starting transfers between devices, xor_permute(): lax.ppermute(value, axis, [(i, i ^ mask) for i in range(lax.axis_size(axi...  10.5 us
    pallas_call x2, Pallas kernels, dense(): call(functools.partial(dense_kernel, block, len(pieces), blank, per_step)...  8.65 us
    ppermute x8, starting transfers between devices, ring_step(): lax.ppermute(forward, 'row', ahead)  8.55 us
    ppermute x12, waiting for transfers between devices, xor_permute(): lax.ppermute(value, axis, [(i, i ^ mask) for i in range(lax.axis_size(axi...  8.39 us
    ppermute x8, starting transfers between devices, ring_step(): lax.ppermute(backward, 'row', back)  7.37 us
    mul x5, other arithmetic, staged(): return value * lax.optimization_barrier(jnp.ones((), value.dtype))  4.57 us
    pallas_call x1, Pallas kernels, factor_two(): call(functools.partial(factor_two_kernel, block, count), 'factor_two', 12...  2.77 us
  transfers between devices with their start and end apart: 28, of which 14 were waited for; matrix products, arithmetic and copies ran while one was open for 7% of the time, Pallas kernels for 22%

profile of v2, /device:TPU:0, one launch (start us, length us, event | category | flops | bytes accessed | tf_op | source)
XLA Modules:
  0.0 76.6 jit_solution(6229312515970596876)
XLA Ops:
  0.7 3.0 %collective-permute-start.1 = (bf16[128,1024]{1,0:T(8,128)(2,1)}, bf16[128,1024]{1,0:T(8,128)(2,1)S(1)}, u32[]{:S(2)}, u32[]{:S(2)}) collective-permute-start(bf16[128,1024]{1,0:T(8,128)(2,1)} %panel_ref.1), channel_id=1, source_target_pairs={{0,2},{1,3},{2,0},{3,1},{4,6},{5,7},{6,4},{7,5},{8,10},{9,11},{10,... | collective-permute-start | bytes 786440 | tf_op jit(solution)/shard_map/ppermute | solution.py:36
  3.7 1.7 %bridge_columns.1 = bf16[128,512]{1,0:T(8,128)(2,1)} custom-call(s32[4]{0:T(128)} %blocks_ref.1, bf16[128,1024]{1,0:T(8,128)(2,1)} %panel_ref.1), custom_call_target="tpu_custom_call" | custom-call | bytes 1300000 | tf_op jit(solution)/shard_map/bridge_columns/pallas_call | solution.py:108
  5.4 2.6 %collective-permute-start.3 = (bf16[128,512]{1,0:T(8,128)(2,1)}, bf16[128,512]{1,0:T(8,128)(2,1)S(1)}, u32[]{:S(2)}, u32[]{:S(2)}) collective-permute-start(bf16[128,512]{1,0:T(8,128)(2,1)} %bridge_columns.1), channel_id=1, source_target_pairs={{0,16},{4,20},{8,24},{12,28},{16,0},{20,4},{24,8},{28,12},{1,17},{... | collective-permute-start | bytes 393224 | tf_op jit(solution)/shard_map/ppermute | solution.py:36
  8.0 2.2 %collective-permute-done.1.refs_3_ = bf16[128,1024]{1,0:T(8,128)(2,1)S(1)} collective-permute-done((bf16[128,1024]{1,0:T(8,128)(2,1)}, bf16[128,1024]{1,0:T(8,128)(2,1)S(1)}, u32[]{:S(2)}, u32[]{:S(2)}) %collective-permute-start.1) | collective-permute-done | bytes 262176 | tf_op jit(solution)/shard_map/ppermute | solution.py:36
  10.2 1.1 %broadcast_multiply_fusion.1.refs_0_.refs_1_ = bf16[512,512]{1,0:T(8,128)(2,1)S(1)} fusion(bf16[512,512]{1,0:T(8,128)(2,1)} %param.13, bf16[]{:T(256)} %constant.159.clone.1), kind=kLoop, calls=%fused_computation.2 | loop fusion | flops 262144 | bytes 1048578 | tf_op jit(solution)/shard_map/mul | solution.py:94
  11.3 1.0 %broadcast_multiply_fusion.3.refs_1_ = bf16[128,1024]{1,0:T(8,128)(2,1)S(1)} fusion(bf16[128,1024]{1,0:T(8,128)(2,1)} %panel_ref.1, bf16[]{:T(256)} %constant.159.clone.1), kind=kLoop, calls=%fused_computation.4 | loop fusion | flops 131072 | bytes 524290 | tf_op jit(solution)/shard_map/mul | solution.py:94
  12.3 1.6 %factor_one.1 = (bf16[512,1024]{1,0:T(8,128)(2,1)S(1)}, bf16[128,1024]{1,0:T(8,128)(2,1)}, bf16[512,256]{1,0:T(8,128)(2,1)S(1)}) custom-call(bf16[512,512]{1,0:T(8,128)(2,1)S(1)} %broadcast_multiply_fusion.1.refs_0_.refs_1_, bf16[128,1024]{1,0:T(8,128)(2,1)S(1)} %broadcast_multiply_fusion.3.refs_1_, bf16[128,1024]{1,0:T(8,128)(2,1)S(1)} %collective-permute-done.refs_2_, ...), custom_call_target="tpu_custom_call" | custom-call | bytes 1600000 | tf_op jit(solution)/shard_map/factor_one/pallas_call | solution.py:161
  13.9 1.3 %collective-permute-done.3 = bf16[128,512]{1,0:T(8,128)(2,1)S(1)} collective-permute-done((bf16[128,512]{1,0:T(8,128)(2,1)}, bf16[128,512]{1,0:T(8,128)(2,1)S(1)}, u32[]{:S(2)}, u32[]{:S(2)}) %collective-permute-start.3) | collective-permute-done | bytes 131104 | tf_op jit(solution)/shard_map/ppermute | solution.py:36
  15.2 0.9 %add.145 = bf16[128,512]{1,0:T(8,128)(2,1)S(1)} add(bf16[128,512]{1,0:T(8,128)(2,1)} %bridge_columns.1, bf16[128,512]{1,0:T(8,128)(2,1)S(1)} %collective-permute-done.3) | non-fusion elementwise | flops 65536 | bytes 393216 | tf_op jit(solution)/shard_map/add | solution.py:427
  16.2 0.8 %collective-permute-start.4 = (bf16[128,512]{1,0:T(8,128)(2,1)S(1)}, bf16[128,512]{1,0:T(8,128)(2,1)S(1)}, u32[]{:S(2)}, u32[]{:S(2)}) collective-permute-start(bf16[128,512]{1,0:T(8,128)(2,1)S(1)} %add.145), channel_id=1, source_target_pairs={{0,8},{4,12},{8,0},{12,4},{16,24},{20,28},{24,16},{28,20},{1,9},{5... | collective-permute-start | bytes 393224 | tf_op jit(solution)/shard_map/ppermute | solution.py:36
  17.0 1.5 %collective-permute-start.7 = (bf16[512,256]{1,0:T(8,128)(2,1)S(1)}, bf16[512,256]{1,0:T(8,128)(2,1)S(1)}, u32[]{:S(2)}, u32[]{:S(2)}) collective-permute-start(bf16[512,256]{1,0:T(8,128)(2,1)S(1)} %get-tuple-element.27.refs_0_), channel_id=1, source_target_pairs={{8,0},{16,8},{24,16},{28,24},{20,28},{12,20},{4,12},{0,4},{9,1},{1... | collective-permute-start | bytes 786440 | tf_op jit(solution)/shard_map/ppermute | solution.py:65
  18.5 0.5 collective-permute-start.6
  19.0 3.6 %collective-permute-done.4 = bf16[128,512]{1,0:T(8,128)(2,1)S(1)} collective-permute-done((bf16[128,512]{1,0:T(8,128)(2,1)S(1)}, bf16[128,512]{1,0:T(8,128)(2,1)S(1)}, u32[]{:S(2)}, u32[]{:S(2)}) %collective-permute-start.4) | collective-permute-done | bytes 131104 | tf_op jit(solution)/shard_map/ppermute | solution.py:36
  22.7 0.7 convert_reduce_fusion.1
  23.4 0.3 collective-permute-start.5
  23.8 1.6 %collective-permute-start.12 = (bf16[128,1024]{1,0:T(8,128)(2,1)S(1)}, bf16[128,1024]{1,0:T(8,128)(2,1)S(1)}, u32[]{:S(2)}, u32[]{:S(2)}) collective-permute-start(bf16[128,1024]{1,0:T(8,128)(2,1)S(1)} %copy-done.1), channel_id=1, source_target_pairs={{0,2},{1,3},{2,0},{3,1},{4,6},{5,7},{6,4},{7,5},{8,10},{9,11},{10,... | collective-permute-start | bytes 786440 | tf_op jit(solution)/shard_map/ppermute | solution.py:36
  25.7 1.3 %collective-permute-done.7.refs_2_ = bf16[512,256]{1,0:T(8,128)(2,1)S(1)} collective-permute-done((bf16[512,256]{1,0:T(8,128)(2,1)S(1)}, bf16[512,256]{1,0:T(8,128)(2,1)S(1)}, u32[]{:S(2)}, u32[]{:S(2)}) %collective-permute-start.7) | collective-permute-done | bytes 262176 | tf_op jit(solution)/shard_map/ppermute | solution.py:65
  26.9 0.8 collective-permute-start.15
  27.7 1.2 %collective-permute-start.14 = (bf16[512,256]{1,0:T(8,128)(2,1)S(1)}, bf16[512,256]{1,0:T(8,128)(2,1)S(1)}, u32[]{:S(2)}, u32[]{:S(2)}) collective-permute-start(bf16[512,256]{1,0:T(8,128)(2,1)S(1)} %collective-permute-done.6.refs_1_), channel_id=1, source_target_pairs={{0,8},{8,16},{16,24},{24,28},{28,20},{20,12},{12,4},{4,0},{1,9},{9... | collective-permute-start | bytes 786440 | tf_op jit(solution)/shard_map/ppermute | solution.py:65
  29.0 0.2 collective-permute-done.5
  29.2 1.6 %collective-permute-start.9 = (bf16[128,512]{1,0:T(8,128)(2,1)S(1)}, bf16[128,512]{1,0:T(8,128)(2,1)S(1)}, u32[]{:S(2)}, u32[]{:S(2)}) collective-permute-start(bf16[128,512]{1,0:T(8,128)(2,1)S(1)} %add.162.refs_4_), channel_id=1, source_target_pairs={{0,2},{1,3},{2,0},{3,1},{4,6},{5,7},{6,4},{7,5},{8,10},{9,11},{10,... | collective-permute-start | bytes 393224 | tf_op jit(solution)/shard_map/ppermute | solution.py:36
  30.9 2.5 %multiply_bitcast_fusion.refs_9_ = bf16[128,128,128]{2,1,0:T(8,128)(2,1)S(1)} fusion(bf16[1,1,128,128,128]{4,3,2,1,0:T(8,128)(2,1)} %param.17, bf16[]{:T(256)} %constant.159.clone.1), kind=kLoop, calls=%fused_computation | loop fusion | flops 2097152 | bytes 8388610 | tf_op jit(solution)/shard_map/mul | solution.py:94
  33.4 0.9 %collective-permute-done.9.refs_6_ = bf16[128,512]{1,0:T(8,128)(2,1)S(1)} collective-permute-done((bf16[128,512]{1,0:T(8,128)(2,1)S(1)}, bf16[128,512]{1,0:T(8,128)(2,1)S(1)}, u32[]{:S(2)}, u32[]{:S(2)}) %collective-permute-start.9) | collective-permute-done | bytes 131104 | tf_op jit(solution)/shard_map/ppermute | solution.py:36
  34.3 0.5 collective-permute-start.10
  34.8 0.6 collective-permute-start.19
  35.4 1.4 %collective-permute-start.17 = (bf16[512,256]{1,0:T(8,128)(2,1)S(1)}, bf16[512,256]{1,0:T(8,128)(2,1)S(1)}, u32[]{:S(2)}, u32[]{:S(2)}) collective-permute-start(bf16[512,256]{1,0:T(8,128)(2,1)S(1)} %collective-permute-done.14.refs_3_), channel_id=1, source_target_pairs={{0,8},{8,16},{16,24},{24,28},{28,20},{20,12},{12,4},{4,0},{1,9},{9... | collective-permute-start | bytes 786440 | tf_op jit(solution)/shard_map/ppermute | solution.py:65
  36.8 1.8 %tile_two.1 = (bf16[512,256]{1,0:T(8,128)(2,1)S(1)}, bf16[512,512]{1,0:T(8,128)(2,1)S(1)}) custom-call(s32[8]{0:T(128)S(1)} %and_select_fusion.14.refs_0_, bf16[512,512]{1,0:T(8,128)(2,1)S(1)} %broadcast_multiply_fusion.1.refs_0_.refs_1_, bf16[512,512]{1,0:T(8,128)(2,1)S(1)} %broadcast_multiply_fusion.refs_2_.refs_1_, ...), custom_call_target="tpu_custom_call" | custom-call | bytes 1600000 | tf_op jit(solution)/shard_map/tile_two/pallas_call | solution.py:200
  38.6 0.6 collective-permute-start.24
  39.3 1.4 %collective-permute-start.16 = (bf16[512,256]{1,0:T(8,128)(2,1)S(1)}, bf16[512,256]{1,0:T(8,128)(2,1)S(1)}, u32[]{:S(2)}, u32[]{:S(2)}) collective-permute-start(bf16[512,256]{1,0:T(8,128)(2,1)S(1)} %get-tuple-element.42.refs_0_), channel_id=1, source_target_pairs={{0,8},{8,16},{16,24},{24,28},{28,20},{20,12},{12,4},{4,0},{1,9},{9... | collective-permute-start | bytes 786440 | tf_op jit(solution)/shard_map/ppermute | solution.py:65
  40.7 3.3 %collective-permute-done.19.refs_6_ = bf16[512,256]{1,0:T(8,128)(2,1)S(1)} collective-permute-done((bf16[512,256]{1,0:T(8,128)(2,1)S(1)}, bf16[512,256]{1,0:T(8,128)(2,1)S(1)}, u32[]{:S(2)}, u32[]{:S(2)}) %collective-permute-start.19) | collective-permute-done | bytes 262176 | tf_op jit(solution)/shard_map/ppermute | solution.py:65
  44.0 0.6 collective-permute-start.20
  44.6 1.5 %collective-permute-start.18 = (bf16[256,256]{1,0:T(8,128)(2,1)S(1)}, bf16[256,256]{1,0:T(8,128)(2,1)S(1)}, u32[]{:S(2)}, u32[]{:S(2)}) collective-permute-start(bf16[256,256]{1,0:T(8,128)(2,1)S(1)} %slice.16), channel_id=1, source_target_pairs={{0,8},{8,16},{16,24},{24,28},{28,20},{20,12},{12,4},{4,0},{1,9},{9... | collective-permute-start | bytes 393224 | tf_op jit(solution)/shard_map/ppermute | solution.py:65
  46.1 2.8 %factor_two.1 = (bf16[512,1024]{1,0:T(8,128)(2,1)S(1)}, bf16[128,1024]{1,0:T(8,128)(2,1)}) custom-call(s32[8]{0:T(128)S(1)} %and_select_fusion.14.refs_0_, bf16[512,512]{1,0:T(8,128)(2,1)S(1)} %broadcast_multiply_fusion.refs_2_.refs_1_, bf16[512,1024]{1,0:T(8,128)(2,1)S(1)} %get-tuple-element.31.refs_3_.refs_2_.left_ref, ...), custom_call_target="tpu_custom_call" | custom-call | bytes 2400000 | tf_op jit(solution)/shard_map/factor_two/pallas_call | solution.py:240
  48.9 2.6 %collective-permute-done.20.refs_8_ = bf16[256,256]{1,0:T(8,128)(2,1)S(1)} collective-permute-done((bf16[256,256]{1,0:T(8,128)(2,1)S(1)}, bf16[256,256]{1,0:T(8,128)(2,1)S(1)}, u32[]{:S(2)}, u32[]{:S(2)}) %collective-permute-start.20) | collective-permute-done | bytes 131104 | tf_op jit(solution)/shard_map/ppermute | solution.py:65
  51.5 0.6 collective-permute-done.18.refs_7_
  52.1 1.7 %collective-permute-start.25 = (bf16[512,256]{1,0:T(8,128)(2,1)S(1)}, bf16[512,256]{1,0:T(8,128)(2,1)S(1)}, u32[]{:S(2)}, u32[]{:S(2)}) collective-permute-start(bf16[512,256]{1,0:T(8,128)(2,1)S(1)} %collective-permute-done.24.refs_2_), channel_id=1, source_target_pairs={{8,0},{16,8},{24,16},{28,24},{20,28},{12,20},{4,12},{0,4},{9,1},{1... | collective-permute-start | bytes 786440 | tf_op jit(solution)/shard_map/ppermute | solution.py:65
  53.8 0.3 collective-permute-start.21
  54.1 5.7 %collective-permute-done.25.refs_4_ = bf16[512,256]{1,0:T(8,128)(2,1)S(1)} collective-permute-done((bf16[512,256]{1,0:T(8,128)(2,1)S(1)}, bf16[512,256]{1,0:T(8,128)(2,1)S(1)}, u32[]{:S(2)}, u32[]{:S(2)}) %collective-permute-start.25) | collective-permute-done | bytes 262176 | tf_op jit(solution)/shard_map/ppermute | solution.py:65
  59.8 1.1 %collective-permute-start.26 = (bf16[512,256]{1,0:T(8,128)(2,1)S(1)}, bf16[512,256]{1,0:T(8,128)(2,1)S(1)}, u32[]{:S(2)}, u32[]{:S(2)}) collective-permute-start(bf16[512,256]{1,0:T(8,128)(2,1)S(1)} %collective-permute-done.25.refs_4_), channel_id=1, source_target_pairs={{8,0},{16,8},{24,16},{28,24},{20,28},{12,20},{4,12},{0,4},{9,1},{1... | collective-permute-start | bytes 786440 | tf_op jit(solution)/shard_map/ppermute | solution.py:65
  60.9 0.2 collective-permute-done.21.refs_3_
  61.1 0.7 collective-permute-start.22
  61.8 3.8 %dense.2.refs_7_.refs_2_ = bf16[128,128,128]{2,1,0:T(8,128)(2,1)S(1)} custom-call(s32[128]{0:T(128)S(1)} %get-tuple-element.51.table_ref, bf16[512,1024]{1,0:T(8,128)(2,1)S(1)} %get-tuple-element.31.refs_3_.refs_2_.left_ref, bf16[512,256]{1,0:T(8,128)(2,1)S(1)} %get-tuple-element.27.refs_0_, bf16[512,256]{1,0:T(8,128)(2,1)S(1)} %collective-permute-done.6.refs_1_, ...), custom_call_target="tpu_custom_call" | custom-call | bytes 5000000 | tf_op jit(solution)/shard_map/dense/pallas_call | solution.py:308
  65.6 1.3 %collective-permute-done.26.refs_6_ = bf16[512,256]{1,0:T(8,128)(2,1)S(1)} collective-permute-done((bf16[512,256]{1,0:T(8,128)(2,1)S(1)}, bf16[512,256]{1,0:T(8,128)(2,1)S(1)}, u32[]{:S(2)}, u32[]{:S(2)}) %collective-permute-start.26) | collective-permute-done | bytes 262176 | tf_op jit(solution)/shard_map/ppermute | solution.py:65
  66.9 0.4 collective-permute-start.27
  67.4 0.3 collective-permute-done.22.refs_5_
  67.7 1.4 %collective-permute-start.23 = (bf16[256,256]{1,0:T(8,128)(2,1)S(1)}, bf16[256,256]{1,0:T(8,128)(2,1)S(1)}, u32[]{:S(2)}, u32[]{:S(2)}) collective-permute-start(bf16[256,256]{1,0:T(8,128)(2,1)S(1)} %slice.14), channel_id=1, source_target_pairs={{0,8},{8,16},{16,24},{24,28},{28,20},{20,12},{12,4},{4,0},{1,9},{9... | collective-permute-start | bytes 393224 | tf_op jit(solution)/shard_map/ppermute | solution.py:65
  69.1 4.9 %dense.3.refs_3_ = bf16[128,128,128]{2,1,0:T(8,128)(2,1)} custom-call(s32[128]{0:T(128)S(1)} %get-tuple-element.50.table_ref, bf16[512,1024]{1,0:T(8,128)(2,1)S(1)} %get-tuple-element.40.left_ref, bf16[512,256]{1,0:T(8,128)(2,1)S(1)} %get-tuple-element.42.refs_0_, bf16[512,256]{1,0:T(8,128)(2,1)S(1)} %collective-permute-done.16.refs_1_, ...), custom_call_target="tpu_custom_call" | custom-call | bytes 5000000 | tf_op jit(solution)/shard_map/dense/pallas_call | solution.py:308
  74.0 2.6 %last.1 = bf16[128,128,128]{2,1,0:T(8,128)(2,1)} custom-call(s32[128]{0:T(128)S(1)} %select_reduce_fusion.table_ref, s32[1]{0:T(128)} %bitcast.4.count_ref, bf16[512,1024]{1,0:T(8,128)(2,1)S(1)} %get-tuple-element.40.left_ref, bf16[256,256]{1,0:T(8,128)(2,1)S(1)} %collective-permute-done.23.refs_0_, ...), custom_call_target="tpu_custom_call", output_to_operand_aliasing={{}: (6, {})} | custom-call | bytes 3000000 | tf_op jit(solution)/shard_map/last/pallas_call | solution.py:349
  (47 shorter events, 0.6 us)
Async XLA Ops:
  0.6 22.0 %copy-start.2 = (s32[1,1,128]{2,1,0:T(1,128)S(1)}, s32[1,1,128]{2,1,0:T(1,128)}, u32[]{:S(2)}) copy-start(s32[1,1,128]{2,1,0:T(1,128)} %param.20) | copy-start | bytes 1540
  0.6 22.0 %copy-start.4 = (s32[1,1,128]{2,1,0:T(1,128)S(1)}, s32[1,1,128]{2,1,0:T(1,128)}, u32[]{:S(2)}) copy-start(s32[1,1,128]{2,1,0:T(1,128)} %param.18) | copy-start | bytes 1540
  0.7 22.0 %copy-start.3 = (s32[1,1,128]{2,1,0:T(1,128)S(1)}, s32[1,1,128]{2,1,0:T(1,128)}, u32[]{:S(2)}) copy-start(s32[1,1,128]{2,1,0:T(1,128)} %param.21) | copy-start | bytes 1540
  0.7 22.0 %copy-start.5 = (s32[1,1,128]{2,1,0:T(1,128)S(1)}, s32[1,1,128]{2,1,0:T(1,128)}, u32[]{:S(2)}) copy-start(s32[1,1,128]{2,1,0:T(1,128)} %param.19) | copy-start | bytes 1540
  0.7 23.1 %copy-start.1 = (bf16[128,1024]{1,0:T(8,128)(2,1)S(1)}, bf16[128,1024]{1,0:T(8,128)(2,1)}, u32[]{:S(2)}) copy-start(bf16[128,1024]{1,0:T(8,128)(2,1)} %param.12) | copy-start | bytes 786436
  0.7 24.7 %copy-start = (bf16[512,512]{1,0:T(8,128)(2,1)S(1)}, bf16[512,512]{1,0:T(8,128)(2,1)}, u32[]{:S(2)}) copy-start(bf16[512,512]{1,0:T(8,128)(2,1)} %param.14) | copy-start | bytes 1572868
  0.7 24.7 %copy-start.6 = (s32[8]{0:T(128)S(1)}, s32[8]{0:T(128)}, u32[]{:S(2)}) copy-start(s32[8]{0:T(128)} %param.16) | copy-start | bytes 100
  0.7 9.5 %collective-permute-start.1 = (bf16[128,1024]{1,0:T(8,128)(2,1)}, bf16[128,1024]{1,0:T(8,128)(2,1)S(1)}, u32[]{:S(2)}, u32[]{:S(2)}) collective-permute-start(bf16[128,1024]{1,0:T(8,128)(2,1)} %panel_ref.1), channel_id=1, source_target_pairs={{0,2},{1,3},{2,0},{3,1},{4,6},{5,7},{6,4},{7,5},{8,10},{9,11},{10,... | collective-permute-start | bytes 786440 | tf_op jit(solution)/shard_map/ppermute | solution.py:36
  3.7 8.6 %collective-permute-start = (bf16[128,1024]{1,0:T(8,128)(2,1)}, bf16[128,1024]{1,0:T(8,128)(2,1)S(1)}, u32[]{:S(2)}, u32[]{:S(2)}) collective-permute-start(bf16[128,1024]{1,0:T(8,128)(2,1)} %panel_ref.1), channel_id=1, source_target_pairs={{0,1},{1,0},{2,3},{3,2},{4,5},{5,4},{6,7},{7,6},{8,9},{9,8},{10,11... | collective-permute-start | bytes 786440 | tf_op jit(solution)/shard_map/ppermute | solution.py:36
  5.4 9.8 %collective-permute-start.3 = (bf16[128,512]{1,0:T(8,128)(2,1)}, bf16[128,512]{1,0:T(8,128)(2,1)S(1)}, u32[]{:S(2)}, u32[]{:S(2)}) collective-permute-start(bf16[128,512]{1,0:T(8,128)(2,1)} %bridge_columns.1), channel_id=1, source_target_pairs={{0,16},{4,20},{8,24},{12,28},{16,0},{20,4},{24,8},{28,12},{1,17},{... | collective-permute-start | bytes 393224 | tf_op jit(solution)/shard_map/ppermute | solution.py:36
  10.2 2.1 %collective-permute-start.2 = (bf16[128,1024]{1,0:T(8,128)(2,1)S(1)}, bf16[128,1024]{1,0:T(8,128)(2,1)S(1)}, u32[]{:S(2)}, u32[]{:S(2)}) collective-permute-start(bf16[128,1024]{1,0:T(8,128)(2,1)S(1)} %collective-permute-done.1.refs_3_), channel_id=1, source_target_pairs={{0,1},{1,0},{2,3},{3,2},{4,5},{5,4},{6,7},{7,6},{8,9},{9,8},{10,11... | collective-permute-start | bytes 786440 | tf_op jit(solution)/shard_map/ppermute | solution.py:36
  16.2 6.5 %collective-permute-start.4 = (bf16[128,512]{1,0:T(8,128)(2,1)S(1)}, bf16[128,512]{1,0:T(8,128)(2,1)S(1)}, u32[]{:S(2)}, u32[]{:S(2)}) collective-permute-start(bf16[128,512]{1,0:T(8,128)(2,1)S(1)} %add.145), channel_id=1, source_target_pairs={{0,8},{4,12},{8,0},{12,4},{16,24},{20,28},{24,16},{28,20},{1,9},{5... | collective-permute-start | bytes 393224 | tf_op jit(solution)/shard_map/ppermute | solution.py:36
  17.0 9.9 %collective-permute-start.7 = (bf16[512,256]{1,0:T(8,128)(2,1)S(1)}, bf16[512,256]{1,0:T(8,128)(2,1)S(1)}, u32[]{:S(2)}, u32[]{:S(2)}) collective-permute-start(bf16[512,256]{1,0:T(8,128)(2,1)S(1)} %get-tuple-element.27.refs_0_), channel_id=1, source_target_pairs={{8,0},{16,8},{24,16},{28,24},{20,28},{12,20},{4,12},{0,4},{9,1},{1... | collective-permute-start | bytes 786440 | tf_op jit(solution)/shard_map/ppermute | solution.py:65
  18.5 9.2 %collective-permute-start.6 = (bf16[512,256]{1,0:T(8,128)(2,1)S(1)}, bf16[512,256]{1,0:T(8,128)(2,1)S(1)}, u32[]{:S(2)}, u32[]{:S(2)}) collective-permute-start(bf16[512,256]{1,0:T(8,128)(2,1)S(1)} %get-tuple-element.27.refs_0_), channel_id=1, source_target_pairs={{0,8},{8,16},{16,24},{24,28},{28,20},{20,12},{12,4},{4,0},{1,9},{9... | collective-permute-start | bytes 786440 | tf_op jit(solution)/shard_map/ppermute | solution.py:65
  23.4 5.8 %collective-permute-start.5 = (bf16[128,512]{1,0:T(8,128)(2,1)S(1)}, bf16[128,512]{1,0:T(8,128)(2,1)S(1)}, u32[]{:S(2)}, u32[]{:S(2)}) collective-permute-start(bf16[128,512]{1,0:T(8,128)(2,1)S(1)} %add.146), channel_id=1, source_target_pairs={{0,4},{4,0},{8,12},{12,8},{16,20},{20,16},{24,28},{28,24},{1,5},{5... | collective-permute-start | bytes 393224 | tf_op jit(solution)/shard_map/ppermute | solution.py:36
  23.8 7.1 %collective-permute-start.12 = (bf16[128,1024]{1,0:T(8,128)(2,1)S(1)}, bf16[128,1024]{1,0:T(8,128)(2,1)S(1)}, u32[]{:S(2)}, u32[]{:S(2)}) collective-permute-start(bf16[128,1024]{1,0:T(8,128)(2,1)S(1)} %copy-done.1), channel_id=1, source_target_pairs={{0,2},{1,3},{2,0},{3,1},{4,6},{5,7},{6,4},{7,5},{8,10},{9,11},{10,... | collective-permute-start | bytes 786440 | tf_op jit(solution)/shard_map/ppermute | solution.py:36
  25.4 8.9 %collective-permute-start.11 = (bf16[128,1024]{1,0:T(8,128)(2,1)S(1)}, bf16[128,1024]{1,0:T(8,128)(2,1)S(1)}, u32[]{:S(2)}, u32[]{:S(2)}) collective-permute-start(bf16[128,1024]{1,0:T(8,128)(2,1)S(1)} %copy-done.1), channel_id=1, source_target_pairs={{0,1},{1,0},{2,3},{3,2},{4,5},{5,4},{6,7},{7,6},{8,9},{9,8},{10,11... | collective-permute-start | bytes 786440 | tf_op jit(solution)/shard_map/ppermute | solution.py:36
  26.9 7.9 %collective-permute-start.15 = (bf16[512,256]{1,0:T(8,128)(2,1)S(1)}, bf16[512,256]{1,0:T(8,128)(2,1)S(1)}, u32[]{:S(2)}, u32[]{:S(2)}) collective-permute-start(bf16[512,256]{1,0:T(8,128)(2,1)S(1)} %collective-permute-done.7.refs_2_), channel_id=1, source_target_pairs={{8,0},{16,8},{24,16},{28,24},{20,28},{12,20},{4,12},{0,4},{9,1},{1... | collective-permute-start | bytes 786440 | tf_op jit(solution)/shard_map/ppermute | solution.py:65
  27.7 7.6 %collective-permute-start.14 = (bf16[512,256]{1,0:T(8,128)(2,1)S(1)}, bf16[512,256]{1,0:T(8,128)(2,1)S(1)}, u32[]{:S(2)}, u32[]{:S(2)}) collective-permute-start(bf16[512,256]{1,0:T(8,128)(2,1)S(1)} %collective-permute-done.6.refs_1_), channel_id=1, source_target_pairs={{0,8},{8,16},{16,24},{24,28},{28,20},{20,12},{12,4},{4,0},{1,9},{9... | collective-permute-start | bytes 786440 | tf_op jit(solution)/shard_map/ppermute | solution.py:65
  29.2 5.0 %collective-permute-start.9 = (bf16[128,512]{1,0:T(8,128)(2,1)S(1)}, bf16[128,512]{1,0:T(8,128)(2,1)S(1)}, u32[]{:S(2)}, u32[]{:S(2)}) collective-permute-start(bf16[128,512]{1,0:T(8,128)(2,1)S(1)} %add.162.refs_4_), channel_id=1, source_target_pairs={{0,2},{1,3},{2,0},{3,1},{4,6},{5,7},{6,4},{7,5},{8,10},{9,11},{10,... | collective-permute-start | bytes 393224 | tf_op jit(solution)/shard_map/ppermute | solution.py:36
  30.9 5.9 %collective-permute-start.13 = (bf16[128,1024]{1,0:T(8,128)(2,1)S(1)}, bf16[128,1024]{1,0:T(8,128)(2,1)S(1)}, u32[]{:S(2)}, u32[]{:S(2)}) collective-permute-start(bf16[128,1024]{1,0:T(8,128)(2,1)S(1)} %collective-permute-done.12.refs_10_.refs_6_), channel_id=1, source_target_pairs={{0,1},{1,0},{2,3},{3,2},{4,5},{5,4},{6,7},{7,6},{8,9},{9,8},{10,11... | collective-permute-start | bytes 786440 | tf_op jit(solution)/shard_map/ppermute | solution.py:36
  34.3 2.6 %collective-permute-start.8 = (bf16[128,512]{1,0:T(8,128)(2,1)S(1)}, bf16[128,512]{1,0:T(8,128)(2,1)S(1)}, u32[]{:S(2)}, u32[]{:S(2)}) collective-permute-start(bf16[128,512]{1,0:T(8,128)(2,1)S(1)} %add.162.refs_4_), channel_id=1, source_target_pairs={{0,1},{1,0},{2,3},{3,2},{4,5},{5,4},{6,7},{7,6},{8,9},{9,8},{10,11... | collective-permute-start | bytes 393224 | tf_op jit(solution)/shard_map/ppermute | solution.py:36
  34.3 2.5 %collective-permute-start.10 = (bf16[128,512]{1,0:T(8,128)(2,1)S(1)}, bf16[128,512]{1,0:T(8,128)(2,1)S(1)}, u32[]{:S(2)}, u32[]{:S(2)}) collective-permute-start(bf16[128,512]{1,0:T(8,128)(2,1)S(1)} %collective-permute-done.9.refs_6_), channel_id=1, source_target_pairs={{0,1},{1,0},{2,3},{3,2},{4,5},{5,4},{6,7},{7,6},{8,9},{9,8},{10,11... | collective-permute-start | bytes 393224 | tf_op jit(solution)/shard_map/ppermute | solution.py:36
  34.8 9.2 %collective-permute-start.19 = (bf16[512,256]{1,0:T(8,128)(2,1)S(1)}, bf16[512,256]{1,0:T(8,128)(2,1)S(1)}, u32[]{:S(2)}, u32[]{:S(2)}) collective-permute-start(bf16[512,256]{1,0:T(8,128)(2,1)S(1)} %collective-permute-done.15.refs_4_), channel_id=1, source_target_pairs={{8,0},{16,8},{24,16},{28,24},{20,28},{12,20},{4,12},{0,4},{9,1},{1... | collective-permute-start | bytes 786440 | tf_op jit(solution)/shard_map/ppermute | solution.py:65
  35.4 9.2 %collective-permute-start.17 = (bf16[512,256]{1,0:T(8,128)(2,1)S(1)}, bf16[512,256]{1,0:T(8,128)(2,1)S(1)}, u32[]{:S(2)}, u32[]{:S(2)}) collective-permute-start(bf16[512,256]{1,0:T(8,128)(2,1)S(1)} %collective-permute-done.14.refs_3_), channel_id=1, source_target_pairs={{0,8},{8,16},{16,24},{24,28},{28,20},{20,12},{12,4},{4,0},{1,9},{9... | collective-permute-start | bytes 786440 | tf_op jit(solution)/shard_map/ppermute | solution.py:65
  38.6 13.5 %collective-permute-start.24 = (bf16[512,256]{1,0:T(8,128)(2,1)S(1)}, bf16[512,256]{1,0:T(8,128)(2,1)S(1)}, u32[]{:S(2)}, u32[]{:S(2)}) collective-permute-start(bf16[512,256]{1,0:T(8,128)(2,1)S(1)} %get-tuple-element.42.refs_0_), channel_id=1, source_target_pairs={{8,0},{16,8},{24,16},{28,24},{20,28},{12,20},{4,12},{0,4},{9,1},{1... | collective-permute-start | bytes 786440 | tf_op jit(solution)/shard_map/ppermute | solution.py:65
  39.3 14.6 %collective-permute-start.16 = (bf16[512,256]{1,0:T(8,128)(2,1)S(1)}, bf16[512,256]{1,0:T(8,128)(2,1)S(1)}, u32[]{:S(2)}, u32[]{:S(2)}) collective-permute-start(bf16[512,256]{1,0:T(8,128)(2,1)S(1)} %get-tuple-element.42.refs_0_), channel_id=1, source_target_pairs={{0,8},{8,16},{16,24},{24,28},{28,20},{20,12},{12,4},{4,0},{1,9},{9... | collective-permute-start | bytes 786440 | tf_op jit(solution)/shard_map/ppermute | solution.py:65
  44.0 7.5 %collective-permute-start.20 = (bf16[256,256]{1,0:T(8,128)(2,1)S(1)}, bf16[256,256]{1,0:T(8,128)(2,1)S(1)}, u32[]{:S(2)}, u32[]{:S(2)}) collective-permute-start(bf16[256,256]{1,0:T(8,128)(2,1)S(1)} %slice.17), channel_id=1, source_target_pairs={{8,0},{16,8},{24,16},{28,24},{20,28},{12,20},{4,12},{0,4},{9,1},{1... | collective-permute-start | bytes 393224 | tf_op jit(solution)/shard_map/ppermute | solution.py:65
  44.6 7.5 %collective-permute-start.18 = (bf16[256,256]{1,0:T(8,128)(2,1)S(1)}, bf16[256,256]{1,0:T(8,128)(2,1)S(1)}, u32[]{:S(2)}, u32[]{:S(2)}) collective-permute-start(bf16[256,256]{1,0:T(8,128)(2,1)S(1)} %slice.16), channel_id=1, source_target_pairs={{0,8},{8,16},{16,24},{24,28},{28,20},{20,12},{12,4},{4,0},{1,9},{9... | collective-permute-start | bytes 393224 | tf_op jit(solution)/shard_map/ppermute | solution.py:65
  52.1 7.7 %collective-permute-start.25 = (bf16[512,256]{1,0:T(8,128)(2,1)S(1)}, bf16[512,256]{1,0:T(8,128)(2,1)S(1)}, u32[]{:S(2)}, u32[]{:S(2)}) collective-permute-start(bf16[512,256]{1,0:T(8,128)(2,1)S(1)} %collective-permute-done.24.refs_2_), channel_id=1, source_target_pairs={{8,0},{16,8},{24,16},{28,24},{20,28},{12,20},{4,12},{0,4},{9,1},{1... | collective-permute-start | bytes 786440 | tf_op jit(solution)/shard_map/ppermute | solution.py:65
  53.8 7.3 %collective-permute-start.21 = (bf16[512,256]{1,0:T(8,128)(2,1)S(1)}, bf16[512,256]{1,0:T(8,128)(2,1)S(1)}, u32[]{:S(2)}, u32[]{:S(2)}) collective-permute-start(bf16[512,256]{1,0:T(8,128)(2,1)S(1)} %collective-permute-done.16.refs_1_), channel_id=1, source_target_pairs={{0,8},{8,16},{16,24},{24,28},{28,20},{20,12},{12,4},{4,0},{1,9},{9... | collective-permute-start | bytes 786440 | tf_op jit(solution)/shard_map/ppermute | solution.py:65
  59.8 7.1 %collective-permute-start.26 = (bf16[512,256]{1,0:T(8,128)(2,1)S(1)}, bf16[512,256]{1,0:T(8,128)(2,1)S(1)}, u32[]{:S(2)}, u32[]{:S(2)}) collective-permute-start(bf16[512,256]{1,0:T(8,128)(2,1)S(1)} %collective-permute-done.25.refs_4_), channel_id=1, source_target_pairs={{8,0},{16,8},{24,16},{28,24},{20,28},{12,20},{4,12},{0,4},{9,1},{1... | collective-permute-start | bytes 786440 | tf_op jit(solution)/shard_map/ppermute | solution.py:65
  61.1 6.5 %collective-permute-start.22 = (bf16[512,256]{1,0:T(8,128)(2,1)S(1)}, bf16[512,256]{1,0:T(8,128)(2,1)S(1)}, u32[]{:S(2)}, u32[]{:S(2)}) collective-permute-start(bf16[512,256]{1,0:T(8,128)(2,1)S(1)} %collective-permute-done.21.refs_3_), channel_id=1, source_target_pairs={{0,8},{8,16},{16,24},{24,28},{28,20},{20,12},{12,4},{4,0},{1,9},{9... | collective-permute-start | bytes 786440 | tf_op jit(solution)/shard_map/ppermute | solution.py:65
  66.9 7.0 %collective-permute-start.27 = (bf16[256,256]{1,0:T(8,128)(2,1)S(1)}, bf16[256,256]{1,0:T(8,128)(2,1)S(1)}, u32[]{:S(2)}, u32[]{:S(2)}) collective-permute-start(bf16[256,256]{1,0:T(8,128)(2,1)S(1)} %slice.15), channel_id=1, source_target_pairs={{8,0},{16,8},{24,16},{28,24},{20,28},{12,20},{4,12},{0,4},{9,1},{1... | collective-permute-start | bytes 393224 | tf_op jit(solution)/shard_map/ppermute | solution.py:65
  67.7 6.3 %collective-permute-start.23 = (bf16[256,256]{1,0:T(8,128)(2,1)S(1)}, bf16[256,256]{1,0:T(8,128)(2,1)S(1)}, u32[]{:S(2)}, u32[]{:S(2)}) collective-permute-start(bf16[256,256]{1,0:T(8,128)(2,1)S(1)} %slice.14), channel_id=1, source_target_pairs={{0,8},{8,16},{16,24},{24,28},{28,20},{20,12},{12,4},{4,0},{1,9},{9... | collective-permute-start | bytes 393224 | tf_op jit(solution)/shard_map/ppermute | solution.py:65

commit v3 on v2

--- a/solution.py
+++ b/solution.py
@@ -108,7 +108,7 @@
     return call(
         functools.partial(bridge_kernel, block, panel.shape[1] // block),
         "bridge_columns",
-        None,
+        8,
         1.3,
         out_shape=jax.ShapeDtypeStruct((slab, count * block), BF16),
         in_specs=[SMEM, VMEM],
@@ -382,38 +382,42 @@
     base = targets.reshape(slots, block, block)
     steps = lax.axis_size("row") // 2
 
-    def ring(tile, between={}):
-        half = tile.shape[0] // 2
-        f = b = tile
-        arrived = [tile]
-        for k in range(1, steps + 1):
-            if k == steps:
-                f, b = f[:half], b[half:]
-            f, b = ring_step(f, b)
-            if between.get(k):
-                earlier = between[k](arrived)
-                f, b = after(f, *earlier), after(b, *earlier)
-            arrived += [f, b]
-        return arrived
-
-    far_one = far_pieces(panel_one)
+    def go_on(arrived, *earlier):
+        k = (len(arrived) + 1) // 2
+        f, b = arrived[-2:] if k > 1 else arrived * 2
+        if earlier:
+            f, b = after(f, *earlier), after(b, *earlier)
+        if k == steps:
+            half = f.shape[0] // 2
+            f, b = f[:half], b[half:]
+        arrived += ring_step(f, b)
+
+    def meet(arrived, *earlier):
+        arrived[-2:] = [after(piece, *earlier) for piece in arrived[-2:]]
+
     raw = bridge_columns(panel_one, column_blocks, block)
+    far_one = far_pieces(after(panel_one, raw))
     inverse_one_here = staged(inverse_one)
     own_one_here = staged(panel_one)
     masks = [1 << i for i in range(lax.axis_size("row").bit_length() - 1)][::-1]
-    for mask in masks:
+    for at, mask in enumerate(masks):
         other = xor_permute(raw, "row", mask)
-        if mask == masks[0]:
+        if at == 0:
+            other = after(other, inverse_one_here, own_one_here)
+        if at == 1:
+            far_one = {m: after(p, raw) for m, p in far_one.items()}
             pieces_one = near_pieces(far_one)
             lower_one, own_one, tile_one = factor_one(
                 inverse_one_here, [own_one_here] + pieces_one[1:], block
             )
-            ring_one = ring(tile_one)
+            ring_one = [tile_one]
+            go_on(ring_one)
             other = after(other, tile_one)
-        if mask == masks[-1]:
+        if at == 2:
             far_two = far_pieces(after(panel_two, raw))
             inverse_two_here = staged(after(inverse_two, raw))
             own_two_here = staged(after(panel_two, raw))
+            other = after(other, inverse_two_here, own_two_here)
             first = after(rows_one, raw).reshape(-1), cols_one.reshape(-1)
             second = after(rows_two, raw).reshape(-1), cols_two.reshape(-1)
             slots_one = slot_products(*first, local)
@@ -422,34 +426,31 @@
                 slots_two, (lax.axis_size("row") - 1) * (local // lax.axis_size("col")) * local
             )
             row_map = after(row_map, raw) % local
-            tables = (slots_one, slots_two, late, late_count, row_map)
-            other = after(other, inverse_two_here, own_two_here, *tables, *ring_one[1:3])
+            other = after(other, slots_one, slots_two, late, late_count, row_map)
         raw = raw + other
     base = staged(base)
+    go_on(ring_one)
     pieces_two = [own_two_here] + near_pieces(far_two)[1:]
-
     far_raw = far_pieces(raw)
-    far_raw = {m: after(p, base) for m, p in far_raw.items()}
+    far_raw = {m: after(p, *ring_one[1:3]) for m, p in far_raw.items()}
     tile, bridge = tile_two(
-        row_map,
-        inverse_one_here,
-        inverse_two_here,
-        lower_one,
-        near_pieces(far_raw),
-        pieces_two,
-        block,
+        row_map, inverse_one_here, inverse_two_here, lower_one, near_pieces(far_raw), pieces_two, block
     )
-    tile = after(tile, *ring_one[3:5])
+    ring_two = [tile]
+    go_on(ring_two)
     lower_two, own_two = factor_two(row_map, inverse_two_here, lower_one, bridge, pieces_two, block)
+    while len(ring_one) < 2 * steps + 1:
+        go_on(ring_one)
     part = dense(slots_one, lower_one, ring_one, 2 * steps, 0, base)
-    result = []
-
-    def most(arrived):
-        result.append(dense(slots_two, lower_two, arrived, 2 * steps - 1, 1, part))
-        return result
-
-    ring_two = ring(tile, {1: lambda _: (own_two,) + tuple(ring_one[7:]), steps - 1: lambda _: (part,), steps: most})
-    done = last(late, late_count, lower_two, ring_two[-2:], part, result[0])
+    meet(ring_two, own_two, *ring_one[3:5], *ring_one[7:])
+    for k in range(2, steps):
+        go_on(ring_two)
+        if k == steps - 1:
+            meet(ring_two, part)
+    go_on(ring_two)
+    done = dense(slots_two, lower_two, ring_two[:-2], 2 * steps - 1, 1, part)
+    meet(ring_two, done)
+    done = last(late, late_count, lower_two, ring_two[-2:], part, done)
     return own_one, own_two, done.reshape(targets.shape)
 
 

time: 76.9 us -> 76.4 us (level)
  starting transfers between devices: 26.4 us -> 30.2 us
  other arithmetic: 6.51 us -> 3.42 us
  waiting for transfers between devices: 23.6 us -> 22.5 us
    ppermute x8, waiting for transfers between devices: 14.1 us -> 0.33 us  [ring_step(): lax.ppermute(backward, 'row', back)]
    ppermute x8, waiting for transfers between devices: 1.15 us -> 13.1 us  [ring_step(): lax.ppermute(forward, 'row', ahead)]
    ppermute x8, starting transfers between devices: 8.55 us -> 11.5 us  [ring_step(): lax.ppermute(forward, 'row', ahead)]
    mul x5, other arithmetic: 4.57 us -> 2.38 us  [staged(): return value * lax.optimization_barrier(jnp.ones((), value.dtype))]
    ppermute x12, starting transfers between devices: 10.5 us -> 12.5 us  [xor_permute(): lax.ppermute(value, axis, [(i, i ^ mask) for i in range(lax.axis_size(axi...]
    ppermute x8, starting transfers between devices: 7.37 us -> 6.22 us  [ring_step(): lax.ppermute(backward, 'row', back)]
    add x3, other arithmetic: 1 us -> 0.1 us  [per_device(): raw = raw + other]
  transfers between devices with their start and end apart: 28 -> 28, of which waited for: 14 -> 12; matrix products, arithmetic and copies ran while one was open for 7% -> 5% of each run, Pallas kernels for 22% -> 19%
where the time goes in v3:
time: 76.4 us; the launch traced here: 76.1 us
  starting transfers between devices  30.2 us (40%)
  waiting for transfers between devices  22.5 us (29%)
  Pallas kernels  18.4 us (24%)
  other arithmetic  3.42 us (4%)
  between operations  0.88 us (1%)
    ppermute x8, waiting for transfers between devices, ring_step(): lax.ppermute(forward, 'row', ahead)  13.1 us
    ppermute x12, starting transfers between devices, xor_permute(): lax.ppermute(value, axis, [(i, i ^ mask) for i in range(lax.axis_size(axi...  12.5 us
    ppermute x8, starting transfers between devices, ring_step(): lax.ppermute(forward, 'row', ahead)  11.5 us
    ppermute x12, waiting for transfers between devices, xor_permute(): lax.ppermute(value, axis, [(i, i ^ mask) for i in range(lax.axis_size(axi...  9.02 us
    pallas_call x2, Pallas kernels, dense(): call(functools.partial(dense_kernel, block, len(pieces), blank, per_step)...  8.68 us
    ppermute x8, starting transfers between devices, ring_step(): lax.ppermute(backward, 'row', back)  6.22 us
    pallas_call x1, Pallas kernels, factor_two(): call(functools.partial(factor_two_kernel, block, count), 'factor_two', 12...  2.78 us
    pallas_call x1, Pallas kernels, last(): call(functools.partial(last_kernel, block, len(pieces), rank * each * loc...  2.45 us
  transfers between devices with their start and end apart: 28, of which 12 were waited for; matrix products, arithmetic and copies ran while one was open for 5% of the time, Pallas kernels for 19%

profile of v3, /device:TPU:0, one launch (start us, length us, event | category | flops | bytes accessed | tf_op | source)
XLA Modules:
  0.0 76.1 jit_solution(7076378998740332058)
XLA Ops:
  0.6 0.6 copy-done
  1.3 1.1 %bridge_columns.1 = bf16[128,512]{1,0:T(8,128)(2,1)S(1)} custom-call(s32[4]{0:T(128)S(1)} %copy-done, bf16[128,1024]{1,0:T(8,128)(2,1)} %panel_ref.1), custom_call_target="tpu_custom_call" | custom-call | bytes 1300000 | tf_op jit(solution)/shard_map/bridge_columns/pallas_call | solution.py:108
  2.4 4.1 %collective-permute-start = (bf16[128,512]{1,0:T(8,128)(2,1)S(1)}, bf16[128,512]{1,0:T(8,128)(2,1)S(1)}, u32[]{:S(2)}, u32[]{:S(2)}) collective-permute-start(bf16[128,512]{1,0:T(8,128)(2,1)S(1)} %bridge_columns.1), channel_id=1, source_target_pairs={{0,16},{4,20},{8,24},{12,28},{16,0},{20,4},{24,8},{28,12},{1,17},{... | collective-permute-start | bytes 393224 | tf_op jit(solution)/shard_map/ppermute | solution.py:36
  6.5 1.5 %collective-permute-start.2 = (bf16[128,1024]{1,0:T(8,128)(2,1)}, bf16[128,1024]{1,0:T(8,128)(2,1)S(1)}, u32[]{:S(2)}, u32[]{:S(2)}) collective-permute-start(bf16[128,1024]{1,0:T(8,128)(2,1)} %panel_ref.1), channel_id=1, source_target_pairs={{0,2},{1,3},{2,0},{3,1},{4,6},{5,7},{6,4},{7,5},{8,10},{9,11},{10,... | collective-permute-start | bytes 786440 | tf_op jit(solution)/shard_map/ppermute | solution.py:36
  8.0 1.1 %broadcast_multiply_fusion.1.refs_0_.refs_1_ = bf16[512,512]{1,0:T(8,128)(2,1)S(1)} fusion(bf16[512,512]{1,0:T(8,128)(2,1)} %param.13, bf16[]{:T(256)} %constant.159.clone.1), kind=kLoop, calls=%fused_computation.2 | loop fusion | flops 262144 | bytes 1048578 | tf_op jit(solution)/shard_map/mul | solution.py:94
  9.1 1.0 %broadcast_multiply_fusion.3.refs_1_ = bf16[128,1024]{1,0:T(8,128)(2,1)S(1)} fusion(bf16[128,1024]{1,0:T(8,128)(2,1)} %panel_ref.1, bf16[]{:T(256)} %constant.159.clone.1), kind=kLoop, calls=%fused_computation.4 | loop fusion | flops 131072 | bytes 524290 | tf_op jit(solution)/shard_map/mul | solution.py:94
  10.1 2.8 %collective-permute-done = bf16[128,512]{1,0:T(8,128)(2,1)S(1)} collective-permute-done((bf16[128,512]{1,0:T(8,128)(2,1)S(1)}, bf16[128,512]{1,0:T(8,128)(2,1)S(1)}, u32[]{:S(2)}, u32[]{:S(2)}) %collective-permute-start) | collective-permute-done | bytes 131104 | tf_op jit(solution)/shard_map/ppermute | solution.py:36
  12.9 0.1 collective-permute-start.1
  12.9 1.6 %collective-permute-done.2.refs_3_ = bf16[128,1024]{1,0:T(8,128)(2,1)S(1)} collective-permute-done((bf16[128,1024]{1,0:T(8,128)(2,1)}, bf16[128,1024]{1,0:T(8,128)(2,1)S(1)}, u32[]{:S(2)}, u32[]{:S(2)}) %collective-permute-start.2) | collective-permute-done | bytes 262176 | tf_op jit(solution)/shard_map/ppermute | solution.py:36
  14.5 1.6 %collective-permute-start.4 = (bf16[128,512]{1,0:T(8,128)(2,1)S(1)}, bf16[128,512]{1,0:T(8,128)(2,1)S(1)}, u32[]{:S(2)}, u32[]{:S(2)}) collective-permute-start(bf16[128,512]{1,0:T(8,128)(2,1)S(1)} %add.145), channel_id=1, source_target_pairs={{0,8},{4,12},{8,0},{12,4},{16,24},{20,28},{24,16},{28,20},{1,9},{5... | collective-permute-start | bytes 393224 | tf_op jit(solution)/shard_map/ppermute | solution.py:36
  16.1 1.6 %factor_one.1 = (bf16[512,1024]{1,0:T(8,128)(2,1)S(1)}, bf16[128,1024]{1,0:T(8,128)(2,1)}, bf16[512,256]{1,0:T(8,128)(2,1)S(1)}) custom-call(bf16[512,512]{1,0:T(8,128)(2,1)S(1)} %broadcast_multiply_fusion.1.refs_0_.refs_1_, bf16[128,1024]{1,0:T(8,128)(2,1)S(1)} %broadcast_multiply_fusion.3.refs_1_, bf16[128,1024]{1,0:T(8,128)(2,1)S(1)} %collective-permute-done.1.refs_2_, ...), custom_call_target="tpu_custom_call" | custom-call | bytes 1600000 | tf_op jit(solution)/shard_map/factor_one/pallas_call | solution.py:161
  17.7 1.5 %collective-permute-start.6 = (bf16[512,256]{1,0:T(8,128)(2,1)S(1)}, bf16[512,256]{1,0:T(8,128)(2,1)S(1)}, u32[]{:S(2)}, u32[]{:S(2)}) collective-permute-start(bf16[512,256]{1,0:T(8,128)(2,1)S(1)} %get-tuple-element.35.refs_0_), channel_id=1, source_target_pairs={{0,8},{8,16},{16,24},{24,28},{28,20},{20,12},{12,4},{4,0},{1,9},{9... | collective-permute-start | bytes 786440 | tf_op jit(solution)/shard_map/ppermute | solution.py:65
  19.2 0.5 collective-permute-start.7
  19.7 0.7 collective-permute-done.4
  20.5 1.6 %collective-permute-start.5 = (bf16[128,512]{1,0:T(8,128)(2,1)S(1)}, bf16[128,512]{1,0:T(8,128)(2,1)S(1)}, u32[]{:S(2)}, u32[]{:S(2)}) collective-permute-start(bf16[128,512]{1,0:T(8,128)(2,1)S(1)} %add.146), channel_id=1, source_target_pairs={{0,4},{4,0},{8,12},{12,8},{16,20},{20,16},{24,28},{28,24},{1,5},{5... | collective-permute-start | bytes 393224 | tf_op jit(solution)/shard_map/ppermute | solution.py:36
  22.1 0.1 collective-permute-start.11
  22.2 1.6 %collective-permute-start.12 = (bf16[128,1024]{1,0:T(8,128)(2,1)S(1)}, bf16[128,1024]{1,0:T(8,128)(2,1)S(1)}, u32[]{:S(2)}, u32[]{:S(2)}) collective-permute-start(bf16[128,1024]{1,0:T(8,128)(2,1)S(1)} %copy-done.3), channel_id=1, source_target_pairs={{0,2},{1,3},{2,0},{3,1},{4,6},{5,7},{6,4},{7,5},{8,10},{9,11},{10,... | collective-permute-start | bytes 786440 | tf_op jit(solution)/shard_map/ppermute | solution.py:36
  23.8 0.7 convert_reduce_fusion.1
  24.5 2.3 %collective-permute-done.6.refs_1_ = bf16[512,256]{1,0:T(8,128)(2,1)S(1)} collective-permute-done((bf16[512,256]{1,0:T(8,128)(2,1)S(1)}, bf16[512,256]{1,0:T(8,128)(2,1)S(1)}, u32[]{:S(2)}, u32[]{:S(2)}) %collective-permute-start.6) | collective-permute-done | bytes 262176 | tf_op jit(solution)/shard_map/ppermute | solution.py:65
  26.8 0.8 %collective-permute-start.15 = (bf16[512,256]{1,0:T(8,128)(2,1)S(1)}, bf16[512,256]{1,0:T(8,128)(2,1)S(1)}, u32[]{:S(2)}, u32[]{:S(2)}) collective-permute-start(bf16[512,256]{1,0:T(8,128)(2,1)S(1)} %collective-permute-done.6.refs_1_), channel_id=1, source_target_pairs={{0,8},{8,16},{16,24},{24,28},{28,20},{20,12},{12,4},{4,0},{1,9},{9... | collective-permute-start | bytes 786440 | tf_op jit(solution)/shard_map/ppermute | solution.py:65
  27.6 1.3 %collective-permute-start.16 = (bf16[512,256]{1,0:T(8,128)(2,1)S(1)}, bf16[512,256]{1,0:T(8,128)(2,1)S(1)}, u32[]{:S(2)}, u32[]{:S(2)}) collective-permute-start(bf16[512,256]{1,0:T(8,128)(2,1)S(1)} %collective-permute-done.7.refs_2_), channel_id=1, source_target_pairs={{8,0},{16,8},{24,16},{28,24},{20,28},{12,20},{4,12},{0,4},{9,1},{1... | collective-permute-start | bytes 786440 | tf_op jit(solution)/shard_map/ppermute | solution.py:65
  28.9 0.1 convert_reduce_fusion
  29.0 0.1 select_reduce_fusion.table_ref
  29.1 0.5 collective-permute-done.5
  29.7 1.6 %collective-permute-start.9 = (bf16[128,512]{1,0:T(8,128)(2,1)S(1)}, bf16[128,512]{1,0:T(8,128)(2,1)S(1)}, u32[]{:S(2)}, u32[]{:S(2)}) collective-permute-start(bf16[128,512]{1,0:T(8,128)(2,1)S(1)} %add.162.refs_4_), channel_id=1, source_target_pairs={{0,2},{1,3},{2,0},{3,1},{4,6},{5,7},{6,4},{7,5},{8,10},{9,11},{10,... | collective-permute-start | bytes 393224 | tf_op jit(solution)/shard_map/ppermute | solution.py:36
  31.2 3.5 %collective-permute-done.9.refs_6_ = bf16[128,512]{1,0:T(8,128)(2,1)S(1)} collective-permute-done((bf16[128,512]{1,0:T(8,128)(2,1)S(1)}, bf16[128,512]{1,0:T(8,128)(2,1)S(1)}, u32[]{:S(2)}, u32[]{:S(2)}) %collective-permute-start.9) | collective-permute-done | bytes 131104 | tf_op jit(solution)/shard_map/ppermute | solution.py:36
  34.7 0.5 collective-permute-start.10
  35.2 0.6 collective-permute-start.17
  35.8 1.5 %collective-permute-start.19 = (bf16[512,256]{1,0:T(8,128)(2,1)S(1)}, bf16[512,256]{1,0:T(8,128)(2,1)S(1)}, u32[]{:S(2)}, u32[]{:S(2)}) collective-permute-start(bf16[512,256]{1,0:T(8,128)(2,1)S(1)} %collective-permute-done.16.refs_4_), channel_id=1, source_target_pairs={{8,0},{16,8},{24,16},{28,24},{20,28},{12,20},{4,12},{0,4},{9,1},{1... | collective-permute-start | bytes 786440 | tf_op jit(solution)/shard_map/ppermute | solution.py:65
  37.2 1.8 %tile_two.1 = (bf16[512,256]{1,0:T(8,128)(2,1)S(1)}, bf16[512,512]{1,0:T(8,128)(2,1)S(1)}) custom-call(s32[8]{0:T(128)S(1)} %and_select_fusion.14.refs_0_, bf16[512,512]{1,0:T(8,128)(2,1)S(1)} %broadcast_multiply_fusion.1.refs_0_.refs_1_, bf16[512,512]{1,0:T(8,128)(2,1)S(1)} %broadcast_multiply_fusion.refs_2_.refs_1_, ...), custom_call_target="tpu_custom_call" | custom-call | bytes 1600000 | tf_op jit(solution)/shard_map/tile_two/pallas_call | solution.py:200
  39.0 0.6 collective-permute-start.14
  39.7 1.4 %collective-permute-start.24 = (bf16[512,256]{1,0:T(8,128)(2,1)S(1)}, bf16[512,256]{1,0:T(8,128)(2,1)S(1)}, u32[]{:S(2)}, u32[]{:S(2)}) collective-permute-start(bf16[512,256]{1,0:T(8,128)(2,1)S(1)} %get-tuple-element.50.refs_0_), channel_id=1, source_target_pairs={{8,0},{16,8},{24,16},{28,24},{20,28},{12,20},{4,12},{0,4},{9,1},{1... | collective-permute-start | bytes 786440 | tf_op jit(solution)/shard_map/ppermute | solution.py:65
  41.1 3.2 %collective-permute-done.17.refs_5_ = bf16[512,256]{1,0:T(8,128)(2,1)S(1)} collective-permute-done((bf16[512,256]{1,0:T(8,128)(2,1)S(1)}, bf16[512,256]{1,0:T(8,128)(2,1)S(1)}, u32[]{:S(2)}, u32[]{:S(2)}) %collective-permute-start.17) | collective-permute-done | bytes 262176 | tf_op jit(solution)/shard_map/ppermute | solution.py:65
  44.4 0.6 collective-permute-start.18
  45.0 1.5 %collective-permute-start.20 = (bf16[256,256]{1,0:T(8,128)(2,1)S(1)}, bf16[256,256]{1,0:T(8,128)(2,1)S(1)}, u32[]{:S(2)}, u32[]{:S(2)}) collective-permute-start(bf16[256,256]{1,0:T(8,128)(2,1)S(1)} %slice.17), channel_id=1, source_target_pairs={{8,0},{16,8},{24,16},{28,24},{20,28},{12,20},{4,12},{0,4},{9,1},{1... | collective-permute-start | bytes 393224 | tf_op jit(solution)/shard_map/ppermute | solution.py:65
  46.5 2.8 %factor_two.1 = (bf16[512,1024]{1,0:T(8,128)(2,1)S(1)}, bf16[128,1024]{1,0:T(8,128)(2,1)}) custom-call(s32[8]{0:T(128)S(1)} %and_select_fusion.14.refs_0_, bf16[512,512]{1,0:T(8,128)(2,1)S(1)} %broadcast_multiply_fusion.refs_2_.refs_1_, bf16[512,1024]{1,0:T(8,128)(2,1)S(1)} %get-tuple-element.39.refs_3_.refs_2_.left_ref, ...), custom_call_target="tpu_custom_call" | custom-call | bytes 2400000 | tf_op jit(solution)/shard_map/factor_two/pallas_call | solution.py:240
  49.3 0.7 collective-permute-done.14.refs_1_
  50.0 2.0 %collective-permute-done.18.refs_7_ = bf16[256,256]{1,0:T(8,128)(2,1)S(1)} collective-permute-done((bf16[256,256]{1,0:T(8,128)(2,1)S(1)}, bf16[256,256]{1,0:T(8,128)(2,1)S(1)}, u32[]{:S(2)}, u32[]{:S(2)}) %collective-permute-start.18) | collective-permute-done | bytes 131104 | tf_op jit(solution)/shard_map/ppermute | solution.py:65
  51.9 0.3 collective-permute-done.20.refs_8_
  52.2 2.4 %collective-permute-start.21 = (bf16[512,256]{1,0:T(8,128)(2,1)S(1)}, bf16[512,256]{1,0:T(8,128)(2,1)S(1)}, u32[]{:S(2)}, u32[]{:S(2)}) collective-permute-start(bf16[512,256]{1,0:T(8,128)(2,1)S(1)} %collective-permute-done.14.refs_1_), channel_id=1, source_target_pairs={{0,8},{8,16},{16,24},{24,28},{28,20},{20,12},{12,4},{4,0},{1,9},{9... | collective-permute-start | bytes 786440 | tf_op jit(solution)/shard_map/ppermute | solution.py:65
  54.6 4.9 %collective-permute-done.21.refs_3_ = bf16[512,256]{1,0:T(8,128)(2,1)S(1)} collective-permute-done((bf16[512,256]{1,0:T(8,128)(2,1)S(1)}, bf16[512,256]{1,0:T(8,128)(2,1)S(1)}, u32[]{:S(2)}, u32[]{:S(2)}) %collective-permute-start.21) | collective-permute-done | bytes 262176 | tf_op jit(solution)/shard_map/ppermute | solution.py:65
  59.5 2.5 %collective-permute-start.22 = (bf16[512,256]{1,0:T(8,128)(2,1)S(1)}, bf16[512,256]{1,0:T(8,128)(2,1)S(1)}, u32[]{:S(2)}, u32[]{:S(2)}) collective-permute-start(bf16[512,256]{1,0:T(8,128)(2,1)S(1)} %collective-permute-done.21.refs_3_), channel_id=1, source_target_pairs={{0,8},{8,16},{16,24},{24,28},{28,20},{20,12},{12,4},{4,0},{1,9},{9... | collective-permute-start | bytes 786440 | tf_op jit(solution)/shard_map/ppermute | solution.py:65
  62.0 0.3 multiply_bitcast_fusion.refs_9_
  62.3 3.8 %dense.2.refs_7_.refs_2_ = bf16[128,128,128]{2,1,0:T(8,128)(2,1)S(1)} custom-call(s32[128]{0:T(128)S(1)} %fusion.2.table_ref, bf16[512,1024]{1,0:T(8,128)(2,1)S(1)} %get-tuple-element.39.refs_3_.refs_2_.left_ref, bf16[512,256]{1,0:T(8,128)(2,1)S(1)} %get-tuple-element.35.refs_0_, bf16[512,256]{1,0:T(8,128)(2,1)S(1)} %collective-permute-done.6.refs_1_, ...), custom_call_target="tpu_custom_call" | custom-call | bytes 5000000 | tf_op jit(solution)/shard_map/dense/pallas_call | solution.py:308
  66.2 2.4 %collective-permute-start.23 = (bf16[256,256]{1,0:T(8,128)(2,1)S(1)}, bf16[256,256]{1,0:T(8,128)(2,1)S(1)}, u32[]{:S(2)}, u32[]{:S(2)}) collective-permute-start(bf16[256,256]{1,0:T(8,128)(2,1)S(1)} %slice.14), channel_id=1, source_target_pairs={{0,8},{8,16},{16,24},{24,28},{28,20},{20,12},{12,4},{4,0},{1,9},{9... | collective-permute-start | bytes 393224 | tf_op jit(solution)/shard_map/ppermute | solution.py:65
  68.7 4.9 %dense.3.refs_3_ = bf16[128,128,128]{2,1,0:T(8,128)(2,1)} custom-call(s32[128]{0:T(128)S(1)} %get-tuple-element.58.table_ref, bf16[512,1024]{1,0:T(8,128)(2,1)S(1)} %get-tuple-element.49.left_ref, bf16[512,256]{1,0:T(8,128)(2,1)S(1)} %get-tuple-element.50.refs_0_, bf16[512,256]{1,0:T(8,128)(2,1)S(1)} %collective-permute-done.14.refs_1_, ...), custom_call_target="tpu_custom_call" | custom-call | bytes 5000000 | tf_op jit(solution)/shard_map/dense/pallas_call | solution.py:308
  73.6 0.1 collective-permute-done.27.refs_1_
  73.6 2.5 %last.1 = bf16[128,128,128]{2,1,0:T(8,128)(2,1)} custom-call(s32[128]{0:T(128)S(1)} %select_reduce_fusion.table_ref, s32[1]{0:T(128)} %bitcast.4.count_ref, bf16[512,1024]{1,0:T(8,128)(2,1)S(1)} %get-tuple-element.49.left_ref, bf16[256,256]{1,0:T(8,128)(2,1)S(1)} %collective-permute-done.23.refs_0_, ...), custom_call_target="tpu_custom_call", output_to_operand_aliasing={{}: (6, {})} | custom-call | bytes 3000000 | tf_op jit(solution)/shard_map/last/pallas_call | solution.py:349
  (52 shorter events, 0.4 us)
Async XLA Ops:
  0.6 0.7 copy-start
  1.3 20.8 %copy-start.3 = (bf16[128,1024]{1,0:T(8,128)(2,1)S(1)}, bf16[128,1024]{1,0:T(8,128)(2,1)}, u32[]{:S(2)}) copy-start(bf16[128,1024]{1,0:T(8,128)(2,1)} %param.12) | copy-start | bytes 786436
  1.3 22.4 %copy-start.2 = (bf16[512,512]{1,0:T(8,128)(2,1)S(1)}, bf16[512,512]{1,0:T(8,128)(2,1)}, u32[]{:S(2)}) copy-start(bf16[512,512]{1,0:T(8,128)(2,1)} %param.14) | copy-start | bytes 1572868
  1.3 22.5 %copy-start.4 = (s32[1,1,128]{2,1,0:T(1,128)S(1)}, s32[1,1,128]{2,1,0:T(1,128)}, u32[]{:S(2)}) copy-start(s32[1,1,128]{2,1,0:T(1,128)} %param.20) | copy-start | bytes 1540
  1.3 22.5 %copy-start.5 = (s32[1,1,128]{2,1,0:T(1,128)S(1)}, s32[1,1,128]{2,1,0:T(1,128)}, u32[]{:S(2)}) copy-start(s32[1,1,128]{2,1,0:T(1,128)} %param.21) | copy-start | bytes 1540
  1.3 23.1 %copy-start.6 = (s32[1,1,128]{2,1,0:T(1,128)S(1)}, s32[1,1,128]{2,1,0:T(1,128)}, u32[]{:S(2)}) copy-start(s32[1,1,128]{2,1,0:T(1,128)} %param.18) | copy-start | bytes 1540
  1.3 23.1 %copy-start.7 = (s32[1,1,128]{2,1,0:T(1,128)S(1)}, s32[1,1,128]{2,1,0:T(1,128)}, u32[]{:S(2)}) copy-start(s32[1,1,128]{2,1,0:T(1,128)} %param.19) | copy-start | bytes 1540
  1.3 23.2 %copy-start.8 = (s32[8]{0:T(128)S(1)}, s32[8]{0:T(128)}, u32[]{:S(2)}) copy-start(s32[8]{0:T(128)} %param.16) | copy-start | bytes 100
  2.4 10.4 %collective-permute-start = (bf16[128,512]{1,0:T(8,128)(2,1)S(1)}, bf16[128,512]{1,0:T(8,128)(2,1)S(1)}, u32[]{:S(2)}, u32[]{:S(2)}) collective-permute-start(bf16[128,512]{1,0:T(8,128)(2,1)S(1)} %bridge_columns.1), channel_id=1, source_target_pairs={{0,16},{4,20},{8,24},{12,28},{16,0},{20,4},{24,8},{28,12},{1,17},{... | collective-permute-start | bytes 393224 | tf_op jit(solution)/shard_map/ppermute | solution.py:36
  6.5 8.0 %collective-permute-start.2 = (bf16[128,1024]{1,0:T(8,128)(2,1)}, bf16[128,1024]{1,0:T(8,128)(2,1)S(1)}, u32[]{:S(2)}, u32[]{:S(2)}) collective-permute-start(bf16[128,1024]{1,0:T(8,128)(2,1)} %panel_ref.1), channel_id=1, source_target_pairs={{0,2},{1,3},{2,0},{3,1},{4,6},{5,7},{6,4},{7,5},{8,10},{9,11},{10,... | collective-permute-start | bytes 786440 | tf_op jit(solution)/shard_map/ppermute | solution.py:36
  12.9 3.2 %collective-permute-start.1 = (bf16[128,1024]{1,0:T(8,128)(2,1)}, bf16[128,1024]{1,0:T(8,128)(2,1)S(1)}, u32[]{:S(2)}, u32[]{:S(2)}) collective-permute-start(bf16[128,1024]{1,0:T(8,128)(2,1)} %panel_ref.1), channel_id=1, source_target_pairs={{0,1},{1,0},{2,3},{3,2},{4,5},{5,4},{6,7},{7,6},{8,9},{9,8},{10,11... | collective-permute-start | bytes 786440 | tf_op jit(solution)/shard_map/ppermute | solution.py:36
  14.5 1.6 %collective-permute-start.3 = (bf16[128,1024]{1,0:T(8,128)(2,1)S(1)}, bf16[128,1024]{1,0:T(8,128)(2,1)S(1)}, u32[]{:S(2)}, u32[]{:S(2)}) collective-permute-start(bf16[128,1024]{1,0:T(8,128)(2,1)S(1)} %collective-permute-done.2.refs_3_), channel_id=1, source_target_pairs={{0,1},{1,0},{2,3},{3,2},{4,5},{5,4},{6,7},{7,6},{8,9},{9,8},{10,11... | collective-permute-start | bytes 786440 | tf_op jit(solution)/shard_map/ppermute | solution.py:36
  14.5 5.9 %collective-permute-start.4 = (bf16[128,512]{1,0:T(8,128)(2,1)S(1)}, bf16[128,512]{1,0:T(8,128)(2,1)S(1)}, u32[]{:S(2)}, u32[]{:S(2)}) collective-permute-start(bf16[128,512]{1,0:T(8,128)(2,1)S(1)} %add.145), channel_id=1, source_target_pairs={{0,8},{4,12},{8,0},{12,4},{16,24},{20,28},{24,16},{28,20},{1,9},{5... | collective-permute-start | bytes 393224 | tf_op jit(solution)/shard_map/ppermute | solution.py:36
  17.7 9.1 %collective-permute-start.6 = (bf16[512,256]{1,0:T(8,128)(2,1)S(1)}, bf16[512,256]{1,0:T(8,128)(2,1)S(1)}, u32[]{:S(2)}, u32[]{:S(2)}) collective-permute-start(bf16[512,256]{1,0:T(8,128)(2,1)S(1)} %get-tuple-element.35.refs_0_), channel_id=1, source_target_pairs={{0,8},{8,16},{16,24},{24,28},{28,20},{20,12},{12,4},{4,0},{1,9},{9... | collective-permute-start | bytes 786440 | tf_op jit(solution)/shard_map/ppermute | solution.py:65
  19.2 8.4 %collective-permute-start.7 = (bf16[512,256]{1,0:T(8,128)(2,1)S(1)}, bf16[512,256]{1,0:T(8,128)(2,1)S(1)}, u32[]{:S(2)}, u32[]{:S(2)}) collective-permute-start(bf16[512,256]{1,0:T(8,128)(2,1)S(1)} %get-tuple-element.35.refs_0_), channel_id=1, source_target_pairs={{8,0},{16,8},{24,16},{28,24},{20,28},{12,20},{4,12},{0,4},{9,1},{1... | collective-permute-start | bytes 786440 | tf_op jit(solution)/shard_map/ppermute | solution.py:65
  20.5 9.2 %collective-permute-start.5 = (bf16[128,512]{1,0:T(8,128)(2,1)S(1)}, bf16[128,512]{1,0:T(8,128)(2,1)S(1)}, u32[]{:S(2)}, u32[]{:S(2)}) collective-permute-start(bf16[128,512]{1,0:T(8,128)(2,1)S(1)} %add.146), channel_id=1, source_target_pairs={{0,4},{4,0},{8,12},{12,8},{16,20},{20,16},{24,28},{28,24},{1,5},{5... | collective-permute-start | bytes 393224 | tf_op jit(solution)/shard_map/ppermute | solution.py:36
  22.1 40.0 %copy-start.1 = (bf16[1,1,128,128,128]{4,3,2,1,0:T(8,128)(2,1)S(1)}, bf16[1,1,128,128,128]{4,3,2,1,0:T(8,128)(2,1)}, u32[]{:S(2)}) copy-start(bf16[1,1,128,128,128]{4,3,2,1,0:T(8,128)(2,1)} %param.17) | copy-start | bytes 12582916
  22.1 12.6 %collective-permute-start.11 = (bf16[128,1024]{1,0:T(8,128)(2,1)S(1)}, bf16[128,1024]{1,0:T(8,128)(2,1)S(1)}, u32[]{:S(2)}, u32[]{:S(2)}) collective-permute-start(bf16[128,1024]{1,0:T(8,128)(2,1)S(1)} %copy-done.3), channel_id=1, source_target_pairs={{0,1},{1,0},{2,3},{3,2},{4,5},{5,4},{6,7},{7,6},{8,9},{9,8},{10,11... | collective-permute-start | bytes 786440 | tf_op jit(solution)/shard_map/ppermute | solution.py:36
  22.2 9.1 %collective-permute-start.12 = (bf16[128,1024]{1,0:T(8,128)(2,1)S(1)}, bf16[128,1024]{1,0:T(8,128)(2,1)S(1)}, u32[]{:S(2)}, u32[]{:S(2)}) collective-permute-start(bf16[128,1024]{1,0:T(8,128)(2,1)S(1)} %copy-done.3), channel_id=1, source_target_pairs={{0,2},{1,3},{2,0},{3,1},{4,6},{5,7},{6,4},{7,5},{8,10},{9,11},{10,... | collective-permute-start | bytes 786440 | tf_op jit(solution)/shard_map/ppermute | solution.py:36
  26.8 8.4 %collective-permute-start.15 = (bf16[512,256]{1,0:T(8,128)(2,1)S(1)}, bf16[512,256]{1,0:T(8,128)(2,1)S(1)}, u32[]{:S(2)}, u32[]{:S(2)}) collective-permute-start(bf16[512,256]{1,0:T(8,128)(2,1)S(1)} %collective-permute-done.6.refs_1_), channel_id=1, source_target_pairs={{0,8},{8,16},{16,24},{24,28},{28,20},{20,12},{12,4},{4,0},{1,9},{9... | collective-permute-start | bytes 786440 | tf_op jit(solution)/shard_map/ppermute | solution.py:65
  27.6 8.2 %collective-permute-start.16 = (bf16[512,256]{1,0:T(8,128)(2,1)S(1)}, bf16[512,256]{1,0:T(8,128)(2,1)S(1)}, u32[]{:S(2)}, u32[]{:S(2)}) collective-permute-start(bf16[512,256]{1,0:T(8,128)(2,1)S(1)} %collective-permute-done.7.refs_2_), channel_id=1, source_target_pairs={{8,0},{16,8},{24,16},{28,24},{20,28},{12,20},{4,12},{0,4},{9,1},{1... | collective-permute-start | bytes 786440 | tf_op jit(solution)/shard_map/ppermute | solution.py:65
  29.7 5.0 %collective-permute-start.9 = (bf16[128,512]{1,0:T(8,128)(2,1)S(1)}, bf16[128,512]{1,0:T(8,128)(2,1)S(1)}, u32[]{:S(2)}, u32[]{:S(2)}) collective-permute-start(bf16[128,512]{1,0:T(8,128)(2,1)S(1)} %add.162.refs_4_), channel_id=1, source_target_pairs={{0,2},{1,3},{2,0},{3,1},{4,6},{5,7},{6,4},{7,5},{8,10},{9,11},{10,... | collective-permute-start | bytes 393224 | tf_op jit(solution)/shard_map/ppermute | solution.py:36
  31.2 6.0 %collective-permute-start.13 = (bf16[128,1024]{1,0:T(8,128)(2,1)S(1)}, bf16[128,1024]{1,0:T(8,128)(2,1)S(1)}, u32[]{:S(2)}, u32[]{:S(2)}) collective-permute-start(bf16[128,1024]{1,0:T(8,128)(2,1)S(1)} %collective-permute-done.12.refs_10_.refs_6_), channel_id=1, source_target_pairs={{0,1},{1,0},{2,3},{3,2},{4,5},{5,4},{6,7},{7,6},{8,9},{9,8},{10,11... | collective-permute-start | bytes 786440 | tf_op jit(solution)/shard_map/ppermute | solution.py:36
  34.7 2.6 %collective-permute-start.8 = (bf16[128,512]{1,0:T(8,128)(2,1)S(1)}, bf16[128,512]{1,0:T(8,128)(2,1)S(1)}, u32[]{:S(2)}, u32[]{:S(2)}) collective-permute-start(bf16[128,512]{1,0:T(8,128)(2,1)S(1)} %add.162.refs_4_), channel_id=1, source_target_pairs={{0,1},{1,0},{2,3},{3,2},{4,5},{5,4},{6,7},{7,6},{8,9},{9,8},{10,11... | collective-permute-start | bytes 393224 | tf_op jit(solution)/shard_map/ppermute | solution.py:36
  34.7 2.5 %collective-permute-start.10 = (bf16[128,512]{1,0:T(8,128)(2,1)S(1)}, bf16[128,512]{1,0:T(8,128)(2,1)S(1)}, u32[]{:S(2)}, u32[]{:S(2)}) collective-permute-start(bf16[128,512]{1,0:T(8,128)(2,1)S(1)} %collective-permute-done.9.refs_6_), channel_id=1, source_target_pairs={{0,1},{1,0},{2,3},{3,2},{4,5},{5,4},{6,7},{7,6},{8,9},{9,8},{10,11... | collective-permute-start | bytes 393224 | tf_op jit(solution)/shard_map/ppermute | solution.py:36
  35.2 9.2 %collective-permute-start.17 = (bf16[512,256]{1,0:T(8,128)(2,1)S(1)}, bf16[512,256]{1,0:T(8,128)(2,1)S(1)}, u32[]{:S(2)}, u32[]{:S(2)}) collective-permute-start(bf16[512,256]{1,0:T(8,128)(2,1)S(1)} %collective-permute-done.15.refs_3_), channel_id=1, source_target_pairs={{0,8},{8,16},{16,24},{24,28},{28,20},{20,12},{12,4},{4,0},{1,9},{9... | collective-permute-start | bytes 786440 | tf_op jit(solution)/shard_map/ppermute | solution.py:65
  35.8 9.2 %collective-permute-start.19 = (bf16[512,256]{1,0:T(8,128)(2,1)S(1)}, bf16[512,256]{1,0:T(8,128)(2,1)S(1)}, u32[]{:S(2)}, u32[]{:S(2)}) collective-permute-start(bf16[512,256]{1,0:T(8,128)(2,1)S(1)} %collective-permute-done.16.refs_4_), channel_id=1, source_target_pairs={{8,0},{16,8},{24,16},{28,24},{20,28},{12,20},{4,12},{0,4},{9,1},{1... | collective-permute-start | bytes 786440 | tf_op jit(solution)/shard_map/ppermute | solution.py:65
  39.0 10.9 %collective-permute-start.14 = (bf16[512,256]{1,0:T(8,128)(2,1)S(1)}, bf16[512,256]{1,0:T(8,128)(2,1)S(1)}, u32[]{:S(2)}, u32[]{:S(2)}) collective-permute-start(bf16[512,256]{1,0:T(8,128)(2,1)S(1)} %get-tuple-element.50.refs_0_), channel_id=1, source_target_pairs={{0,8},{8,16},{16,24},{24,28},{28,20},{20,12},{12,4},{4,0},{1,9},{9... | collective-permute-start | bytes 786440 | tf_op jit(solution)/shard_map/ppermute | solution.py:65
  39.7 14.9 %collective-permute-start.24 = (bf16[512,256]{1,0:T(8,128)(2,1)S(1)}, bf16[512,256]{1,0:T(8,128)(2,1)S(1)}, u32[]{:S(2)}, u32[]{:S(2)}) collective-permute-start(bf16[512,256]{1,0:T(8,128)(2,1)S(1)} %get-tuple-element.50.refs_0_), channel_id=1, source_target_pairs={{8,0},{16,8},{24,16},{28,24},{20,28},{12,20},{4,12},{0,4},{9,1},{1... | collective-permute-start | bytes 786440 | tf_op jit(solution)/shard_map/ppermute | solution.py:65
  44.4 7.6 %collective-permute-start.18 = (bf16[256,256]{1,0:T(8,128)(2,1)S(1)}, bf16[256,256]{1,0:T(8,128)(2,1)S(1)}, u32[]{:S(2)}, u32[]{:S(2)}) collective-permute-start(bf16[256,256]{1,0:T(8,128)(2,1)S(1)} %slice.16), channel_id=1, source_target_pairs={{0,8},{8,16},{16,24},{24,28},{28,20},{20,12},{12,4},{4,0},{1,9},{9... | collective-permute-start | bytes 393224 | tf_op jit(solution)/shard_map/ppermute | solution.py:65
  45.0 7.2 %collective-permute-start.20 = (bf16[256,256]{1,0:T(8,128)(2,1)S(1)}, bf16[256,256]{1,0:T(8,128)(2,1)S(1)}, u32[]{:S(2)}, u32[]{:S(2)}) collective-permute-start(bf16[256,256]{1,0:T(8,128)(2,1)S(1)} %slice.17), channel_id=1, source_target_pairs={{8,0},{16,8},{24,16},{28,24},{20,28},{12,20},{4,12},{0,4},{9,1},{1... | collective-permute-start | bytes 393224 | tf_op jit(solution)/shard_map/ppermute | solution.py:65
  52.2 7.3 %collective-permute-start.21 = (bf16[512,256]{1,0:T(8,128)(2,1)S(1)}, bf16[512,256]{1,0:T(8,128)(2,1)S(1)}, u32[]{:S(2)}, u32[]{:S(2)}) collective-permute-start(bf16[512,256]{1,0:T(8,128)(2,1)S(1)} %collective-permute-done.14.refs_1_), channel_id=1, source_target_pairs={{0,8},{8,16},{16,24},{24,28},{28,20},{20,12},{12,4},{4,0},{1,9},{9... | collective-permute-start | bytes 786440 | tf_op jit(solution)/shard_map/ppermute | solution.py:65
  54.6 7.4 %collective-permute-start.25 = (bf16[512,256]{1,0:T(8,128)(2,1)S(1)}, bf16[512,256]{1,0:T(8,128)(2,1)S(1)}, u32[]{:S(2)}, u32[]{:S(2)}) collective-permute-start(bf16[512,256]{1,0:T(8,128)(2,1)S(1)} %collective-permute-done.24.refs_2_), channel_id=1, source_target_pairs={{8,0},{16,8},{24,16},{28,24},{20,28},{12,20},{4,12},{0,4},{9,1},{1... | collective-permute-start | bytes 786440 | tf_op jit(solution)/shard_map/ppermute | solution.py:65
  59.5 6.6 %collective-permute-start.22 = (bf16[512,256]{1,0:T(8,128)(2,1)S(1)}, bf16[512,256]{1,0:T(8,128)(2,1)S(1)}, u32[]{:S(2)}, u32[]{:S(2)}) collective-permute-start(bf16[512,256]{1,0:T(8,128)(2,1)S(1)} %collective-permute-done.21.refs_3_), channel_id=1, source_target_pairs={{0,8},{8,16},{16,24},{24,28},{28,20},{20,12},{12,4},{4,0},{1,9},{9... | collective-permute-start | bytes 786440 | tf_op jit(solution)/shard_map/ppermute | solution.py:65
  62.0 6.6 %collective-permute-start.26 = (bf16[512,256]{1,0:T(8,128)(2,1)S(1)}, bf16[512,256]{1,0:T(8,128)(2,1)S(1)}, u32[]{:S(2)}, u32[]{:S(2)}) collective-permute-start(bf16[512,256]{1,0:T(8,128)(2,1)S(1)} %collective-permute-done.25.refs_4_), channel_id=1, source_target_pairs={{8,0},{16,8},{24,16},{28,24},{20,28},{12,20},{4,12},{0,4},{9,1},{1... | collective-permute-start | bytes 786440 | tf_op jit(solution)/shard_map/ppermute | solution.py:65
  66.2 7.4 %collective-permute-start.23 = (bf16[256,256]{1,0:T(8,128)(2,1)S(1)}, bf16[256,256]{1,0:T(8,128)(2,1)S(1)}, u32[]{:S(2)}, u32[]{:S(2)}) collective-permute-start(bf16[256,256]{1,0:T(8,128)(2,1)S(1)} %slice.14), channel_id=1, source_target_pairs={{0,8},{8,16},{16,24},{24,28},{28,20},{20,12},{12,4},{4,0},{1,9},{9... | collective-permute-start | bytes 393224 | tf_op jit(solution)/shard_map/ppermute | solution.py:65
  68.6 5.0 %collective-permute-start.27 = (bf16[256,256]{1,0:T(8,128)(2,1)S(1)}, bf16[256,256]{1,0:T(8,128)(2,1)S(1)}, u32[]{:S(2)}, u32[]{:S(2)}) collective-permute-start(bf16[256,256]{1,0:T(8,128)(2,1)S(1)} %slice.15), channel_id=1, source_target_pairs={{8,0},{16,8},{24,16},{28,24},{20,28},{12,20},{4,12},{0,4},{9,1},{1... | collective-permute-start | bytes 393224 | tf_op jit(solution)/shard_map/ppermute | solution.py:65

commit v4 on v3

--- a/solution.py
+++ b/solution.py
@@ -84,10 +84,14 @@
     places = jnp.arange(slots, dtype=jnp.int32)
     late = products >= first
     place = jnp.sum(late[None, :] & (places[None, :] < places[:, None]), -1, dtype=jnp.int32)
-    code = products * slots + places
     here = late[None, :] & (place[None, :] == places[:, None])
-    table = jnp.sum(jnp.where(here, code[None, :], 0), -1, dtype=jnp.int32)
-    return table, jnp.sum(late, dtype=jnp.int32).reshape(1)
+    listed = lambda values: jnp.sum(jnp.where(here, values[None, :], 0), -1, dtype=jnp.int32)
+    return listed(places), listed(products - first), jnp.sum(late, dtype=jnp.int32).reshape(1)
+
+
+def within(products, first, count):
+    place = products - first
+    return jnp.where((place >= 0) & (place < count), place, count)
 
 
 def staged(value):
@@ -273,94 +277,104 @@
         n += 1
 
 
-def dense_kernel(block, tiles, blank, per_step, table_ref, left_ref, *refs):
-    pieces = refs[:tiles]
-    base_ref, out_hbm, products_ref, *held = refs[tiles:]
+def dense_kernel(block, groups, per_step, *refs):
+    tables, refs = refs[: len(groups)], refs[len(groups) :]
+    lefts, pieces = [], []
+    for tiles in groups:
+        lefts, pieces, refs = lefts + [refs[0]], pieces + [refs[1 : 1 + tiles]], refs[1 + tiles :]
+    base_ref, out_hbm, *products = refs[: 2 + len(groups)]
+    held = refs[2 + len(groups) :]
     out_ref = held[0] if held else out_hbm
-    last = products_ref.shape[0] - 1
-    if blank:
+    for left_ref, tiles, products_ref in zip(lefts, pieces, products):
+        last = products_ref.shape[0] - 1
         products_ref[last] = jnp.zeros_like(products_ref[last])
-    products_of(left_ref, pieces, products_ref, block)
+        products_of(left_ref, tiles, products_ref, block)
+
+    def copy(i):
+        part = pl.ds(i * per_step, per_step)
+        return pltpu.make_async_copy(out_ref.at[part], out_hbm.at[part], held[1].at[i])
 
     def step(i, _):
         for u in range(per_step):
             s = i * per_step + u
-            product = products_ref[jnp.minimum(table_ref[s], last)]
-            out_ref[s] = (base_ref[s].astype(F32) - product).astype(BF16)
+            value = base_ref[s].astype(F32)
+            for table_ref, products_ref in zip(tables, products):
+                value = value - products_ref[table_ref[s]]
+            out_ref[s] = value.astype(BF16)
         if held:
             copy(i).start()
         return _
 
-    def copy(i):
-        part = pl.ds(i * per_step, per_step)
-        return pltpu.make_async_copy(out_ref.at[part], out_hbm.at[part], held[1].at[i])
-
-    steps = table_ref.shape[0] // per_step
+    steps = tables[0].shape[0] // per_step
     lax.fori_loop(0, steps, step, 0)
     for i in range(steps if held else 0):
         copy(i).wait()
 
 
-def dense(table, left, pieces, count, blank, base, per_step=16):
+def dense(groups, base, final, per_step=16):
     slots, block, _ = base.shape
-    local = left.shape[1] // block
-    each = pieces[0].shape[1] // block
-    return call(
-        functools.partial(dense_kernel, block, len(pieces), blank, per_step),
+    products = []
+    for _, left, pieces in groups:
+        rows = left.shape[1] // block * (pieces[0].shape[1] // block)
+        tiles = sum(p.shape[0] for p in pieces) // left.shape[0]
+        products.append(pltpu.VMEM((tiles * rows + 1, block, block), F32))
+    held = [pltpu.VMEM(base.shape, BF16), pltpu.SemaphoreType.DMA((slots // per_step,))]
+    operands = [x for _, left, pieces in groups for x in (left, *pieces)]
+    return call(
+        functools.partial(dense_kernel, block, [len(p) for _, _, p in groups], per_step),
         "dense",
         24,
         5,
         out_shape=jax.ShapeDtypeStruct(base.shape, BF16),
-        in_specs=[SMEM] + [VMEM] * (2 + len(pieces)),
-        out_specs=HBM if blank else VMEM,
-        scratch_shapes=[pltpu.VMEM((count * each * local + blank, block, block), F32)]
-        + ([pltpu.VMEM(base.shape, BF16), pltpu.SemaphoreType.DMA((slots // per_step,))] if blank else []),
-    )(table, left, *pieces, base)
-
-
-def last_kernel(block, tiles, first, table_ref, count_ref, left_ref, *refs):
+        in_specs=[SMEM] * len(groups) + [VMEM] * (1 + len(operands)),
+        out_specs=HBM if final else VMEM,
+        scratch_shapes=products + (held if final else []),
+    )(*[table for table, _, _ in groups], *operands, base)
+
+
+def last_kernel(block, tiles, slots_ref, places_ref, count_ref, left_ref, *refs):
     pieces = refs[:tiles]
     base_ref, _, out_hbm = refs[tiles : tiles + 3]
     products_ref, held_ref, sem = refs[tiles + 3 :]
-    slots = table_ref.shape[0]
+    count = count_ref[0]
     products_of(left_ref, pieces, products_ref, block)
 
     def update(i, _):
-        code = table_ref[i]
-        s = code % slots
-        product = products_ref[code // slots - first]
+        s = slots_ref[i]
+        product = products_ref[places_ref[i]]
         held_ref[s] = (base_ref[s].astype(F32) - product).astype(BF16)
         pltpu.make_async_copy(held_ref.at[s], out_hbm.at[s], sem).start()
         return _
 
-    def finish(i, _):
-        pltpu.make_async_copy(held_ref.at[0], out_hbm.at[0], sem).wait()
+    def finish(size, i, _):
+        part = pl.ds(0, size)
+        pltpu.make_async_copy(held_ref.at[part], out_hbm.at[part], sem).wait()
         return _
 
-    lax.fori_loop(0, count_ref[0], update, 0)
-    lax.fori_loop(0, count_ref[0], finish, 0)
-
-
-def last(table, count, left, pieces, base, done):
+    lax.fori_loop(0, count, update, 0)
+    lax.fori_loop(0, count // 8, functools.partial(finish, 8), 0)
+    lax.fori_loop(0, count % 8, functools.partial(finish, 1), 0)
+
+
+def last(late, left, pieces, base, done):
     slots, block, _ = base.shape
     local = left.shape[1] // block
     each = pieces[0].shape[1] // block
-    rank = lax.axis_size("row") - 1
-    return call(
-        functools.partial(last_kernel, block, len(pieces), rank * each * local),
+    return call(
+        functools.partial(last_kernel, block, len(pieces)),
         "last",
         12,
         3,
         out_shape=jax.ShapeDtypeStruct(base.shape, BF16),
-        in_specs=[SMEM] * 2 + [VMEM] * (2 + len(pieces)) + [HBM],
+        in_specs=[SMEM] * 3 + [VMEM] * (2 + len(pieces)) + [HBM],
         out_specs=HBM,
-        input_output_aliases={4 + len(pieces): 0},
+        input_output_aliases={5 + len(pieces): 0},
         scratch_shapes=[
             pltpu.VMEM((each * local, block, block), F32),
             pltpu.VMEM((slots, block, block), BF16),
             pltpu.SemaphoreType.DMA,
         ],
-    )(table, count, left, *pieces, base, done)
+    )(*late, left, *pieces, base, done)
 
 
 def per_device(
@@ -395,17 +409,14 @@
     def meet(arrived, *earlier):
         arrived[-2:] = [after(piece, *earlier) for piece in arrived[-2:]]
 
+    far_one = far_pieces(panel_one)
     raw = bridge_columns(panel_one, column_blocks, block)
-    far_one = far_pieces(after(panel_one, raw))
     inverse_one_here = staged(inverse_one)
     own_one_here = staged(panel_one)
     masks = [1 << i for i in range(lax.axis_size("row").bit_length() - 1)][::-1]
     for at, mask in enumerate(masks):
         other = xor_permute(raw, "row", mask)
         if at == 0:
-            other = after(other, inverse_one_here, own_one_here)
-        if at == 1:
-            far_one = {m: after(p, raw) for m, p in far_one.items()}
             pieces_one = near_pieces(far_one)
             lower_one, own_one, tile_one = factor_one(
                 inverse_one_here, [own_one_here] + pieces_one[1:], block
@@ -422,35 +433,40 @@
             second = after(rows_two, raw).reshape(-1), cols_two.reshape(-1)
             slots_one = slot_products(*first, local)
             slots_two = slot_products(*second, local)
-            late, late_count = late_slots(
-                slots_two, (lax.axis_size("row") - 1) * (local // lax.axis_size("col")) * local
-            )
+            tile_products = local // lax.axis_size("col") * local
+            late = late_slots(slots_two, (2 * steps - 1) * tile_products)
+            early = within(slots_two, 0, 3 * tile_products)
+            middle = within(slots_two, 3 * tile_products, (2 * steps - 1 - 3) * tile_products)
             row_map = after(row_map, raw) % local
-            other = after(other, slots_one, slots_two, late, late_count, row_map)
+            other = after(other, slots_one, early, middle, *late, row_map)
+            other = after(other, *ring_one[1:3])
         raw = raw + other
     base = staged(base)
     go_on(ring_one)
     pieces_two = [own_two_here] + near_pieces(far_two)[1:]
     far_raw = far_pieces(raw)
-    far_raw = {m: after(p, *ring_one[1:3]) for m, p in far_raw.items()}
+    far_raw = {m: after(p, base) for m, p in far_raw.items()}
     tile, bridge = tile_two(
         row_map, inverse_one_here, inverse_two_here, lower_one, near_pieces(far_raw), pieces_two, block
     )
+    tile = after(tile, *ring_one[3:5])
     ring_two = [tile]
     go_on(ring_two)
     lower_two, own_two = factor_two(row_map, inverse_two_here, lower_one, bridge, pieces_two, block)
     while len(ring_one) < 2 * steps + 1:
         go_on(ring_one)
-    part = dense(slots_one, lower_one, ring_one, 2 * steps, 0, base)
     meet(ring_two, own_two, *ring_one[3:5], *ring_one[7:])
+    part = dense(
+        [(slots_one, lower_one, ring_one), (early, lower_two, ring_two[:3])], base, final=False
+    )
     for k in range(2, steps):
         go_on(ring_two)
-        if k == steps - 1:
+        if k == 2:
             meet(ring_two, part)
     go_on(ring_two)
-    done = dense(slots_two, lower_two, ring_two[:-2], 2 * steps - 1, 1, part)
+    done = dense([(middle, lower_two, ring_two[3:-2])], part, final=True)
     meet(ring_two, done)
-    done = last(late, late_count, lower_two, ring_two[-2:], part, done)
+    done = last(late, lower_two, ring_two[-2:], part, done)
     return own_one, own_two, done.reshape(targets.shape)
 
 

time: 76.4 us -> 75.5 us (0.988)
  starting transfers between devices: 30.2 us -> 25 us
  waiting for transfers between devices: 22.5 us -> 24.7 us
  other arithmetic: 3.42 us -> 4.75 us
  local copies, waits for them, and re-layouts: 0.72 us -> 1.7 us
    ppermute x8, waiting for transfers between devices: 0.33 us -> 13.4 us  [ring_step(): lax.ppermute(backward, 'row', back)]
    ppermute x8, waiting for transfers between devices: 13.1 us -> 1.57 us  [ring_step(): lax.ppermute(forward, 'row', ahead)]
    ppermute x8, starting transfers between devices: 11.5 us -> 7.27 us  [ring_step(): lax.ppermute(forward, 'row', ahead)]
    ppermute x12, starting transfers between devices: 12.5 us -> 8.63 us  [xor_permute(): lax.ppermute(value, axis, [(i, i ^ mask) for i in range(lax.axis_size(axi...]
    ppermute x8, starting transfers between devices: 6.22 us -> 9.1 us  [ring_step(): lax.ppermute(backward, 'row', back)]
    mul x5, other arithmetic: 2.38 us -> 3.62 us  [staged(): return value * lax.optimization_barrier(jnp.ones((), value.dtype))]
    unnamed x18, local copies, waits for them, and re-layouts: 0.68 us -> 1.66 us
    ppermute x12, waiting for transfers between devices: 9.02 us -> 9.79 us  [xor_permute(): lax.ppermute(value, axis, [(i, i ^ mask) for i in range(lax.axis_size(axi...]
  transfers between devices with their start and end apart: 28 -> 28, of which waited for: 12 -> 13; matrix products, arithmetic and copies ran while one was open for 5% -> 6% of each run, Pallas kernels for 19% -> 21%
where the time goes in v4:
time: 75.5 us; the launch traced here: 75.3 us
  starting transfers between devices  25 us (33%)
  waiting for transfers between devices  24.7 us (33%)
  Pallas kernels  18.2 us (24%)
  other arithmetic  4.75 us (6%)
  local copies, waits for them, and re-layouts  1.7 us (2%)
  between operations  0.86 us (1%)
    ppermute x8, waiting for transfers between devices, ring_step(): lax.ppermute(backward, 'row', back)  13.4 us
    ppermute x12, waiting for transfers between devices, xor_permute(): lax.ppermute(value, axis, [(i, i ^ mask) for i in range(lax.axis_size(axi...  9.79 us
    ppermute x8, starting transfers between devices, ring_step(): lax.ppermute(backward, 'row', back)  9.1 us
    pallas_call x2, Pallas kernels, dense(): call(functools.partial(dense_kernel, block, [len(p) for _, _, p in groups...  9.03 us
    ppermute x12, starting transfers between devices, xor_permute(): lax.ppermute(value, axis, [(i, i ^ mask) for i in range(lax.axis_size(axi...  8.63 us
    ppermute x8, starting transfers between devices, ring_step(): lax.ppermute(forward, 'row', ahead)  7.27 us
    mul x5, other arithmetic, staged(): return value * lax.optimization_barrier(jnp.ones((), value.dtype))  3.62 us
    pallas_call x1, Pallas kernels, factor_two(): call(functools.partial(factor_two_kernel, block, count), 'factor_two', 12...  2.74 us
  transfers between devices with their start and end apart: 28, of which 13 were waited for; matrix products, arithmetic and copies ran while one was open for 6% of the time, Pallas kernels for 21%

profile of v4, /device:TPU:0, one launch (start us, length us, event | category | flops | bytes accessed | tf_op | source)
XLA Modules:
  0.0 75.3 jit_solution(15330432333685598291)
XLA Ops:
  0.6 3.0 %collective-permute-start.1 = (bf16[128,1024]{1,0:T(8,128)(2,1)}, bf16[128,1024]{1,0:T(8,128)(2,1)S(1)}, u32[]{:S(2)}, u32[]{:S(2)}) collective-permute-start(bf16[128,1024]{1,0:T(8,128)(2,1)} %panel_ref.1), channel_id=1, source_target_pairs={{0,2},{1,3},{2,0},{3,1},{4,6},{5,7},{6,4},{7,5},{8,10},{9,11},{10,... | collective-permute-start | bytes 786440 | tf_op jit(solution)/shard_map/ppermute | solution.py:36
  3.6 1.0 %copy-done = bf16[128,1024]{1,0:T(8,128)(2,1)S(1)} copy-done((bf16[128,1024]{1,0:T(8,128)(2,1)S(1)}, bf16[128,1024]{1,0:T(8,128)(2,1)}, u32[]{:S(2)}) %copy-start) | copy-done | bytes 262168
  4.6 0.7 copy-done.1
  5.3 0.6 bridge_columns.1
  5.9 2.7 %collective-permute-start.3 = (bf16[128,512]{1,0:T(8,128)(2,1)S(1)}, bf16[128,512]{1,0:T(8,128)(2,1)S(1)}, u32[]{:S(2)}, u32[]{:S(2)}) collective-permute-start(bf16[128,512]{1,0:T(8,128)(2,1)S(1)} %bridge_columns.1), channel_id=1, source_target_pairs={{0,16},{4,20},{8,24},{12,28},{16,0},{20,4},{24,8},{28,12},{1,17},{... | collective-permute-start | bytes 393224 | tf_op jit(solution)/shard_map/ppermute | solution.py:36
  8.6 1.6 %collective-permute-done.1.refs_3_ = bf16[128,1024]{1,0:T(8,128)(2,1)S(1)} collective-permute-done((bf16[128,1024]{1,0:T(8,128)(2,1)}, bf16[128,1024]{1,0:T(8,128)(2,1)S(1)}, u32[]{:S(2)}, u32[]{:S(2)}) %collective-permute-start.1) | collective-permute-done | bytes 262176 | tf_op jit(solution)/shard_map/ppermute | solution.py:36
  10.2 1.1 %broadcast_multiply_fusion.1.refs_0_.refs_1_ = bf16[512,512]{1,0:T(8,128)(2,1)S(1)} fusion(bf16[512,512]{1,0:T(8,128)(2,1)} %param.13, bf16[]{:T(256)} %constant.164.clone.1), kind=kLoop, calls=%fused_computation.2 | loop fusion | flops 262144 | bytes 1048578 | tf_op jit(solution)/shard_map/mul | solution.py:98
  11.3 0.4 collective-permute-done.2.refs_4_
  11.7 1.6 %factor_one.1 = (bf16[512,1024]{1,0:T(8,128)(2,1)S(1)}, bf16[128,1024]{1,0:T(8,128)(2,1)}, bf16[512,256]{1,0:T(8,128)(2,1)S(1)}) custom-call(bf16[512,512]{1,0:T(8,128)(2,1)S(1)} %broadcast_multiply_fusion.1.refs_0_.refs_1_, bf16[128,1024]{1,0:T(8,128)(2,1)S(1)} %broadcast_multiply_fusion.3.refs_1_, bf16[128,1024]{1,0:T(8,128)(2,1)S(1)} %collective-permute-done.refs_2_, ...), custom_call_target="tpu_custom_call" | custom-call | bytes 1600000 | tf_op jit(solution)/shard_map/factor_one/pallas_call | solution.py:165
  13.3 2.3 %collective-permute-done.3 = bf16[128,512]{1,0:T(8,128)(2,1)S(1)} collective-permute-done((bf16[128,512]{1,0:T(8,128)(2,1)S(1)}, bf16[128,512]{1,0:T(8,128)(2,1)S(1)}, u32[]{:S(2)}, u32[]{:S(2)}) %collective-permute-start.3) | collective-permute-done | bytes 131104 | tf_op jit(solution)/shard_map/ppermute | solution.py:36
  15.6 0.8 %collective-permute-start.4 = (bf16[128,512]{1,0:T(8,128)(2,1)S(1)}, bf16[128,512]{1,0:T(8,128)(2,1)S(1)}, u32[]{:S(2)}, u32[]{:S(2)}) collective-permute-start(bf16[128,512]{1,0:T(8,128)(2,1)S(1)} %add.151), channel_id=1, source_target_pairs={{0,8},{4,12},{8,0},{12,4},{16,24},{20,28},{24,16},{28,20},{1,9},{5... | collective-permute-start | bytes 393224 | tf_op jit(solution)/shard_map/ppermute | solution.py:36
  16.4 1.5 %collective-permute-start.7 = (bf16[512,256]{1,0:T(8,128)(2,1)S(1)}, bf16[512,256]{1,0:T(8,128)(2,1)S(1)}, u32[]{:S(2)}, u32[]{:S(2)}) collective-permute-start(bf16[512,256]{1,0:T(8,128)(2,1)S(1)} %get-tuple-element.29.refs_3_), channel_id=1, source_target_pairs={{8,0},{16,8},{24,16},{28,24},{20,28},{12,20},{4,12},{0,4},{9,1},{1... | collective-permute-start | bytes 786440 | tf_op jit(solution)/shard_map/ppermute | solution.py:65
  17.9 0.5 collective-permute-start.6
  18.4 3.7 %collective-permute-done.4 = bf16[128,512]{1,0:T(8,128)(2,1)S(1)} collective-permute-done((bf16[128,512]{1,0:T(8,128)(2,1)S(1)}, bf16[128,512]{1,0:T(8,128)(2,1)S(1)}, u32[]{:S(2)}, u32[]{:S(2)}) %collective-permute-start.4) | collective-permute-done | bytes 131104 | tf_op jit(solution)/shard_map/ppermute | solution.py:36
  22.1 0.7 convert_reduce_fusion.1
  22.9 0.3 collective-permute-start.5
  23.3 0.6 collective-permute-start.12
  24.1 0.1 select_reduce_fusion
  24.2 2.2 %collective-permute-done.7.refs_5_ = bf16[512,256]{1,0:T(8,128)(2,1)S(1)} collective-permute-done((bf16[512,256]{1,0:T(8,128)(2,1)S(1)}, bf16[512,256]{1,0:T(8,128)(2,1)S(1)}, u32[]{:S(2)}, u32[]{:S(2)}) %collective-permute-start.7) | collective-permute-done | bytes 262176 | tf_op jit(solution)/shard_map/ppermute | solution.py:65
  26.4 0.7 collective-permute-start.15
  27.1 1.3 %collective-permute-start.14 = (bf16[512,256]{1,0:T(8,128)(2,1)S(1)}, bf16[512,256]{1,0:T(8,128)(2,1)S(1)}, u32[]{:S(2)}, u32[]{:S(2)}) collective-permute-start(bf16[512,256]{1,0:T(8,128)(2,1)S(1)} %collective-permute-done.6.refs_4_), channel_id=1, source_target_pairs={{0,8},{8,16},{16,24},{24,28},{28,20},{20,12},{12,4},{4,0},{1,9},{9... | collective-permute-start | bytes 786440 | tf_op jit(solution)/shard_map/ppermute | solution.py:65
  28.5 0.8 %collective-permute-start.9 = (bf16[128,512]{1,0:T(8,128)(2,1)S(1)}, bf16[128,512]{1,0:T(8,128)(2,1)S(1)}, u32[]{:S(2)}, u32[]{:S(2)}) collective-permute-start(bf16[128,512]{1,0:T(8,128)(2,1)S(1)} %add.167.refs_4_), channel_id=1, source_target_pairs={{0,2},{1,3},{2,0},{3,1},{4,6},{5,7},{6,4},{7,5},{8,10},{9,11},{10,... | collective-permute-start | bytes 393224 | tf_op jit(solution)/shard_map/ppermute | solution.py:36
  29.2 1.0 %collective-permute-done.12.refs_10_.refs_6_ = bf16[128,1024]{1,0:T(8,128)(2,1)S(1)} collective-permute-done((bf16[128,1024]{1,0:T(8,128)(2,1)S(1)}, bf16[128,1024]{1,0:T(8,128)(2,1)S(1)}, u32[]{:S(2)}, u32[]{:S(2)}) %collective-permute-start.12) | collective-permute-done | bytes 262176 | tf_op jit(solution)/shard_map/ppermute | solution.py:36
  30.3 2.5 %multiply_bitcast_fusion.refs_16_ = bf16[128,128,128]{2,1,0:T(8,128)(2,1)S(1)} fusion(bf16[1,1,128,128,128]{4,3,2,1,0:T(8,128)(2,1)} %param.17, bf16[]{:T(256)} %constant.164.clone.1), kind=kLoop, calls=%fused_computation | loop fusion | flops 2097152 | bytes 8388610 | tf_op jit(solution)/shard_map/mul | solution.py:98
  32.7 0.8 %collective-permute-done.9.refs_6_ = bf16[128,512]{1,0:T(8,128)(2,1)S(1)} collective-permute-done((bf16[128,512]{1,0:T(8,128)(2,1)S(1)}, bf16[128,512]{1,0:T(8,128)(2,1)S(1)}, u32[]{:S(2)}, u32[]{:S(2)}) %collective-permute-start.9) | collective-permute-done | bytes 131104 | tf_op jit(solution)/shard_map/ppermute | solution.py:36
  33.5 0.5 collective-permute-start.10
  34.0 1.3 %collective-permute-start.19 = (bf16[512,256]{1,0:T(8,128)(2,1)S(1)}, bf16[512,256]{1,0:T(8,128)(2,1)S(1)}, u32[]{:S(2)}, u32[]{:S(2)}) collective-permute-start(bf16[512,256]{1,0:T(8,128)(2,1)S(1)} %collective-permute-done.15.refs_7_), channel_id=1, source_target_pairs={{8,0},{16,8},{24,16},{28,24},{20,28},{12,20},{4,12},{0,4},{9,1},{1... | collective-permute-start | bytes 786440 | tf_op jit(solution)/shard_map/ppermute | solution.py:65
  35.4 0.7 collective-permute-start.17
  36.1 1.8 %tile_two.1 = (bf16[512,256]{1,0:T(8,128)(2,1)S(1)}, bf16[512,512]{1,0:T(8,128)(2,1)S(1)}) custom-call(s32[8]{0:T(128)S(1)} %and_select_fusion.16.refs_0_, bf16[512,512]{1,0:T(8,128)(2,1)S(1)} %broadcast_multiply_fusion.1.refs_0_.refs_1_, bf16[512,512]{1,0:T(8,128)(2,1)S(1)} %broadcast_multiply_fusion.refs_2_.refs_1_, ...), custom_call_target="tpu_custom_call" | custom-call | bytes 1600000 | tf_op jit(solution)/shard_map/tile_two/pallas_call | solution.py:204
  37.8 1.4 %collective-permute-start.22 = (bf16[512,256]{1,0:T(8,128)(2,1)S(1)}, bf16[512,256]{1,0:T(8,128)(2,1)S(1)}, u32[]{:S(2)}, u32[]{:S(2)}) collective-permute-start(bf16[512,256]{1,0:T(8,128)(2,1)S(1)} %get-tuple-element.46.refs_13_), channel_id=1, source_target_pairs={{8,0},{16,8},{24,16},{28,24},{20,28},{12,20},{4,12},{0,4},{9,1},{1... | collective-permute-start | bytes 786440 | tf_op jit(solution)/shard_map/ppermute | solution.py:65
  39.2 0.7 collective-permute-start.16
  39.9 3.3 %collective-permute-done.19.refs_9_ = bf16[512,256]{1,0:T(8,128)(2,1)S(1)} collective-permute-done((bf16[512,256]{1,0:T(8,128)(2,1)S(1)}, bf16[512,256]{1,0:T(8,128)(2,1)S(1)}, u32[]{:S(2)}, u32[]{:S(2)}) %collective-permute-start.19) | collective-permute-done | bytes 262176 | tf_op jit(solution)/shard_map/ppermute | solution.py:65
  43.2 1.3 %collective-permute-start.20 = (bf16[256,256]{1,0:T(8,128)(2,1)S(1)}, bf16[256,256]{1,0:T(8,128)(2,1)S(1)}, u32[]{:S(2)}, u32[]{:S(2)}) collective-permute-start(bf16[256,256]{1,0:T(8,128)(2,1)S(1)} %slice.17), channel_id=1, source_target_pairs={{8,0},{16,8},{24,16},{28,24},{20,28},{12,20},{4,12},{0,4},{9,1},{1... | collective-permute-start | bytes 393224 | tf_op jit(solution)/shard_map/ppermute | solution.py:65
  44.6 0.8 %collective-permute-start.18 = (bf16[256,256]{1,0:T(8,128)(2,1)S(1)}, bf16[256,256]{1,0:T(8,128)(2,1)S(1)}, u32[]{:S(2)}, u32[]{:S(2)}) collective-permute-start(bf16[256,256]{1,0:T(8,128)(2,1)S(1)} %slice.16), channel_id=1, source_target_pairs={{0,8},{8,16},{16,24},{24,28},{28,20},{20,12},{12,4},{4,0},{1,9},{9... | collective-permute-start | bytes 393224 | tf_op jit(solution)/shard_map/ppermute | solution.py:65
  45.3 2.7 %factor_two.1 = (bf16[512,1024]{1,0:T(8,128)(2,1)S(1)}, bf16[128,1024]{1,0:T(8,128)(2,1)}) custom-call(s32[8]{0:T(128)S(1)} %and_select_fusion.16.refs_0_, bf16[512,512]{1,0:T(8,128)(2,1)S(1)} %broadcast_multiply_fusion.refs_2_.refs_1_, bf16[512,1024]{1,0:T(8,128)(2,1)S(1)} %get-tuple-element.33.refs_3_.refs_2_, ...), custom_call_target="tpu_custom_call" | custom-call | bytes 2400000 | tf_op jit(solution)/shard_map/factor_two/pallas_call | solution.py:244
  48.1 2.6 %collective-permute-done.20.refs_11_ = bf16[256,256]{1,0:T(8,128)(2,1)S(1)} collective-permute-done((bf16[256,256]{1,0:T(8,128)(2,1)S(1)}, bf16[256,256]{1,0:T(8,128)(2,1)S(1)}, u32[]{:S(2)}, u32[]{:S(2)}) %collective-permute-start.20) | collective-permute-done | bytes 131104 | tf_op jit(solution)/shard_map/ppermute | solution.py:65
  50.7 1.4 %collective-permute-done.18.refs_10_ = bf16[256,256]{1,0:T(8,128)(2,1)S(1)} collective-permute-done((bf16[256,256]{1,0:T(8,128)(2,1)S(1)}, bf16[256,256]{1,0:T(8,128)(2,1)S(1)}, u32[]{:S(2)}, u32[]{:S(2)}) %collective-permute-start.18) | collective-permute-done | bytes 131104 | tf_op jit(solution)/shard_map/ppermute | solution.py:65
  52.2 1.0 %collective-permute-start.25 = (bf16[512,256]{1,0:T(8,128)(2,1)S(1)}, bf16[512,256]{1,0:T(8,128)(2,1)S(1)}, u32[]{:S(2)}, u32[]{:S(2)}) collective-permute-start(bf16[512,256]{1,0:T(8,128)(2,1)S(1)} %collective-permute-done.22.refs_15_), channel_id=1, source_target_pairs={{8,0},{16,8},{24,16},{28,24},{20,28},{12,20},{4,12},{0,4},{9,1},{1... | collective-permute-start | bytes 786440 | tf_op jit(solution)/shard_map/ppermute | solution.py:65
  53.2 1.0 %collective-permute-start.21 = (bf16[512,256]{1,0:T(8,128)(2,1)S(1)}, bf16[512,256]{1,0:T(8,128)(2,1)S(1)}, u32[]{:S(2)}, u32[]{:S(2)}) collective-permute-start(bf16[512,256]{1,0:T(8,128)(2,1)S(1)} %collective-permute-done.16.refs_14_), channel_id=1, source_target_pairs={{0,8},{8,16},{16,24},{24,28},{28,20},{20,12},{12,4},{4,0},{1,9},{9... | collective-permute-start | bytes 786440 | tf_op jit(solution)/shard_map/ppermute | solution.py:65
  54.2 5.0 %dense.2.refs_6_.refs_2_ = bf16[128,128,128]{2,1,0:T(8,128)(2,1)S(1)} custom-call(s32[128]{0:T(128)S(1)} %fusion.2.refs_0_, s32[128]{0:T(128)S(1)} %get-tuple-element.59.refs_1_, bf16[512,1024]{1,0:T(8,128)(2,1)S(1)} %get-tuple-element.33.refs_3_.refs_2_, bf16[512,256]{1,0:T(8,128)(2,1)S(1)} %get-tuple-element.29.refs_3_, ...), custom_call_target="tpu_custom_call" | custom-call | bytes 5000000 | tf_op jit(solution)/shard_map/dense/pallas_call | solution.py:323
  59.2 0.5 collective-permute-done.25.refs_3_
  59.7 0.8 %collective-permute-start.26 = (bf16[512,256]{1,0:T(8,128)(2,1)S(1)}, bf16[512,256]{1,0:T(8,128)(2,1)S(1)}, u32[]{:S(2)}, u32[]{:S(2)}) collective-permute-start(bf16[512,256]{1,0:T(8,128)(2,1)S(1)} %collective-permute-done.25.refs_3_), channel_id=1, source_target_pairs={{8,0},{16,8},{24,16},{28,24},{20,28},{12,20},{4,12},{0,4},{9,1},{1... | collective-permute-start | bytes 786440 | tf_op jit(solution)/shard_map/ppermute | solution.py:65
  60.6 1.1 %collective-permute-start.23 = (bf16[512,256]{1,0:T(8,128)(2,1)S(1)}, bf16[512,256]{1,0:T(8,128)(2,1)S(1)}, u32[]{:S(2)}, u32[]{:S(2)}) collective-permute-start(bf16[512,256]{1,0:T(8,128)(2,1)S(1)} %collective-permute-done.21.refs_2_), channel_id=1, source_target_pairs={{0,8},{8,16},{16,24},{24,28},{28,20},{20,12},{12,4},{4,0},{1,9},{9... | collective-permute-start | bytes 786440 | tf_op jit(solution)/shard_map/ppermute | solution.py:65
  61.7 4.8 %collective-permute-done.26.refs_5_ = bf16[512,256]{1,0:T(8,128)(2,1)S(1)} collective-permute-done((bf16[512,256]{1,0:T(8,128)(2,1)S(1)}, bf16[512,256]{1,0:T(8,128)(2,1)S(1)}, u32[]{:S(2)}, u32[]{:S(2)}) %collective-permute-start.26) | collective-permute-done | bytes 262176 | tf_op jit(solution)/shard_map/ppermute | solution.py:65
  66.6 1.0 %collective-permute-start.27 = (bf16[256,256]{1,0:T(8,128)(2,1)S(1)}, bf16[256,256]{1,0:T(8,128)(2,1)S(1)}, u32[]{:S(2)}, u32[]{:S(2)}) collective-permute-start(bf16[256,256]{1,0:T(8,128)(2,1)S(1)} %slice.19), channel_id=1, source_target_pairs={{8,0},{16,8},{24,16},{28,24},{20,28},{12,20},{4,12},{0,4},{9,1},{1... | collective-permute-start | bytes 393224 | tf_op jit(solution)/shard_map/ppermute | solution.py:65
  67.5 1.2 %collective-permute-start.24 = (bf16[256,256]{1,0:T(8,128)(2,1)S(1)}, bf16[256,256]{1,0:T(8,128)(2,1)S(1)}, u32[]{:S(2)}, u32[]{:S(2)}) collective-permute-start(bf16[256,256]{1,0:T(8,128)(2,1)S(1)} %slice.18), channel_id=1, source_target_pairs={{0,8},{8,16},{16,24},{24,28},{28,20},{20,12},{12,4},{4,0},{1,9},{9... | collective-permute-start | bytes 393224 | tf_op jit(solution)/shard_map/ppermute | solution.py:65
  68.7 4.0 %dense.3.refs_3_ = bf16[128,128,128]{2,1,0:T(8,128)(2,1)} custom-call(s32[128]{0:T(128)S(1)} %get-tuple-element.58.refs_0_, bf16[512,1024]{1,0:T(8,128)(2,1)S(1)} %get-tuple-element.44.refs_12_.refs_1_.left_ref, bf16[512,256]{1,0:T(8,128)(2,1)S(1)} %collective-permute-done.21.refs_2_, bf16[512,256]{1,0:T(8,128)(2,1)S(1)} %collective-permute-done.25.refs_3_, ...), custom_call_target="tpu_custom_call" | custom-call | bytes 5000000 | tf_op jit(solution)/shard_map/dense/pallas_call | solution.py:323
  72.7 2.5 %last.1 = bf16[128,128,128]{2,1,0:T(8,128)(2,1)} custom-call(s32[128]{0:T(128)S(1)} %get-tuple-element.54.slots_ref, s32[128]{0:T(128)S(1)} %get-tuple-element.53.places_ref, s32[1]{0:T(128)} %bitcast.4.count_ref, bf16[512,1024]{1,0:T(8,128)(2,1)S(1)} %get-tuple-element.44.refs_12_.refs_1_.left_ref, ...), custom_call_target="tpu_custom_call", output_to_operand_aliasing={{}: (7, {})} | custom-call | bytes 3000000 | tf_op jit(solution)/shard_map/last/pallas_call | solution.py:363
  (52 shorter events, 0.6 us)
Async XLA Ops:
  0.6 9.5 %collective-permute-start.1 = (bf16[128,1024]{1,0:T(8,128)(2,1)}, bf16[128,1024]{1,0:T(8,128)(2,1)S(1)}, u32[]{:S(2)}, u32[]{:S(2)}) collective-permute-start(bf16[128,1024]{1,0:T(8,128)(2,1)} %panel_ref.1), channel_id=1, source_target_pairs={{0,2},{1,3},{2,0},{3,1},{4,6},{5,7},{6,4},{7,5},{8,10},{9,11},{10,... | collective-permute-start | bytes 786440 | tf_op jit(solution)/shard_map/ppermute | solution.py:36
  3.6 7.6 %collective-permute-start = (bf16[128,1024]{1,0:T(8,128)(2,1)}, bf16[128,1024]{1,0:T(8,128)(2,1)S(1)}, u32[]{:S(2)}, u32[]{:S(2)}) collective-permute-start(bf16[128,1024]{1,0:T(8,128)(2,1)} %panel_ref.1), channel_id=1, source_target_pairs={{0,1},{1,0},{2,3},{3,2},{4,5},{5,4},{6,7},{7,6},{8,9},{9,8},{10,11... | collective-permute-start | bytes 786440 | tf_op jit(solution)/shard_map/ppermute | solution.py:36
  3.6 1.0 %copy-start = (bf16[128,1024]{1,0:T(8,128)(2,1)S(1)}, bf16[128,1024]{1,0:T(8,128)(2,1)}, u32[]{:S(2)}) copy-start(bf16[128,1024]{1,0:T(8,128)(2,1)} %panel_ref.1) | copy-start | bytes 786436
  4.6 0.7 copy-start.1
  5.3 16.8 %copy-start.4 = (s32[1,1,128]{2,1,0:T(1,128)S(1)}, s32[1,1,128]{2,1,0:T(1,128)}, u32[]{:S(2)}) copy-start(s32[1,1,128]{2,1,0:T(1,128)} %param.20) | copy-start | bytes 1540
  5.3 16.9 %copy-start.5 = (s32[1,1,128]{2,1,0:T(1,128)S(1)}, s32[1,1,128]{2,1,0:T(1,128)}, u32[]{:S(2)}) copy-start(s32[1,1,128]{2,1,0:T(1,128)} %param.21) | copy-start | bytes 1540
  5.3 18.0 %copy-start.3 = (bf16[128,1024]{1,0:T(8,128)(2,1)S(1)}, bf16[128,1024]{1,0:T(8,128)(2,1)}, u32[]{:S(2)}) copy-start(bf16[128,1024]{1,0:T(8,128)(2,1)} %param.12) | copy-start | bytes 786436
  5.3 18.6 %copy-start.2 = (bf16[512,512]{1,0:T(8,128)(2,1)S(1)}, bf16[512,512]{1,0:T(8,128)(2,1)}, u32[]{:S(2)}) copy-start(bf16[512,512]{1,0:T(8,128)(2,1)} %param.14) | copy-start | bytes 1572868
  5.3 18.6 %copy-start.6 = (s32[1,1,128]{2,1,0:T(1,128)S(1)}, s32[1,1,128]{2,1,0:T(1,128)}, u32[]{:S(2)}) copy-start(s32[1,1,128]{2,1,0:T(1,128)} %param.18) | copy-start | bytes 1540
  5.3 18.6 %copy-start.7 = (s32[1,1,128]{2,1,0:T(1,128)S(1)}, s32[1,1,128]{2,1,0:T(1,128)}, u32[]{:S(2)}) copy-start(s32[1,1,128]{2,1,0:T(1,128)} %param.19) | copy-start | bytes 1540
  5.3 18.7 %copy-start.8 = (s32[8]{0:T(128)S(1)}, s32[8]{0:T(128)}, u32[]{:S(2)}) copy-start(s32[8]{0:T(128)} %param.16) | copy-start | bytes 100
  5.9 9.7 %collective-permute-start.3 = (bf16[128,512]{1,0:T(8,128)(2,1)S(1)}, bf16[128,512]{1,0:T(8,128)(2,1)S(1)}, u32[]{:S(2)}, u32[]{:S(2)}) collective-permute-start(bf16[128,512]{1,0:T(8,128)(2,1)S(1)} %bridge_columns.1), channel_id=1, source_target_pairs={{0,16},{4,20},{8,24},{12,28},{16,0},{20,4},{24,8},{28,12},{1,17},{... | collective-permute-start | bytes 393224 | tf_op jit(solution)/shard_map/ppermute | solution.py:36
  10.2 1.5 %collective-permute-start.2 = (bf16[128,1024]{1,0:T(8,128)(2,1)S(1)}, bf16[128,1024]{1,0:T(8,128)(2,1)S(1)}, u32[]{:S(2)}, u32[]{:S(2)}) collective-permute-start(bf16[128,1024]{1,0:T(8,128)(2,1)S(1)} %collective-permute-done.1.refs_3_), channel_id=1, source_target_pairs={{0,1},{1,0},{2,3},{3,2},{4,5},{5,4},{6,7},{7,6},{8,9},{9,8},{10,11... | collective-permute-start | bytes 786440 | tf_op jit(solution)/shard_map/ppermute | solution.py:36
  15.6 6.5 %collective-permute-start.4 = (bf16[128,512]{1,0:T(8,128)(2,1)S(1)}, bf16[128,512]{1,0:T(8,128)(2,1)S(1)}, u32[]{:S(2)}, u32[]{:S(2)}) collective-permute-start(bf16[128,512]{1,0:T(8,128)(2,1)S(1)} %add.151), channel_id=1, source_target_pairs={{0,8},{4,12},{8,0},{12,4},{16,24},{20,28},{24,16},{28,20},{1,9},{5... | collective-permute-start | bytes 393224 | tf_op jit(solution)/shard_map/ppermute | solution.py:36
  16.4 10.0 %collective-permute-start.7 = (bf16[512,256]{1,0:T(8,128)(2,1)S(1)}, bf16[512,256]{1,0:T(8,128)(2,1)S(1)}, u32[]{:S(2)}, u32[]{:S(2)}) collective-permute-start(bf16[512,256]{1,0:T(8,128)(2,1)S(1)} %get-tuple-element.29.refs_3_), channel_id=1, source_target_pairs={{8,0},{16,8},{24,16},{28,24},{20,28},{12,20},{4,12},{0,4},{9,1},{1... | collective-permute-start | bytes 786440 | tf_op jit(solution)/shard_map/ppermute | solution.py:65
  17.9 9.2 %collective-permute-start.6 = (bf16[512,256]{1,0:T(8,128)(2,1)S(1)}, bf16[512,256]{1,0:T(8,128)(2,1)S(1)}, u32[]{:S(2)}, u32[]{:S(2)}) collective-permute-start(bf16[512,256]{1,0:T(8,128)(2,1)S(1)} %get-tuple-element.29.refs_3_), channel_id=1, source_target_pairs={{0,8},{8,16},{16,24},{24,28},{28,20},{20,12},{12,4},{4,0},{1,9},{9... | collective-permute-start | bytes 786440 | tf_op jit(solution)/shard_map/ppermute | solution.py:65
  22.9 5.5 %collective-permute-start.5 = (bf16[128,512]{1,0:T(8,128)(2,1)S(1)}, bf16[128,512]{1,0:T(8,128)(2,1)S(1)}, u32[]{:S(2)}, u32[]{:S(2)}) collective-permute-start(bf16[128,512]{1,0:T(8,128)(2,1)S(1)} %add.152), channel_id=1, source_target_pairs={{0,4},{4,0},{8,12},{12,8},{16,20},{20,16},{24,28},{28,24},{1,5},{5... | collective-permute-start | bytes 393224 | tf_op jit(solution)/shard_map/ppermute | solution.py:36
  23.3 7.0 %collective-permute-start.12 = (bf16[128,1024]{1,0:T(8,128)(2,1)S(1)}, bf16[128,1024]{1,0:T(8,128)(2,1)S(1)}, u32[]{:S(2)}, u32[]{:S(2)}) collective-permute-start(bf16[128,1024]{1,0:T(8,128)(2,1)S(1)} %copy-done.3), channel_id=1, source_target_pairs={{0,2},{1,3},{2,0},{3,1},{4,6},{5,7},{6,4},{7,5},{8,10},{9,11},{10,... | collective-permute-start | bytes 786440 | tf_op jit(solution)/shard_map/ppermute | solution.py:36
  23.9 9.6 %collective-permute-start.11 = (bf16[128,1024]{1,0:T(8,128)(2,1)S(1)}, bf16[128,1024]{1,0:T(8,128)(2,1)S(1)}, u32[]{:S(2)}, u32[]{:S(2)}) collective-permute-start(bf16[128,1024]{1,0:T(8,128)(2,1)S(1)} %copy-done.3), channel_id=1, source_target_pairs={{0,1},{1,0},{2,3},{3,2},{4,5},{5,4},{6,7},{7,6},{8,9},{9,8},{10,11... | collective-permute-start | bytes 786440 | tf_op jit(solution)/shard_map/ppermute | solution.py:36
  26.4 7.6 %collective-permute-start.15 = (bf16[512,256]{1,0:T(8,128)(2,1)S(1)}, bf16[512,256]{1,0:T(8,128)(2,1)S(1)}, u32[]{:S(2)}, u32[]{:S(2)}) collective-permute-start(bf16[512,256]{1,0:T(8,128)(2,1)S(1)} %collective-permute-done.7.refs_5_), channel_id=1, source_target_pairs={{8,0},{16,8},{24,16},{28,24},{20,28},{12,20},{4,12},{0,4},{9,1},{1... | collective-permute-start | bytes 786440 | tf_op jit(solution)/shard_map/ppermute | solution.py:65
  27.1 8.3 %collective-permute-start.14 = (bf16[512,256]{1,0:T(8,128)(2,1)S(1)}, bf16[512,256]{1,0:T(8,128)(2,1)S(1)}, u32[]{:S(2)}, u32[]{:S(2)}) collective-permute-start(bf16[512,256]{1,0:T(8,128)(2,1)S(1)} %collective-permute-done.6.refs_4_), channel_id=1, source_target_pairs={{0,8},{8,16},{16,24},{24,28},{28,20},{20,12},{12,4},{4,0},{1,9},{9... | collective-permute-start | bytes 786440 | tf_op jit(solution)/shard_map/ppermute | solution.py:65
  28.5 5.0 %collective-permute-start.9 = (bf16[128,512]{1,0:T(8,128)(2,1)S(1)}, bf16[128,512]{1,0:T(8,128)(2,1)S(1)}, u32[]{:S(2)}, u32[]{:S(2)}) collective-permute-start(bf16[128,512]{1,0:T(8,128)(2,1)S(1)} %add.167.refs_4_), channel_id=1, source_target_pairs={{0,2},{1,3},{2,0},{3,1},{4,6},{5,7},{6,4},{7,5},{8,10},{9,11},{10,... | collective-permute-start | bytes 393224 | tf_op jit(solution)/shard_map/ppermute | solution.py:36
  30.3 5.8 %collective-permute-start.13 = (bf16[128,1024]{1,0:T(8,128)(2,1)S(1)}, bf16[128,1024]{1,0:T(8,128)(2,1)S(1)}, u32[]{:S(2)}, u32[]{:S(2)}) collective-permute-start(bf16[128,1024]{1,0:T(8,128)(2,1)S(1)} %collective-permute-done.12.refs_10_.refs_6_), channel_id=1, source_target_pairs={{0,1},{1,0},{2,3},{3,2},{4,5},{5,4},{6,7},{7,6},{8,9},{9,8},{10,11... | collective-permute-start | bytes 786440 | tf_op jit(solution)/shard_map/ppermute | solution.py:36
  33.5 2.6 %collective-permute-start.8 = (bf16[128,512]{1,0:T(8,128)(2,1)S(1)}, bf16[128,512]{1,0:T(8,128)(2,1)S(1)}, u32[]{:S(2)}, u32[]{:S(2)}) collective-permute-start(bf16[128,512]{1,0:T(8,128)(2,1)S(1)} %add.167.refs_4_), channel_id=1, source_target_pairs={{0,1},{1,0},{2,3},{3,2},{4,5},{5,4},{6,7},{7,6},{8,9},{9,8},{10,11... | collective-permute-start | bytes 393224 | tf_op jit(solution)/shard_map/ppermute | solution.py:36
  33.5 2.5 %collective-permute-start.10 = (bf16[128,512]{1,0:T(8,128)(2,1)S(1)}, bf16[128,512]{1,0:T(8,128)(2,1)S(1)}, u32[]{:S(2)}, u32[]{:S(2)}) collective-permute-start(bf16[128,512]{1,0:T(8,128)(2,1)S(1)} %collective-permute-done.9.refs_6_), channel_id=1, source_target_pairs={{0,1},{1,0},{2,3},{3,2},{4,5},{5,4},{6,7},{7,6},{8,9},{9,8},{10,11... | collective-permute-start | bytes 393224 | tf_op jit(solution)/shard_map/ppermute | solution.py:36
  34.0 9.2 %collective-permute-start.19 = (bf16[512,256]{1,0:T(8,128)(2,1)S(1)}, bf16[512,256]{1,0:T(8,128)(2,1)S(1)}, u32[]{:S(2)}, u32[]{:S(2)}) collective-permute-start(bf16[512,256]{1,0:T(8,128)(2,1)S(1)} %collective-permute-done.15.refs_7_), channel_id=1, source_target_pairs={{8,0},{16,8},{24,16},{28,24},{20,28},{12,20},{4,12},{0,4},{9,1},{1... | collective-permute-start | bytes 786440 | tf_op jit(solution)/shard_map/ppermute | solution.py:65
  35.4 9.2 %collective-permute-start.17 = (bf16[512,256]{1,0:T(8,128)(2,1)S(1)}, bf16[512,256]{1,0:T(8,128)(2,1)S(1)}, u32[]{:S(2)}, u32[]{:S(2)}) collective-permute-start(bf16[512,256]{1,0:T(8,128)(2,1)S(1)} %collective-permute-done.14.refs_6_), channel_id=1, source_target_pairs={{0,8},{8,16},{16,24},{24,28},{28,20},{20,12},{12,4},{4,0},{1,9},{9... | collective-permute-start | bytes 786440 | tf_op jit(solution)/shard_map/ppermute | solution.py:65
  37.8 14.3 %collective-permute-start.22 = (bf16[512,256]{1,0:T(8,128)(2,1)S(1)}, bf16[512,256]{1,0:T(8,128)(2,1)S(1)}, u32[]{:S(2)}, u32[]{:S(2)}) collective-permute-start(bf16[512,256]{1,0:T(8,128)(2,1)S(1)} %get-tuple-element.46.refs_13_), channel_id=1, source_target_pairs={{8,0},{16,8},{24,16},{28,24},{20,28},{12,20},{4,12},{0,4},{9,1},{1... | collective-permute-start | bytes 786440 | tf_op jit(solution)/shard_map/ppermute | solution.py:65
  39.2 14.0 %collective-permute-start.16 = (bf16[512,256]{1,0:T(8,128)(2,1)S(1)}, bf16[512,256]{1,0:T(8,128)(2,1)S(1)}, u32[]{:S(2)}, u32[]{:S(2)}) collective-permute-start(bf16[512,256]{1,0:T(8,128)(2,1)S(1)} %get-tuple-element.46.refs_13_), channel_id=1, source_target_pairs={{0,8},{8,16},{16,24},{24,28},{28,20},{20,12},{12,4},{4,0},{1,9},{9... | collective-permute-start | bytes 786440 | tf_op jit(solution)/shard_map/ppermute | solution.py:65
  43.2 7.5 %collective-permute-start.20 = (bf16[256,256]{1,0:T(8,128)(2,1)S(1)}, bf16[256,256]{1,0:T(8,128)(2,1)S(1)}, u32[]{:S(2)}, u32[]{:S(2)}) collective-permute-start(bf16[256,256]{1,0:T(8,128)(2,1)S(1)} %slice.17), channel_id=1, source_target_pairs={{8,0},{16,8},{24,16},{28,24},{20,28},{12,20},{4,12},{0,4},{9,1},{1... | collective-permute-start | bytes 393224 | tf_op jit(solution)/shard_map/ppermute | solution.py:65
  44.6 7.6 %collective-permute-start.18 = (bf16[256,256]{1,0:T(8,128)(2,1)S(1)}, bf16[256,256]{1,0:T(8,128)(2,1)S(1)}, u32[]{:S(2)}, u32[]{:S(2)}) collective-permute-start(bf16[256,256]{1,0:T(8,128)(2,1)S(1)} %slice.16), channel_id=1, source_target_pairs={{0,8},{8,16},{16,24},{24,28},{28,20},{20,12},{12,4},{4,0},{1,9},{9... | collective-permute-start | bytes 393224 | tf_op jit(solution)/shard_map/ppermute | solution.py:65
  52.2 7.5 %collective-permute-start.25 = (bf16[512,256]{1,0:T(8,128)(2,1)S(1)}, bf16[512,256]{1,0:T(8,128)(2,1)S(1)}, u32[]{:S(2)}, u32[]{:S(2)}) collective-permute-start(bf16[512,256]{1,0:T(8,128)(2,1)S(1)} %collective-permute-done.22.refs_15_), channel_id=1, source_target_pairs={{8,0},{16,8},{24,16},{28,24},{20,28},{12,20},{4,12},{0,4},{9,1},{1... | collective-permute-start | bytes 786440 | tf_op jit(solution)/shard_map/ppermute | solution.py:65
  53.2 7.4 %collective-permute-start.21 = (bf16[512,256]{1,0:T(8,128)(2,1)S(1)}, bf16[512,256]{1,0:T(8,128)(2,1)S(1)}, u32[]{:S(2)}, u32[]{:S(2)}) collective-permute-start(bf16[512,256]{1,0:T(8,128)(2,1)S(1)} %collective-permute-done.16.refs_14_), channel_id=1, source_target_pairs={{0,8},{8,16},{16,24},{24,28},{28,20},{20,12},{12,4},{4,0},{1,9},{9... | collective-permute-start | bytes 786440 | tf_op jit(solution)/shard_map/ppermute | solution.py:65
  59.7 6.8 %collective-permute-start.26 = (bf16[512,256]{1,0:T(8,128)(2,1)S(1)}, bf16[512,256]{1,0:T(8,128)(2,1)S(1)}, u32[]{:S(2)}, u32[]{:S(2)}) collective-permute-start(bf16[512,256]{1,0:T(8,128)(2,1)S(1)} %collective-permute-done.25.refs_3_), channel_id=1, source_target_pairs={{8,0},{16,8},{24,16},{28,24},{20,28},{12,20},{4,12},{0,4},{9,1},{1... | collective-permute-start | bytes 786440 | tf_op jit(solution)/shard_map/ppermute | solution.py:65
  60.6 6.9 %collective-permute-start.23 = (bf16[512,256]{1,0:T(8,128)(2,1)S(1)}, bf16[512,256]{1,0:T(8,128)(2,1)S(1)}, u32[]{:S(2)}, u32[]{:S(2)}) collective-permute-start(bf16[512,256]{1,0:T(8,128)(2,1)S(1)} %collective-permute-done.21.refs_2_), channel_id=1, source_target_pairs={{0,8},{8,16},{16,24},{24,28},{28,20},{20,12},{12,4},{4,0},{1,9},{9... | collective-permute-start | bytes 786440 | tf_op jit(solution)/shard_map/ppermute | solution.py:65
  66.6 6.2 %collective-permute-start.27 = (bf16[256,256]{1,0:T(8,128)(2,1)S(1)}, bf16[256,256]{1,0:T(8,128)(2,1)S(1)}, u32[]{:S(2)}, u32[]{:S(2)}) collective-permute-start(bf16[256,256]{1,0:T(8,128)(2,1)S(1)} %slice.19), channel_id=1, source_target_pairs={{8,0},{16,8},{24,16},{28,24},{20,28},{12,20},{4,12},{0,4},{9,1},{1... | collective-permute-start | bytes 393224 | tf_op jit(solution)/shard_map/ppermute | solution.py:65
  67.5 5.2 %collective-permute-start.24 = (bf16[256,256]{1,0:T(8,128)(2,1)S(1)}, bf16[256,256]{1,0:T(8,128)(2,1)S(1)}, u32[]{:S(2)}, u32[]{:S(2)}) collective-permute-start(bf16[256,256]{1,0:T(8,128)(2,1)S(1)} %slice.18), channel_id=1, source_target_pairs={{0,8},{8,16},{16,24},{24,28},{28,20},{20,12},{12,4},{4,0},{1,9},{9... | collective-permute-start | bytes 393224 | tf_op jit(solution)/shard_map/ppermute | solution.py:65

commit v5 on v4

--- a/solution.py
+++ b/solution.py
@@ -424,8 +424,9 @@
             ring_one = [tile_one]
             go_on(ring_one)
             other = after(other, tile_one)
+        if at == 1:
+            far_two = far_pieces(after(panel_two, raw))
         if at == 2:
-            far_two = far_pieces(after(panel_two, raw))
             inverse_two_here = staged(after(inverse_two, raw))
             own_two_here = staged(after(panel_two, raw))
             other = after(other, inverse_two_here, own_two_here)
@@ -446,8 +447,9 @@
     pieces_two = [own_two_here] + near_pieces(far_two)[1:]
     far_raw = far_pieces(raw)
     far_raw = {m: after(p, base) for m, p in far_raw.items()}
+    raw = near_pieces(far_raw)
     tile, bridge = tile_two(
-        row_map, inverse_one_here, inverse_two_here, lower_one, near_pieces(far_raw), pieces_two, block
+        row_map, inverse_one_here, inverse_two_here, lower_one, raw, pieces_two, block
     )
     tile = after(tile, *ring_one[3:5])
     ring_two = [tile]

time: 75.5 us -> 75.1 us (level)
  waiting for transfers between devices: 24.7 us -> 22.9 us
  starting transfers between devices: 25 us -> 26.3 us
    ppermute x8, starting transfers between devices: 7.27 us -> 8.6 us  [ring_step(): lax.ppermute(forward, 'row', ahead)]
    ppermute x8, starting transfers between devices: 9.1 us -> 7.86 us  [ring_step(): lax.ppermute(backward, 'row', back)]
    ppermute x12, starting transfers between devices: 8.63 us -> 9.83 us  [xor_permute(): lax.ppermute(value, axis, [(i, i ^ mask) for i in range(lax.axis_size(axi...]
    ppermute x8, waiting for transfers between devices: 1.57 us -> 0.44 us  [ring_step(): lax.ppermute(forward, 'row', ahead)]
    ppermute x8, waiting for transfers between devices: 13.4 us -> 12.3 us  [ring_step(): lax.ppermute(backward, 'row', back)]
where the time goes in v5:
time: 75.1 us; the launch traced here: 74.7 us
  starting transfers between devices  26.3 us (35%)
  waiting for transfers between devices  22.9 us (30%)
  Pallas kernels  18.2 us (24%)
  other arithmetic  4.75 us (6%)
  local copies, waits for them, and re-layouts  1.7 us (2%)
  between operations  0.87 us (1%)
    ppermute x8, waiting for transfers between devices, ring_step(): lax.ppermute(backward, 'row', back)  12.3 us
    ppermute x12, waiting for transfers between devices, xor_permute(): lax.ppermute(value, axis, [(i, i ^ mask) for i in range(lax.axis_size(axi...  10.2 us
    ppermute x12, starting transfers between devices, xor_permute(): lax.ppermute(value, axis, [(i, i ^ mask) for i in range(lax.axis_size(axi...  9.83 us
    pallas_call x2, Pallas kernels, dense(): call(functools.partial(dense_kernel, block, [len(p) for _, _, p in groups...  9.02 us
    ppermute x8, starting transfers between devices, ring_step(): lax.ppermute(forward, 'row', ahead)  8.6 us
    ppermute x8, starting transfers between devices, ring_step(): lax.ppermute(backward, 'row', back)  7.86 us
    mul x5, other arithmetic, staged(): return value * lax.optimization_barrier(jnp.ones((), value.dtype))  3.62 us
    pallas_call x1, Pallas kernels, factor_two(): call(functools.partial(factor_two_kernel, block, count), 'factor_two', 12...  2.75 us
  transfers between devices with their start and end apart: 28, of which 13 were waited for; matrix products, arithmetic and copies ran while one was open for 6% of the time, Pallas kernels for 21%

profile of v5, /device:TPU:0, one launch (start us, length us, event | category | flops | bytes accessed | tf_op | source)
XLA Modules:
  0.0 74.7 jit_solution(9398096426828877758)
XLA Ops:
  0.6 3.0 %collective-permute-start.1 = (bf16[128,1024]{1,0:T(8,128)(2,1)}, bf16[128,1024]{1,0:T(8,128)(2,1)S(1)}, u32[]{:S(2)}, u32[]{:S(2)}) collective-permute-start(bf16[128,1024]{1,0:T(8,128)(2,1)} %panel_ref.1), channel_id=1, source_target_pairs={{0,2},{1,3},{2,0},{3,1},{4,6},{5,7},{6,4},{7,5},{8,10},{9,11},{10,... | collective-permute-start | bytes 786440 | tf_op jit(solution)/shard_map/ppermute | solution.py:36
  3.6 1.0 %copy-done = bf16[128,1024]{1,0:T(8,128)(2,1)S(1)} copy-done((bf16[128,1024]{1,0:T(8,128)(2,1)S(1)}, bf16[128,1024]{1,0:T(8,128)(2,1)}, u32[]{:S(2)}) %copy-start) | copy-done | bytes 262168
  4.6 0.7 copy-done.1
  5.3 0.6 bridge_columns.1
  5.9 2.7 %collective-permute-start.3 = (bf16[128,512]{1,0:T(8,128)(2,1)S(1)}, bf16[128,512]{1,0:T(8,128)(2,1)S(1)}, u32[]{:S(2)}, u32[]{:S(2)}) collective-permute-start(bf16[128,512]{1,0:T(8,128)(2,1)S(1)} %bridge_columns.1), channel_id=1, source_target_pairs={{0,16},{4,20},{8,24},{12,28},{16,0},{20,4},{24,8},{28,12},{1,17},{... | collective-permute-start | bytes 393224 | tf_op jit(solution)/shard_map/ppermute | solution.py:36
  8.6 1.6 %collective-permute-done.1.refs_3_ = bf16[128,1024]{1,0:T(8,128)(2,1)S(1)} collective-permute-done((bf16[128,1024]{1,0:T(8,128)(2,1)}, bf16[128,1024]{1,0:T(8,128)(2,1)S(1)}, u32[]{:S(2)}, u32[]{:S(2)}) %collective-permute-start.1) | collective-permute-done | bytes 262176 | tf_op jit(solution)/shard_map/ppermute | solution.py:36
  10.2 1.1 %broadcast_multiply_fusion.1.refs_0_.refs_1_ = bf16[512,512]{1,0:T(8,128)(2,1)S(1)} fusion(bf16[512,512]{1,0:T(8,128)(2,1)} %param.13, bf16[]{:T(256)} %constant.164.clone.1), kind=kLoop, calls=%fused_computation.2 | loop fusion | flops 262144 | bytes 1048578 | tf_op jit(solution)/shard_map/mul | solution.py:98
  11.3 0.4 collective-permute-done.2.refs_4_
  11.7 1.6 %factor_one.1 = (bf16[512,1024]{1,0:T(8,128)(2,1)S(1)}, bf16[128,1024]{1,0:T(8,128)(2,1)}, bf16[512,256]{1,0:T(8,128)(2,1)S(1)}) custom-call(bf16[512,512]{1,0:T(8,128)(2,1)S(1)} %broadcast_multiply_fusion.1.refs_0_.refs_1_, bf16[128,1024]{1,0:T(8,128)(2,1)S(1)} %broadcast_multiply_fusion.3.refs_1_, bf16[128,1024]{1,0:T(8,128)(2,1)S(1)} %collective-permute-done.refs_2_, ...), custom_call_target="tpu_custom_call" | custom-call | bytes 1600000 | tf_op jit(solution)/shard_map/factor_one/pallas_call | solution.py:165
  13.3 2.3 %collective-permute-done.3 = bf16[128,512]{1,0:T(8,128)(2,1)S(1)} collective-permute-done((bf16[128,512]{1,0:T(8,128)(2,1)S(1)}, bf16[128,512]{1,0:T(8,128)(2,1)S(1)}, u32[]{:S(2)}, u32[]{:S(2)}) %collective-permute-start.3) | collective-permute-done | bytes 131104 | tf_op jit(solution)/shard_map/ppermute | solution.py:36
  15.6 0.8 %collective-permute-start.4 = (bf16[128,512]{1,0:T(8,128)(2,1)S(1)}, bf16[128,512]{1,0:T(8,128)(2,1)S(1)}, u32[]{:S(2)}, u32[]{:S(2)}) collective-permute-start(bf16[128,512]{1,0:T(8,128)(2,1)S(1)} %add.151), channel_id=1, source_target_pairs={{0,8},{4,12},{8,0},{12,4},{16,24},{20,28},{24,16},{28,20},{1,9},{5... | collective-permute-start | bytes 393224 | tf_op jit(solution)/shard_map/ppermute | solution.py:36
  16.4 0.5 collective-permute-start.12
  16.9 1.5 %collective-permute-start.7 = (bf16[512,256]{1,0:T(8,128)(2,1)S(1)}, bf16[512,256]{1,0:T(8,128)(2,1)S(1)}, u32[]{:S(2)}, u32[]{:S(2)}) collective-permute-start(bf16[512,256]{1,0:T(8,128)(2,1)S(1)} %get-tuple-element.30.refs_3_), channel_id=1, source_target_pairs={{8,0},{16,8},{24,16},{28,24},{20,28},{12,20},{4,12},{0,4},{9,1},{1... | collective-permute-start | bytes 786440 | tf_op jit(solution)/shard_map/ppermute | solution.py:65
  18.4 0.5 collective-permute-start.6
  18.9 2.6 %collective-permute-done.4 = bf16[128,512]{1,0:T(8,128)(2,1)S(1)} collective-permute-done((bf16[128,512]{1,0:T(8,128)(2,1)S(1)}, bf16[128,512]{1,0:T(8,128)(2,1)S(1)}, u32[]{:S(2)}, u32[]{:S(2)}) %collective-permute-start.4) | collective-permute-done | bytes 131104 | tf_op jit(solution)/shard_map/ppermute | solution.py:36
  21.6 0.7 %convert_reduce_fusion.1 = (s32[]{:T(128)}, s32[128]{0:T(128)S(1)}) fusion(s32[1,1,128]{2,1,0:T(1,128)S(1)} %copy-done.4, s32[1,1,128]{2,1,0:T(1,128)S(1)} %copy-done.5, s32[]{:T(128)S(6)} %select_n.174), kind=kLoop, calls=%fused_computation.74 | loop fusion | flops 11903 | bytes 1544 | tf_op jit(solution)/shard_map/reduce_sum | solution.py:89
  22.4 0.8 %collective-permute-start.5 = (bf16[128,512]{1,0:T(8,128)(2,1)S(1)}, bf16[128,512]{1,0:T(8,128)(2,1)S(1)}, u32[]{:S(2)}, u32[]{:S(2)}) collective-permute-start(bf16[128,512]{1,0:T(8,128)(2,1)S(1)} %add.152), channel_id=1, source_target_pairs={{0,4},{4,0},{8,12},{12,8},{16,20},{20,16},{24,28},{28,24},{1,5},{5... | collective-permute-start | bytes 393224 | tf_op jit(solution)/shard_map/ppermute | solution.py:36
  23.6 1.0 %collective-permute-done.12.refs_10_.refs_6_ = bf16[128,1024]{1,0:T(8,128)(2,1)S(1)} collective-permute-done((bf16[128,1024]{1,0:T(8,128)(2,1)}, bf16[128,1024]{1,0:T(8,128)(2,1)S(1)}, u32[]{:S(2)}, u32[]{:S(2)}) %collective-permute-start.12) | collective-permute-done | bytes 262176 | tf_op jit(solution)/shard_map/ppermute | solution.py:36
  24.6 1.8 %collective-permute-done.7.refs_5_ = bf16[512,256]{1,0:T(8,128)(2,1)S(1)} collective-permute-done((bf16[512,256]{1,0:T(8,128)(2,1)S(1)}, bf16[512,256]{1,0:T(8,128)(2,1)S(1)}, u32[]{:S(2)}, u32[]{:S(2)}) %collective-permute-start.7) | collective-permute-done | bytes 262176 | tf_op jit(solution)/shard_map/ppermute | solution.py:65
  26.4 1.1 %collective-permute-start.15 = (bf16[512,256]{1,0:T(8,128)(2,1)S(1)}, bf16[512,256]{1,0:T(8,128)(2,1)S(1)}, u32[]{:S(2)}, u32[]{:S(2)}) collective-permute-start(bf16[512,256]{1,0:T(8,128)(2,1)S(1)} %collective-permute-done.7.refs_5_), channel_id=1, source_target_pairs={{8,0},{16,8},{24,16},{28,24},{20,28},{12,20},{4,12},{0,4},{9,1},{1... | collective-permute-start | bytes 786440 | tf_op jit(solution)/shard_map/ppermute | solution.py:65
  27.6 0.8 %collective-permute-start.14 = (bf16[512,256]{1,0:T(8,128)(2,1)S(1)}, bf16[512,256]{1,0:T(8,128)(2,1)S(1)}, u32[]{:S(2)}, u32[]{:S(2)}) collective-permute-start(bf16[512,256]{1,0:T(8,128)(2,1)S(1)} %collective-permute-done.6.refs_4_), channel_id=1, source_target_pairs={{0,8},{8,16},{16,24},{24,28},{28,20},{20,12},{12,4},{4,0},{1,9},{9... | collective-permute-start | bytes 786440 | tf_op jit(solution)/shard_map/ppermute | solution.py:65
  28.4 1.3 %collective-permute-done.5 = bf16[128,512]{1,0:T(8,128)(2,1)S(1)} collective-permute-done((bf16[128,512]{1,0:T(8,128)(2,1)S(1)}, bf16[128,512]{1,0:T(8,128)(2,1)S(1)}, u32[]{:S(2)}, u32[]{:S(2)}) %collective-permute-start.5) | collective-permute-done | bytes 131104 | tf_op jit(solution)/shard_map/ppermute | solution.py:36
  29.7 1.6 %collective-permute-start.9 = (bf16[128,512]{1,0:T(8,128)(2,1)S(1)}, bf16[128,512]{1,0:T(8,128)(2,1)S(1)}, u32[]{:S(2)}, u32[]{:S(2)}) collective-permute-start(bf16[128,512]{1,0:T(8,128)(2,1)S(1)} %add.167.refs_4_), channel_id=1, source_target_pairs={{0,2},{1,3},{2,0},{3,1},{4,6},{5,7},{6,4},{7,5},{8,10},{9,11},{10,... | collective-permute-start | bytes 393224 | tf_op jit(solution)/shard_map/ppermute | solution.py:36
  31.3 2.5 %multiply_bitcast_fusion.refs_16_ = bf16[128,128,128]{2,1,0:T(8,128)(2,1)S(1)} fusion(bf16[1,1,128,128,128]{4,3,2,1,0:T(8,128)(2,1)} %param.17, bf16[]{:T(256)} %constant.164.clone.1), kind=kLoop, calls=%fused_computation | loop fusion | flops 2097152 | bytes 8388610 | tf_op jit(solution)/shard_map/mul | solution.py:98
  33.7 1.0 %collective-permute-done.9.refs_6_ = bf16[128,512]{1,0:T(8,128)(2,1)S(1)} collective-permute-done((bf16[128,512]{1,0:T(8,128)(2,1)S(1)}, bf16[128,512]{1,0:T(8,128)(2,1)S(1)}, u32[]{:S(2)}, u32[]{:S(2)}) %collective-permute-start.9) | collective-permute-done | bytes 131104 | tf_op jit(solution)/shard_map/ppermute | solution.py:36
  34.8 0.5 collective-permute-start.10
  35.3 0.7 collective-permute-start.19
  35.9 1.4 %collective-permute-start.17 = (bf16[512,256]{1,0:T(8,128)(2,1)S(1)}, bf16[512,256]{1,0:T(8,128)(2,1)S(1)}, u32[]{:S(2)}, u32[]{:S(2)}) collective-permute-start(bf16[512,256]{1,0:T(8,128)(2,1)S(1)} %collective-permute-done.14.refs_6_), channel_id=1, source_target_pairs={{0,8},{8,16},{16,24},{24,28},{28,20},{20,12},{12,4},{4,0},{1,9},{9... | collective-permute-start | bytes 786440 | tf_op jit(solution)/shard_map/ppermute | solution.py:65
  37.3 1.8 %tile_two.1 = (bf16[512,256]{1,0:T(8,128)(2,1)S(1)}, bf16[512,512]{1,0:T(8,128)(2,1)S(1)}) custom-call(s32[8]{0:T(128)S(1)} %and_select_fusion.16.refs_0_, bf16[512,512]{1,0:T(8,128)(2,1)S(1)} %broadcast_multiply_fusion.1.refs_0_.refs_1_, bf16[512,512]{1,0:T(8,128)(2,1)S(1)} %broadcast_multiply_fusion.refs_2_.refs_1_, ...), custom_call_target="tpu_custom_call" | custom-call | bytes 1600000 | tf_op jit(solution)/shard_map/tile_two/pallas_call | solution.py:204
  39.1 0.7 collective-permute-start.22
  39.8 1.4 %collective-permute-start.16 = (bf16[512,256]{1,0:T(8,128)(2,1)S(1)}, bf16[512,256]{1,0:T(8,128)(2,1)S(1)}, u32[]{:S(2)}, u32[]{:S(2)}) collective-permute-start(bf16[512,256]{1,0:T(8,128)(2,1)S(1)} %get-tuple-element.48.refs_13_), channel_id=1, source_target_pairs={{0,8},{8,16},{16,24},{24,28},{28,20},{20,12},{12,4},{4,0},{1,9},{9... | collective-permute-start | bytes 786440 | tf_op jit(solution)/shard_map/ppermute | solution.py:65
  41.2 3.3 %collective-permute-done.19.refs_9_ = bf16[512,256]{1,0:T(8,128)(2,1)S(1)} collective-permute-done((bf16[512,256]{1,0:T(8,128)(2,1)S(1)}, bf16[512,256]{1,0:T(8,128)(2,1)S(1)}, u32[]{:S(2)}, u32[]{:S(2)}) %collective-permute-start.19) | collective-permute-done | bytes 262176 | tf_op jit(solution)/shard_map/ppermute | solution.py:65
  44.5 0.7 collective-permute-start.20
  45.2 1.4 %collective-permute-start.18 = (bf16[256,256]{1,0:T(8,128)(2,1)S(1)}, bf16[256,256]{1,0:T(8,128)(2,1)S(1)}, u32[]{:S(2)}, u32[]{:S(2)}) collective-permute-start(bf16[256,256]{1,0:T(8,128)(2,1)S(1)} %slice.16), channel_id=1, source_target_pairs={{0,8},{8,16},{16,24},{24,28},{28,20},{20,12},{12,4},{4,0},{1,9},{9... | collective-permute-start | bytes 393224 | tf_op jit(solution)/shard_map/ppermute | solution.py:65
  46.6 2.7 %factor_two.1 = (bf16[512,1024]{1,0:T(8,128)(2,1)S(1)}, bf16[128,1024]{1,0:T(8,128)(2,1)}) custom-call(s32[8]{0:T(128)S(1)} %and_select_fusion.16.refs_0_, bf16[512,512]{1,0:T(8,128)(2,1)S(1)} %broadcast_multiply_fusion.refs_2_.refs_1_, bf16[512,1024]{1,0:T(8,128)(2,1)S(1)} %get-tuple-element.34.refs_3_.refs_2_, ...), custom_call_target="tpu_custom_call" | custom-call | bytes 2400000 | tf_op jit(solution)/shard_map/factor_two/pallas_call | solution.py:244
  49.3 0.7 collective-permute-done.22.refs_15_
  50.1 1.9 %collective-permute-done.20.refs_11_ = bf16[256,256]{1,0:T(8,128)(2,1)S(1)} collective-permute-done((bf16[256,256]{1,0:T(8,128)(2,1)S(1)}, bf16[256,256]{1,0:T(8,128)(2,1)S(1)}, u32[]{:S(2)}, u32[]{:S(2)}) %collective-permute-start.20) | collective-permute-done | bytes 131104 | tf_op jit(solution)/shard_map/ppermute | solution.py:65
  52.0 0.4 collective-permute-done.18.refs_10_
  52.4 1.0 %collective-permute-start.25 = (bf16[512,256]{1,0:T(8,128)(2,1)S(1)}, bf16[512,256]{1,0:T(8,128)(2,1)S(1)}, u32[]{:S(2)}, u32[]{:S(2)}) collective-permute-start(bf16[512,256]{1,0:T(8,128)(2,1)S(1)} %collective-permute-done.22.refs_15_), channel_id=1, source_target_pairs={{8,0},{16,8},{24,16},{28,24},{20,28},{12,20},{4,12},{0,4},{9,1},{1... | collective-permute-start | bytes 786440 | tf_op jit(solution)/shard_map/ppermute | solution.py:65
  53.4 1.0 %collective-permute-start.21 = (bf16[512,256]{1,0:T(8,128)(2,1)S(1)}, bf16[512,256]{1,0:T(8,128)(2,1)S(1)}, u32[]{:S(2)}, u32[]{:S(2)}) collective-permute-start(bf16[512,256]{1,0:T(8,128)(2,1)S(1)} %collective-permute-done.16.refs_14_), channel_id=1, source_target_pairs={{0,8},{8,16},{16,24},{24,28},{28,20},{20,12},{12,4},{4,0},{1,9},{9... | collective-permute-start | bytes 786440 | tf_op jit(solution)/shard_map/ppermute | solution.py:65
  54.4 5.0 %dense.2.refs_6_.refs_2_ = bf16[128,128,128]{2,1,0:T(8,128)(2,1)S(1)} custom-call(s32[128]{0:T(128)S(1)} %fusion.2.refs_0_, s32[128]{0:T(128)S(1)} %get-tuple-element.61.refs_1_, bf16[512,1024]{1,0:T(8,128)(2,1)S(1)} %get-tuple-element.34.refs_3_.refs_2_, bf16[512,256]{1,0:T(8,128)(2,1)S(1)} %get-tuple-element.30.refs_3_, ...), custom_call_target="tpu_custom_call" | custom-call | bytes 5000000 | tf_op jit(solution)/shard_map/dense/pallas_call | solution.py:323
  59.5 1.0 %collective-permute-start.26 = (bf16[512,256]{1,0:T(8,128)(2,1)S(1)}, bf16[512,256]{1,0:T(8,128)(2,1)S(1)}, u32[]{:S(2)}, u32[]{:S(2)}) collective-permute-start(bf16[512,256]{1,0:T(8,128)(2,1)S(1)} %collective-permute-done.25.refs_3_), channel_id=1, source_target_pairs={{8,0},{16,8},{24,16},{28,24},{20,28},{12,20},{4,12},{0,4},{9,1},{1... | collective-permute-start | bytes 786440 | tf_op jit(solution)/shard_map/ppermute | solution.py:65
  60.5 1.0 %collective-permute-start.23 = (bf16[512,256]{1,0:T(8,128)(2,1)S(1)}, bf16[512,256]{1,0:T(8,128)(2,1)S(1)}, u32[]{:S(2)}, u32[]{:S(2)}) collective-permute-start(bf16[512,256]{1,0:T(8,128)(2,1)S(1)} %collective-permute-done.21.refs_2_), channel_id=1, source_target_pairs={{0,8},{8,16},{16,24},{24,28},{28,20},{20,12},{12,4},{4,0},{1,9},{9... | collective-permute-start | bytes 786440 | tf_op jit(solution)/shard_map/ppermute | solution.py:65
  61.5 4.5 %collective-permute-done.26.refs_5_ = bf16[512,256]{1,0:T(8,128)(2,1)S(1)} collective-permute-done((bf16[512,256]{1,0:T(8,128)(2,1)S(1)}, bf16[512,256]{1,0:T(8,128)(2,1)S(1)}, u32[]{:S(2)}, u32[]{:S(2)}) %collective-permute-start.26) | collective-permute-done | bytes 262176 | tf_op jit(solution)/shard_map/ppermute | solution.py:65
  66.0 1.0 %collective-permute-start.27 = (bf16[256,256]{1,0:T(8,128)(2,1)S(1)}, bf16[256,256]{1,0:T(8,128)(2,1)S(1)}, u32[]{:S(2)}, u32[]{:S(2)}) collective-permute-start(bf16[256,256]{1,0:T(8,128)(2,1)S(1)} %slice.19), channel_id=1, source_target_pairs={{8,0},{16,8},{24,16},{28,24},{20,28},{12,20},{4,12},{0,4},{9,1},{1... | collective-permute-start | bytes 393224 | tf_op jit(solution)/shard_map/ppermute | solution.py:65
  67.1 1.1 %collective-permute-start.24 = (bf16[256,256]{1,0:T(8,128)(2,1)S(1)}, bf16[256,256]{1,0:T(8,128)(2,1)S(1)}, u32[]{:S(2)}, u32[]{:S(2)}) collective-permute-start(bf16[256,256]{1,0:T(8,128)(2,1)S(1)} %slice.18), channel_id=1, source_target_pairs={{0,8},{8,16},{16,24},{24,28},{28,20},{20,12},{12,4},{4,0},{1,9},{9... | collective-permute-start | bytes 393224 | tf_op jit(solution)/shard_map/ppermute | solution.py:65
  68.2 4.0 %dense.3.refs_3_ = bf16[128,128,128]{2,1,0:T(8,128)(2,1)} custom-call(s32[128]{0:T(128)S(1)} %get-tuple-element.60.refs_0_, bf16[512,1024]{1,0:T(8,128)(2,1)S(1)} %get-tuple-element.46.refs_12_.refs_1_.left_ref, bf16[512,256]{1,0:T(8,128)(2,1)S(1)} %collective-permute-done.21.refs_2_, bf16[512,256]{1,0:T(8,128)(2,1)S(1)} %collective-permute-done.25.refs_3_, ...), custom_call_target="tpu_custom_call" | custom-call | bytes 5000000 | tf_op jit(solution)/shard_map/dense/pallas_call | solution.py:323
  72.2 2.5 %last.1 = bf16[128,128,128]{2,1,0:T(8,128)(2,1)} custom-call(s32[128]{0:T(128)S(1)} %get-tuple-element.56.slots_ref, s32[128]{0:T(128)S(1)} %get-tuple-element.55.places_ref, s32[1]{0:T(128)} %bitcast.4.count_ref, bf16[512,1024]{1,0:T(8,128)(2,1)S(1)} %get-tuple-element.46.refs_12_.refs_1_.left_ref, ...), custom_call_target="tpu_custom_call", output_to_operand_aliasing={{}: (7, {})} | custom-call | bytes 3000000 | tf_op jit(solution)/shard_map/last/pallas_call | solution.py:363
  (52 shorter events, 0.7 us)
Async XLA Ops:
  0.6 9.5 %collective-permute-start.1 = (bf16[128,1024]{1,0:T(8,128)(2,1)}, bf16[128,1024]{1,0:T(8,128)(2,1)S(1)}, u32[]{:S(2)}, u32[]{:S(2)}) collective-permute-start(bf16[128,1024]{1,0:T(8,128)(2,1)} %panel_ref.1), channel_id=1, source_target_pairs={{0,2},{1,3},{2,0},{3,1},{4,6},{5,7},{6,4},{7,5},{8,10},{9,11},{10,... | collective-permute-start | bytes 786440 | tf_op jit(solution)/shard_map/ppermute | solution.py:36
  3.6 7.6 %collective-permute-start = (bf16[128,1024]{1,0:T(8,128)(2,1)}, bf16[128,1024]{1,0:T(8,128)(2,1)S(1)}, u32[]{:S(2)}, u32[]{:S(2)}) collective-permute-start(bf16[128,1024]{1,0:T(8,128)(2,1)} %panel_ref.1), channel_id=1, source_target_pairs={{0,1},{1,0},{2,3},{3,2},{4,5},{5,4},{6,7},{7,6},{8,9},{9,8},{10,11... | collective-permute-start | bytes 786440 | tf_op jit(solution)/shard_map/ppermute | solution.py:36
  3.6 1.0 %copy-start = (bf16[128,1024]{1,0:T(8,128)(2,1)S(1)}, bf16[128,1024]{1,0:T(8,128)(2,1)}, u32[]{:S(2)}) copy-start(bf16[128,1024]{1,0:T(8,128)(2,1)} %panel_ref.1) | copy-start | bytes 786436
  4.6 0.7 copy-start.1
  5.3 16.3 %copy-start.4 = (s32[1,1,128]{2,1,0:T(1,128)S(1)}, s32[1,1,128]{2,1,0:T(1,128)}, u32[]{:S(2)}) copy-start(s32[1,1,128]{2,1,0:T(1,128)} %param.20) | copy-start | bytes 1540
  5.3 16.3 %copy-start.5 = (s32[1,1,128]{2,1,0:T(1,128)S(1)}, s32[1,1,128]{2,1,0:T(1,128)}, u32[]{:S(2)}) copy-start(s32[1,1,128]{2,1,0:T(1,128)} %param.21) | copy-start | bytes 1540
  5.3 17.9 %copy-start.3 = (bf16[128,1024]{1,0:T(8,128)(2,1)S(1)}, bf16[128,1024]{1,0:T(8,128)(2,1)}, u32[]{:S(2)}) copy-start(bf16[128,1024]{1,0:T(8,128)(2,1)} %param.12) | copy-start | bytes 786436
  5.3 17.9 %copy-start.2 = (bf16[512,512]{1,0:T(8,128)(2,1)S(1)}, bf16[512,512]{1,0:T(8,128)(2,1)}, u32[]{:S(2)}) copy-start(bf16[512,512]{1,0:T(8,128)(2,1)} %param.14) | copy-start | bytes 1572868
  5.3 18.0 %copy-start.6 = (s32[1,1,128]{2,1,0:T(1,128)S(1)}, s32[1,1,128]{2,1,0:T(1,128)}, u32[]{:S(2)}) copy-start(s32[1,1,128]{2,1,0:T(1,128)} %param.18) | copy-start | bytes 1540
  5.3 18.0 %copy-start.7 = (s32[1,1,128]{2,1,0:T(1,128)S(1)}, s32[1,1,128]{2,1,0:T(1,128)}, u32[]{:S(2)}) copy-start(s32[1,1,128]{2,1,0:T(1,128)} %param.19) | copy-start | bytes 1540
  5.3 18.0 %copy-start.8 = (s32[8]{0:T(128)S(1)}, s32[8]{0:T(128)}, u32[]{:S(2)}) copy-start(s32[8]{0:T(128)} %param.16) | copy-start | bytes 100
  5.9 9.7 %collective-permute-start.3 = (bf16[128,512]{1,0:T(8,128)(2,1)S(1)}, bf16[128,512]{1,0:T(8,128)(2,1)S(1)}, u32[]{:S(2)}, u32[]{:S(2)}) collective-permute-start(bf16[128,512]{1,0:T(8,128)(2,1)S(1)} %bridge_columns.1), channel_id=1, source_target_pairs={{0,16},{4,20},{8,24},{12,28},{16,0},{20,4},{24,8},{28,12},{1,17},{... | collective-permute-start | bytes 393224 | tf_op jit(solution)/shard_map/ppermute | solution.py:36
  10.2 1.5 %collective-permute-start.2 = (bf16[128,1024]{1,0:T(8,128)(2,1)S(1)}, bf16[128,1024]{1,0:T(8,128)(2,1)S(1)}, u32[]{:S(2)}, u32[]{:S(2)}) collective-permute-start(bf16[128,1024]{1,0:T(8,128)(2,1)S(1)} %collective-permute-done.1.refs_3_), channel_id=1, source_target_pairs={{0,1},{1,0},{2,3},{3,2},{4,5},{5,4},{6,7},{7,6},{8,9},{9,8},{10,11... | collective-permute-start | bytes 786440 | tf_op jit(solution)/shard_map/ppermute | solution.py:36
  15.6 6.0 %collective-permute-start.4 = (bf16[128,512]{1,0:T(8,128)(2,1)S(1)}, bf16[128,512]{1,0:T(8,128)(2,1)S(1)}, u32[]{:S(2)}, u32[]{:S(2)}) collective-permute-start(bf16[128,512]{1,0:T(8,128)(2,1)S(1)} %add.151), channel_id=1, source_target_pairs={{0,8},{4,12},{8,0},{12,4},{16,24},{20,28},{24,16},{28,20},{1,9},{5... | collective-permute-start | bytes 393224 | tf_op jit(solution)/shard_map/ppermute | solution.py:36
  16.4 8.2 %collective-permute-start.12 = (bf16[128,1024]{1,0:T(8,128)(2,1)}, bf16[128,1024]{1,0:T(8,128)(2,1)S(1)}, u32[]{:S(2)}, u32[]{:S(2)}) collective-permute-start(bf16[128,1024]{1,0:T(8,128)(2,1)} %param.12), channel_id=1, source_target_pairs={{0,2},{1,3},{2,0},{3,1},{4,6},{5,7},{6,4},{7,5},{8,10},{9,11},{10,... | collective-permute-start | bytes 786440 | tf_op jit(solution)/shard_map/ppermute | solution.py:36
  16.9 17.9 %collective-permute-start.11 = (bf16[128,1024]{1,0:T(8,128)(2,1)}, bf16[128,1024]{1,0:T(8,128)(2,1)S(1)}, u32[]{:S(2)}, u32[]{:S(2)}) collective-permute-start(bf16[128,1024]{1,0:T(8,128)(2,1)} %param.12), channel_id=1, source_target_pairs={{0,1},{1,0},{2,3},{3,2},{4,5},{5,4},{6,7},{7,6},{8,9},{9,8},{10,11... | collective-permute-start | bytes 786440 | tf_op jit(solution)/shard_map/ppermute | solution.py:36
  16.9 9.5 %collective-permute-start.7 = (bf16[512,256]{1,0:T(8,128)(2,1)S(1)}, bf16[512,256]{1,0:T(8,128)(2,1)S(1)}, u32[]{:S(2)}, u32[]{:S(2)}) collective-permute-start(bf16[512,256]{1,0:T(8,128)(2,1)S(1)} %get-tuple-element.30.refs_3_), channel_id=1, source_target_pairs={{8,0},{16,8},{24,16},{28,24},{20,28},{12,20},{4,12},{0,4},{9,1},{1... | collective-permute-start | bytes 786440 | tf_op jit(solution)/shard_map/ppermute | solution.py:65
  18.4 9.1 %collective-permute-start.6 = (bf16[512,256]{1,0:T(8,128)(2,1)S(1)}, bf16[512,256]{1,0:T(8,128)(2,1)S(1)}, u32[]{:S(2)}, u32[]{:S(2)}) collective-permute-start(bf16[512,256]{1,0:T(8,128)(2,1)S(1)} %get-tuple-element.30.refs_3_), channel_id=1, source_target_pairs={{0,8},{8,16},{16,24},{24,28},{28,20},{20,12},{12,4},{4,0},{1,9},{9... | collective-permute-start | bytes 786440 | tf_op jit(solution)/shard_map/ppermute | solution.py:65
  22.4 7.3 %collective-permute-start.5 = (bf16[128,512]{1,0:T(8,128)(2,1)S(1)}, bf16[128,512]{1,0:T(8,128)(2,1)S(1)}, u32[]{:S(2)}, u32[]{:S(2)}) collective-permute-start(bf16[128,512]{1,0:T(8,128)(2,1)S(1)} %add.152), channel_id=1, source_target_pairs={{0,4},{4,0},{8,12},{12,8},{16,20},{20,16},{24,28},{28,24},{1,5},{5... | collective-permute-start | bytes 393224 | tf_op jit(solution)/shard_map/ppermute | solution.py:36
  24.6 12.7 %collective-permute-start.13 = (bf16[128,1024]{1,0:T(8,128)(2,1)S(1)}, bf16[128,1024]{1,0:T(8,128)(2,1)S(1)}, u32[]{:S(2)}, u32[]{:S(2)}) collective-permute-start(bf16[128,1024]{1,0:T(8,128)(2,1)S(1)} %collective-permute-done.12.refs_10_.refs_6_), channel_id=1, source_target_pairs={{0,1},{1,0},{2,3},{3,2},{4,5},{5,4},{6,7},{7,6},{8,9},{9,8},{10,11... | collective-permute-start | bytes 786440 | tf_op jit(solution)/shard_map/ppermute | solution.py:36
  26.4 8.9 %collective-permute-start.15 = (bf16[512,256]{1,0:T(8,128)(2,1)S(1)}, bf16[512,256]{1,0:T(8,128)(2,1)S(1)}, u32[]{:S(2)}, u32[]{:S(2)}) collective-permute-start(bf16[512,256]{1,0:T(8,128)(2,1)S(1)} %collective-permute-done.7.refs_5_), channel_id=1, source_target_pairs={{8,0},{16,8},{24,16},{28,24},{20,28},{12,20},{4,12},{0,4},{9,1},{1... | collective-permute-start | bytes 786440 | tf_op jit(solution)/shard_map/ppermute | solution.py:65
  27.6 8.4 %collective-permute-start.14 = (bf16[512,256]{1,0:T(8,128)(2,1)S(1)}, bf16[512,256]{1,0:T(8,128)(2,1)S(1)}, u32[]{:S(2)}, u32[]{:S(2)}) collective-permute-start(bf16[512,256]{1,0:T(8,128)(2,1)S(1)} %collective-permute-done.6.refs_4_), channel_id=1, source_target_pairs={{0,8},{8,16},{16,24},{24,28},{28,20},{20,12},{12,4},{4,0},{1,9},{9... | collective-permute-start | bytes 786440 | tf_op jit(solution)/shard_map/ppermute | solution.py:65
  29.7 5.0 %collective-permute-start.9 = (bf16[128,512]{1,0:T(8,128)(2,1)S(1)}, bf16[128,512]{1,0:T(8,128)(2,1)S(1)}, u32[]{:S(2)}, u32[]{:S(2)}) collective-permute-start(bf16[128,512]{1,0:T(8,128)(2,1)S(1)} %add.167.refs_4_), channel_id=1, source_target_pairs={{0,2},{1,3},{2,0},{3,1},{4,6},{5,7},{6,4},{7,5},{8,10},{9,11},{10,... | collective-permute-start | bytes 393224 | tf_op jit(solution)/shard_map/ppermute | solution.py:36
  34.8 2.6 %collective-permute-start.8 = (bf16[128,512]{1,0:T(8,128)(2,1)S(1)}, bf16[128,512]{1,0:T(8,128)(2,1)S(1)}, u32[]{:S(2)}, u32[]{:S(2)}) collective-permute-start(bf16[128,512]{1,0:T(8,128)(2,1)S(1)} %add.167.refs_4_), channel_id=1, source_target_pairs={{0,1},{1,0},{2,3},{3,2},{4,5},{5,4},{6,7},{7,6},{8,9},{9,8},{10,11... | collective-permute-start | bytes 393224 | tf_op jit(solution)/shard_map/ppermute | solution.py:36
  34.8 2.6 %collective-permute-start.10 = (bf16[128,512]{1,0:T(8,128)(2,1)S(1)}, bf16[128,512]{1,0:T(8,128)(2,1)S(1)}, u32[]{:S(2)}, u32[]{:S(2)}) collective-permute-start(bf16[128,512]{1,0:T(8,128)(2,1)S(1)} %collective-permute-done.9.refs_6_), channel_id=1, source_target_pairs={{0,1},{1,0},{2,3},{3,2},{4,5},{5,4},{6,7},{7,6},{8,9},{9,8},{10,11... | collective-permute-start | bytes 393224 | tf_op jit(solution)/shard_map/ppermute | solution.py:36
  35.3 9.2 %collective-permute-start.19 = (bf16[512,256]{1,0:T(8,128)(2,1)S(1)}, bf16[512,256]{1,0:T(8,128)(2,1)S(1)}, u32[]{:S(2)}, u32[]{:S(2)}) collective-permute-start(bf16[512,256]{1,0:T(8,128)(2,1)S(1)} %collective-permute-done.15.refs_7_), channel_id=1, source_target_pairs={{8,0},{16,8},{24,16},{28,24},{20,28},{12,20},{4,12},{0,4},{9,1},{1... | collective-permute-start | bytes 786440 | tf_op jit(solution)/shard_map/ppermute | solution.py:65
  35.9 9.2 %collective-permute-start.17 = (bf16[512,256]{1,0:T(8,128)(2,1)S(1)}, bf16[512,256]{1,0:T(8,128)(2,1)S(1)}, u32[]{:S(2)}, u32[]{:S(2)}) collective-permute-start(bf16[512,256]{1,0:T(8,128)(2,1)S(1)} %collective-permute-done.14.refs_6_), channel_id=1, source_target_pairs={{0,8},{8,16},{16,24},{24,28},{28,20},{20,12},{12,4},{4,0},{1,9},{9... | collective-permute-start | bytes 786440 | tf_op jit(solution)/shard_map/ppermute | solution.py:65
  39.1 11.0 %collective-permute-start.22 = (bf16[512,256]{1,0:T(8,128)(2,1)S(1)}, bf16[512,256]{1,0:T(8,128)(2,1)S(1)}, u32[]{:S(2)}, u32[]{:S(2)}) collective-permute-start(bf16[512,256]{1,0:T(8,128)(2,1)S(1)} %get-tuple-element.48.refs_13_), channel_id=1, source_target_pairs={{8,0},{16,8},{24,16},{28,24},{20,28},{12,20},{4,12},{0,4},{9,1},{1... | collective-permute-start | bytes 786440 | tf_op jit(solution)/shard_map/ppermute | solution.py:65
  39.8 13.6 %collective-permute-start.16 = (bf16[512,256]{1,0:T(8,128)(2,1)S(1)}, bf16[512,256]{1,0:T(8,128)(2,1)S(1)}, u32[]{:S(2)}, u32[]{:S(2)}) collective-permute-start(bf16[512,256]{1,0:T(8,128)(2,1)S(1)} %get-tuple-element.48.refs_13_), channel_id=1, source_target_pairs={{0,8},{8,16},{16,24},{24,28},{28,20},{20,12},{12,4},{4,0},{1,9},{9... | collective-permute-start | bytes 786440 | tf_op jit(solution)/shard_map/ppermute | solution.py:65
  44.5 7.5 %collective-permute-start.20 = (bf16[256,256]{1,0:T(8,128)(2,1)S(1)}, bf16[256,256]{1,0:T(8,128)(2,1)S(1)}, u32[]{:S(2)}, u32[]{:S(2)}) collective-permute-start(bf16[256,256]{1,0:T(8,128)(2,1)S(1)} %slice.17), channel_id=1, source_target_pairs={{8,0},{16,8},{24,16},{28,24},{20,28},{12,20},{4,12},{0,4},{9,1},{1... | collective-permute-start | bytes 393224 | tf_op jit(solution)/shard_map/ppermute | solution.py:65
  45.2 7.2 %collective-permute-start.18 = (bf16[256,256]{1,0:T(8,128)(2,1)S(1)}, bf16[256,256]{1,0:T(8,128)(2,1)S(1)}, u32[]{:S(2)}, u32[]{:S(2)}) collective-permute-start(bf16[256,256]{1,0:T(8,128)(2,1)S(1)} %slice.16), channel_id=1, source_target_pairs={{0,8},{8,16},{16,24},{24,28},{28,20},{20,12},{12,4},{4,0},{1,9},{9... | collective-permute-start | bytes 393224 | tf_op jit(solution)/shard_map/ppermute | solution.py:65
  52.4 7.1 %collective-permute-start.25 = (bf16[512,256]{1,0:T(8,128)(2,1)S(1)}, bf16[512,256]{1,0:T(8,128)(2,1)S(1)}, u32[]{:S(2)}, u32[]{:S(2)}) collective-permute-start(bf16[512,256]{1,0:T(8,128)(2,1)S(1)} %collective-permute-done.22.refs_15_), channel_id=1, source_target_pairs={{8,0},{16,8},{24,16},{28,24},{20,28},{12,20},{4,12},{0,4},{9,1},{1... | collective-permute-start | bytes 786440 | tf_op jit(solution)/shard_map/ppermute | solution.py:65
  53.4 7.1 %collective-permute-start.21 = (bf16[512,256]{1,0:T(8,128)(2,1)S(1)}, bf16[512,256]{1,0:T(8,128)(2,1)S(1)}, u32[]{:S(2)}, u32[]{:S(2)}) collective-permute-start(bf16[512,256]{1,0:T(8,128)(2,1)S(1)} %collective-permute-done.16.refs_14_), channel_id=1, source_target_pairs={{0,8},{8,16},{16,24},{24,28},{28,20},{20,12},{12,4},{4,0},{1,9},{9... | collective-permute-start | bytes 786440 | tf_op jit(solution)/shard_map/ppermute | solution.py:65
  59.5 6.6 %collective-permute-start.26 = (bf16[512,256]{1,0:T(8,128)(2,1)S(1)}, bf16[512,256]{1,0:T(8,128)(2,1)S(1)}, u32[]{:S(2)}, u32[]{:S(2)}) collective-permute-start(bf16[512,256]{1,0:T(8,128)(2,1)S(1)} %collective-permute-done.25.refs_3_), channel_id=1, source_target_pairs={{8,0},{16,8},{24,16},{28,24},{20,28},{12,20},{4,12},{0,4},{9,1},{1... | collective-permute-start | bytes 786440 | tf_op jit(solution)/shard_map/ppermute | solution.py:65
  60.5 6.6 %collective-permute-start.23 = (bf16[512,256]{1,0:T(8,128)(2,1)S(1)}, bf16[512,256]{1,0:T(8,128)(2,1)S(1)}, u32[]{:S(2)}, u32[]{:S(2)}) collective-permute-start(bf16[512,256]{1,0:T(8,128)(2,1)S(1)} %collective-permute-done.21.refs_2_), channel_id=1, source_target_pairs={{0,8},{8,16},{16,24},{24,28},{28,20},{20,12},{12,4},{4,0},{1,9},{9... | collective-permute-start | bytes 786440 | tf_op jit(solution)/shard_map/ppermute | solution.py:65
  66.0 6.2 %collective-permute-start.27 = (bf16[256,256]{1,0:T(8,128)(2,1)S(1)}, bf16[256,256]{1,0:T(8,128)(2,1)S(1)}, u32[]{:S(2)}, u32[]{:S(2)}) collective-permute-start(bf16[256,256]{1,0:T(8,128)(2,1)S(1)} %slice.19), channel_id=1, source_target_pairs={{8,0},{16,8},{24,16},{28,24},{20,28},{12,20},{4,12},{0,4},{9,1},{1... | collective-permute-start | bytes 393224 | tf_op jit(solution)/shard_map/ppermute | solution.py:65
  67.1 5.1 %collective-permute-start.24 = (bf16[256,256]{1,0:T(8,128)(2,1)S(1)}, bf16[256,256]{1,0:T(8,128)(2,1)S(1)}, u32[]{:S(2)}, u32[]{:S(2)}) collective-permute-start(bf16[256,256]{1,0:T(8,128)(2,1)S(1)} %slice.18), channel_id=1, source_target_pairs={{0,8},{8,16},{16,24},{24,28},{28,20},{20,12},{12,4},{4,0},{1,9},{9... | collective-permute-start | bytes 393224 | tf_op jit(solution)/shard_map/ppermute | solution.py:65

commit v6 on v5

--- a/solution.py
+++ b/solution.py
@@ -265,8 +265,18 @@
     while tiles:
         tile = tiles.pop(0)
         if tile.shape[0] == half:
-            product = transposed_dot(left_ref[:half], tile[...])
-            product = product + transposed_dot(left_ref[half:], tiles.pop(0)[...])
+            rest = tiles.pop(0)
+            for begin in range(0, left_ref.shape[1], 2 * block):
+                rows = slice(begin, begin + 2 * block)
+                product = transposed_dot(left_ref[:half, rows], tile[...])
+                product = product + transposed_dot(left_ref[half:, rows], rest[...])
+                for t in range(each):
+                    for a in range(2):
+                        products_ref[(n * each + t) * local + begin // block + a] = product[
+                            a * block : (a + 1) * block, t * block : (t + 1) * block
+                        ]
+            n += 1
+            continue
         else:
             product = transposed_dot(left_ref[...], tile[...])
         for t in range(each):

time: 75.1 us -> 75 us (level)
  no operation moved by 1% of the time
where the time goes in v6:
time: 75 us; the launch traced here: 74.7 us
  starting transfers between devices  26.3 us (35%)
  waiting for transfers between devices  22.9 us (31%)
  Pallas kernels  18.3 us (24%)
  other arithmetic  4.75 us (6%)
  local copies, waits for them, and re-layouts  1.7 us (2%)
  between operations  0.87 us (1%)
    ppermute x8, waiting for transfers between devices, ring_step(): lax.ppermute(backward, 'row', back)  12.2 us
    ppermute x12, waiting for transfers between devices, xor_permute(): lax.ppermute(value, axis, [(i, i ^ mask) for i in range(lax.axis_size(axi...  10.2 us
    ppermute x12, starting transfers between devices, xor_permute(): lax.ppermute(value, axis, [(i, i ^ mask) for i in range(lax.axis_size(axi...  9.83 us
    pallas_call x2, Pallas kernels, dense(): call(functools.partial(dense_kernel, block, [len(p) for _, _, p in groups...  9.03 us
    ppermute x8, starting transfers between devices, ring_step(): lax.ppermute(forward, 'row', ahead)  8.6 us
    ppermute x8, starting transfers between devices, ring_step(): lax.ppermute(backward, 'row', back)  7.86 us
    mul x5, other arithmetic, staged(): return value * lax.optimization_barrier(jnp.ones((), value.dtype))  3.62 us
    pallas_call x1, Pallas kernels, factor_two(): call(functools.partial(factor_two_kernel, block, count), 'factor_two', 12...  2.78 us
  transfers between devices with their start and end apart: 28, of which 13 were waited for; matrix products, arithmetic and copies ran while one was open for 6% of the time, Pallas kernels for 21%

profile of v6, /device:TPU:0, one launch (start us, length us, event | category | flops | bytes accessed | tf_op | source)
XLA Modules:
  0.0 74.7 jit_solution(13011800108300969869)
XLA Ops:
  0.6 3.0 %collective-permute-start.1 = (bf16[128,1024]{1,0:T(8,128)(2,1)}, bf16[128,1024]{1,0:T(8,128)(2,1)S(1)}, u32[]{:S(2)}, u32[]{:S(2)}) collective-permute-start(bf16[128,1024]{1,0:T(8,128)(2,1)} %panel_ref.1), channel_id=1, source_target_pairs={{0,2},{1,3},{2,0},{3,1},{4,6},{5,7},{6,4},{7,5},{8,10},{9,11},{10,... | collective-permute-start | bytes 786440 | tf_op jit(solution)/shard_map/ppermute | solution.py:36
  3.6 1.0 %copy-done = bf16[128,1024]{1,0:T(8,128)(2,1)S(1)} copy-done((bf16[128,1024]{1,0:T(8,128)(2,1)S(1)}, bf16[128,1024]{1,0:T(8,128)(2,1)}, u32[]{:S(2)}) %copy-start) | copy-done | bytes 262168
  4.6 0.7 copy-done.1
  5.3 0.6 bridge_columns.1
  5.9 2.7 %collective-permute-start.3 = (bf16[128,512]{1,0:T(8,128)(2,1)S(1)}, bf16[128,512]{1,0:T(8,128)(2,1)S(1)}, u32[]{:S(2)}, u32[]{:S(2)}) collective-permute-start(bf16[128,512]{1,0:T(8,128)(2,1)S(1)} %bridge_columns.1), channel_id=1, source_target_pairs={{0,16},{4,20},{8,24},{12,28},{16,0},{20,4},{24,8},{28,12},{1,17},{... | collective-permute-start | bytes 393224 | tf_op jit(solution)/shard_map/ppermute | solution.py:36
  8.6 1.6 %collective-permute-done.1.refs_3_ = bf16[128,1024]{1,0:T(8,128)(2,1)S(1)} collective-permute-done((bf16[128,1024]{1,0:T(8,128)(2,1)}, bf16[128,1024]{1,0:T(8,128)(2,1)S(1)}, u32[]{:S(2)}, u32[]{:S(2)}) %collective-permute-start.1) | collective-permute-done | bytes 262176 | tf_op jit(solution)/shard_map/ppermute | solution.py:36
  10.2 1.1 %broadcast_multiply_fusion.1.refs_0_.refs_1_ = bf16[512,512]{1,0:T(8,128)(2,1)S(1)} fusion(bf16[512,512]{1,0:T(8,128)(2,1)} %param.13, bf16[]{:T(256)} %constant.164.clone.1), kind=kLoop, calls=%fused_computation.2 | loop fusion | flops 262144 | bytes 1048578 | tf_op jit(solution)/shard_map/mul | solution.py:98
  11.3 0.4 collective-permute-done.2.refs_4_
  11.7 1.6 %factor_one.1 = (bf16[512,1024]{1,0:T(8,128)(2,1)S(1)}, bf16[128,1024]{1,0:T(8,128)(2,1)}, bf16[512,256]{1,0:T(8,128)(2,1)S(1)}) custom-call(bf16[512,512]{1,0:T(8,128)(2,1)S(1)} %broadcast_multiply_fusion.1.refs_0_.refs_1_, bf16[128,1024]{1,0:T(8,128)(2,1)S(1)} %broadcast_multiply_fusion.3.refs_1_, bf16[128,1024]{1,0:T(8,128)(2,1)S(1)} %collective-permute-done.refs_2_, ...), custom_call_target="tpu_custom_call" | custom-call | bytes 1600000 | tf_op jit(solution)/shard_map/factor_one/pallas_call | solution.py:165
  13.3 2.3 %collective-permute-done.3 = bf16[128,512]{1,0:T(8,128)(2,1)S(1)} collective-permute-done((bf16[128,512]{1,0:T(8,128)(2,1)S(1)}, bf16[128,512]{1,0:T(8,128)(2,1)S(1)}, u32[]{:S(2)}, u32[]{:S(2)}) %collective-permute-start.3) | collective-permute-done | bytes 131104 | tf_op jit(solution)/shard_map/ppermute | solution.py:36
  15.6 0.8 %collective-permute-start.4 = (bf16[128,512]{1,0:T(8,128)(2,1)S(1)}, bf16[128,512]{1,0:T(8,128)(2,1)S(1)}, u32[]{:S(2)}, u32[]{:S(2)}) collective-permute-start(bf16[128,512]{1,0:T(8,128)(2,1)S(1)} %add.151), channel_id=1, source_target_pairs={{0,8},{4,12},{8,0},{12,4},{16,24},{20,28},{24,16},{28,20},{1,9},{5... | collective-permute-start | bytes 393224 | tf_op jit(solution)/shard_map/ppermute | solution.py:36
  16.4 0.5 collective-permute-start.12
  16.9 1.5 %collective-permute-start.7 = (bf16[512,256]{1,0:T(8,128)(2,1)S(1)}, bf16[512,256]{1,0:T(8,128)(2,1)S(1)}, u32[]{:S(2)}, u32[]{:S(2)}) collective-permute-start(bf16[512,256]{1,0:T(8,128)(2,1)S(1)} %get-tuple-element.30.refs_3_), channel_id=1, source_target_pairs={{8,0},{16,8},{24,16},{28,24},{20,28},{12,20},{4,12},{0,4},{9,1},{1... | collective-permute-start | bytes 786440 | tf_op jit(solution)/shard_map/ppermute | solution.py:65
  18.4 0.5 collective-permute-start.6
  18.9 2.6 %collective-permute-done.4 = bf16[128,512]{1,0:T(8,128)(2,1)S(1)} collective-permute-done((bf16[128,512]{1,0:T(8,128)(2,1)S(1)}, bf16[128,512]{1,0:T(8,128)(2,1)S(1)}, u32[]{:S(2)}, u32[]{:S(2)}) %collective-permute-start.4) | collective-permute-done | bytes 131104 | tf_op jit(solution)/shard_map/ppermute | solution.py:36
  21.6 0.7 %convert_reduce_fusion.1 = (s32[]{:T(128)}, s32[128]{0:T(128)S(1)}) fusion(s32[1,1,128]{2,1,0:T(1,128)S(1)} %copy-done.4, s32[1,1,128]{2,1,0:T(1,128)S(1)} %copy-done.5, s32[]{:T(128)S(6)} %select_n.174), kind=kLoop, calls=%fused_computation.74 | loop fusion | flops 11903 | bytes 1544 | tf_op jit(solution)/shard_map/reduce_sum | solution.py:89
  22.4 0.8 %collective-permute-start.5 = (bf16[128,512]{1,0:T(8,128)(2,1)S(1)}, bf16[128,512]{1,0:T(8,128)(2,1)S(1)}, u32[]{:S(2)}, u32[]{:S(2)}) collective-permute-start(bf16[128,512]{1,0:T(8,128)(2,1)S(1)} %add.152), channel_id=1, source_target_pairs={{0,4},{4,0},{8,12},{12,8},{16,20},{20,16},{24,28},{28,24},{1,5},{5... | collective-permute-start | bytes 393224 | tf_op jit(solution)/shard_map/ppermute | solution.py:36
  23.6 1.0 %collective-permute-done.12.refs_10_.refs_6_ = bf16[128,1024]{1,0:T(8,128)(2,1)S(1)} collective-permute-done((bf16[128,1024]{1,0:T(8,128)(2,1)}, bf16[128,1024]{1,0:T(8,128)(2,1)S(1)}, u32[]{:S(2)}, u32[]{:S(2)}) %collective-permute-start.12) | collective-permute-done | bytes 262176 | tf_op jit(solution)/shard_map/ppermute | solution.py:36
  24.6 1.8 %collective-permute-done.7.refs_5_ = bf16[512,256]{1,0:T(8,128)(2,1)S(1)} collective-permute-done((bf16[512,256]{1,0:T(8,128)(2,1)S(1)}, bf16[512,256]{1,0:T(8,128)(2,1)S(1)}, u32[]{:S(2)}, u32[]{:S(2)}) %collective-permute-start.7) | collective-permute-done | bytes 262176 | tf_op jit(solution)/shard_map/ppermute | solution.py:65
  26.4 1.1 %collective-permute-start.15 = (bf16[512,256]{1,0:T(8,128)(2,1)S(1)}, bf16[512,256]{1,0:T(8,128)(2,1)S(1)}, u32[]{:S(2)}, u32[]{:S(2)}) collective-permute-start(bf16[512,256]{1,0:T(8,128)(2,1)S(1)} %collective-permute-done.7.refs_5_), channel_id=1, source_target_pairs={{8,0},{16,8},{24,16},{28,24},{20,28},{12,20},{4,12},{0,4},{9,1},{1... | collective-permute-start | bytes 786440 | tf_op jit(solution)/shard_map/ppermute | solution.py:65
  27.6 0.8 %collective-permute-start.14 = (bf16[512,256]{1,0:T(8,128)(2,1)S(1)}, bf16[512,256]{1,0:T(8,128)(2,1)S(1)}, u32[]{:S(2)}, u32[]{:S(2)}) collective-permute-start(bf16[512,256]{1,0:T(8,128)(2,1)S(1)} %collective-permute-done.6.refs_4_), channel_id=1, source_target_pairs={{0,8},{8,16},{16,24},{24,28},{28,20},{20,12},{12,4},{4,0},{1,9},{9... | collective-permute-start | bytes 786440 | tf_op jit(solution)/shard_map/ppermute | solution.py:65
  28.4 1.3 %collective-permute-done.5 = bf16[128,512]{1,0:T(8,128)(2,1)S(1)} collective-permute-done((bf16[128,512]{1,0:T(8,128)(2,1)S(1)}, bf16[128,512]{1,0:T(8,128)(2,1)S(1)}, u32[]{:S(2)}, u32[]{:S(2)}) %collective-permute-start.5) | collective-permute-done | bytes 131104 | tf_op jit(solution)/shard_map/ppermute | solution.py:36
  29.7 1.6 %collective-permute-start.9 = (bf16[128,512]{1,0:T(8,128)(2,1)S(1)}, bf16[128,512]{1,0:T(8,128)(2,1)S(1)}, u32[]{:S(2)}, u32[]{:S(2)}) collective-permute-start(bf16[128,512]{1,0:T(8,128)(2,1)S(1)} %add.167.refs_4_), channel_id=1, source_target_pairs={{0,2},{1,3},{2,0},{3,1},{4,6},{5,7},{6,4},{7,5},{8,10},{9,11},{10,... | collective-permute-start | bytes 393224 | tf_op jit(solution)/shard_map/ppermute | solution.py:36
  31.3 2.5 %multiply_bitcast_fusion.refs_16_ = bf16[128,128,128]{2,1,0:T(8,128)(2,1)S(1)} fusion(bf16[1,1,128,128,128]{4,3,2,1,0:T(8,128)(2,1)} %param.17, bf16[]{:T(256)} %constant.164.clone.1), kind=kLoop, calls=%fused_computation | loop fusion | flops 2097152 | bytes 8388610 | tf_op jit(solution)/shard_map/mul | solution.py:98
  33.7 1.0 %collective-permute-done.9.refs_6_ = bf16[128,512]{1,0:T(8,128)(2,1)S(1)} collective-permute-done((bf16[128,512]{1,0:T(8,128)(2,1)S(1)}, bf16[128,512]{1,0:T(8,128)(2,1)S(1)}, u32[]{:S(2)}, u32[]{:S(2)}) %collective-permute-start.9) | collective-permute-done | bytes 131104 | tf_op jit(solution)/shard_map/ppermute | solution.py:36
  34.8 0.5 collective-permute-start.10
  35.3 0.7 collective-permute-start.19
  35.9 1.4 %collective-permute-start.17 = (bf16[512,256]{1,0:T(8,128)(2,1)S(1)}, bf16[512,256]{1,0:T(8,128)(2,1)S(1)}, u32[]{:S(2)}, u32[]{:S(2)}) collective-permute-start(bf16[512,256]{1,0:T(8,128)(2,1)S(1)} %collective-permute-done.14.refs_6_), channel_id=1, source_target_pairs={{0,8},{8,16},{16,24},{24,28},{28,20},{20,12},{12,4},{4,0},{1,9},{9... | collective-permute-start | bytes 786440 | tf_op jit(solution)/shard_map/ppermute | solution.py:65
  37.3 1.8 %tile_two.1 = (bf16[512,256]{1,0:T(8,128)(2,1)S(1)}, bf16[512,512]{1,0:T(8,128)(2,1)S(1)}) custom-call(s32[8]{0:T(128)S(1)} %and_select_fusion.16.refs_0_, bf16[512,512]{1,0:T(8,128)(2,1)S(1)} %broadcast_multiply_fusion.1.refs_0_.refs_1_, bf16[512,512]{1,0:T(8,128)(2,1)S(1)} %broadcast_multiply_fusion.refs_2_.refs_1_, ...), custom_call_target="tpu_custom_call" | custom-call | bytes 1600000 | tf_op jit(solution)/shard_map/tile_two/pallas_call | solution.py:204
  39.1 0.7 collective-permute-start.22
  39.8 1.4 %collective-permute-start.16 = (bf16[512,256]{1,0:T(8,128)(2,1)S(1)}, bf16[512,256]{1,0:T(8,128)(2,1)S(1)}, u32[]{:S(2)}, u32[]{:S(2)}) collective-permute-start(bf16[512,256]{1,0:T(8,128)(2,1)S(1)} %get-tuple-element.48.refs_13_), channel_id=1, source_target_pairs={{0,8},{8,16},{16,24},{24,28},{28,20},{20,12},{12,4},{4,0},{1,9},{9... | collective-permute-start | bytes 786440 | tf_op jit(solution)/shard_map/ppermute | solution.py:65
  41.2 3.3 %collective-permute-done.19.refs_9_ = bf16[512,256]{1,0:T(8,128)(2,1)S(1)} collective-permute-done((bf16[512,256]{1,0:T(8,128)(2,1)S(1)}, bf16[512,256]{1,0:T(8,128)(2,1)S(1)}, u32[]{:S(2)}, u32[]{:S(2)}) %collective-permute-start.19) | collective-permute-done | bytes 262176 | tf_op jit(solution)/shard_map/ppermute | solution.py:65
  44.5 0.7 collective-permute-start.20
  45.2 1.4 %collective-permute-start.18 = (bf16[256,256]{1,0:T(8,128)(2,1)S(1)}, bf16[256,256]{1,0:T(8,128)(2,1)S(1)}, u32[]{:S(2)}, u32[]{:S(2)}) collective-permute-start(bf16[256,256]{1,0:T(8,128)(2,1)S(1)} %slice.16), channel_id=1, source_target_pairs={{0,8},{8,16},{16,24},{24,28},{28,20},{20,12},{12,4},{4,0},{1,9},{9... | collective-permute-start | bytes 393224 | tf_op jit(solution)/shard_map/ppermute | solution.py:65
  46.6 2.8 %factor_two.1 = (bf16[512,1024]{1,0:T(8,128)(2,1)S(1)}, bf16[128,1024]{1,0:T(8,128)(2,1)}) custom-call(s32[8]{0:T(128)S(1)} %and_select_fusion.16.refs_0_, bf16[512,512]{1,0:T(8,128)(2,1)S(1)} %broadcast_multiply_fusion.refs_2_.refs_1_, bf16[512,1024]{1,0:T(8,128)(2,1)S(1)} %get-tuple-element.34.refs_3_.refs_2_, ...), custom_call_target="tpu_custom_call" | custom-call | bytes 2400000 | tf_op jit(solution)/shard_map/factor_two/pallas_call | solution.py:244
  49.4 0.7 collective-permute-done.22.refs_15_
  50.1 1.9 %collective-permute-done.20.refs_11_ = bf16[256,256]{1,0:T(8,128)(2,1)S(1)} collective-permute-done((bf16[256,256]{1,0:T(8,128)(2,1)S(1)}, bf16[256,256]{1,0:T(8,128)(2,1)S(1)}, u32[]{:S(2)}, u32[]{:S(2)}) %collective-permute-start.20) | collective-permute-done | bytes 131104 | tf_op jit(solution)/shard_map/ppermute | solution.py:65
  52.0 0.4 collective-permute-done.18.refs_10_
  52.4 1.0 %collective-permute-start.25 = (bf16[512,256]{1,0:T(8,128)(2,1)S(1)}, bf16[512,256]{1,0:T(8,128)(2,1)S(1)}, u32[]{:S(2)}, u32[]{:S(2)}) collective-permute-start(bf16[512,256]{1,0:T(8,128)(2,1)S(1)} %collective-permute-done.22.refs_15_), channel_id=1, source_target_pairs={{8,0},{16,8},{24,16},{28,24},{20,28},{12,20},{4,12},{0,4},{9,1},{1... | collective-permute-start | bytes 786440 | tf_op jit(solution)/shard_map/ppermute | solution.py:65
  53.4 1.0 %collective-permute-start.21 = (bf16[512,256]{1,0:T(8,128)(2,1)S(1)}, bf16[512,256]{1,0:T(8,128)(2,1)S(1)}, u32[]{:S(2)}, u32[]{:S(2)}) collective-permute-start(bf16[512,256]{1,0:T(8,128)(2,1)S(1)} %collective-permute-done.16.refs_14_), channel_id=1, source_target_pairs={{0,8},{8,16},{16,24},{24,28},{28,20},{20,12},{12,4},{4,0},{1,9},{9... | collective-permute-start | bytes 786440 | tf_op jit(solution)/shard_map/ppermute | solution.py:65
  54.4 5.0 %dense.2.refs_6_.refs_2_ = bf16[128,128,128]{2,1,0:T(8,128)(2,1)S(1)} custom-call(s32[128]{0:T(128)S(1)} %fusion.2.refs_0_, s32[128]{0:T(128)S(1)} %get-tuple-element.61.refs_1_, bf16[512,1024]{1,0:T(8,128)(2,1)S(1)} %get-tuple-element.34.refs_3_.refs_2_, bf16[512,256]{1,0:T(8,128)(2,1)S(1)} %get-tuple-element.30.refs_3_, ...), custom_call_target="tpu_custom_call" | custom-call | bytes 5000000 | tf_op jit(solution)/shard_map/dense/pallas_call | solution.py:333
  59.5 1.0 %collective-permute-start.26 = (bf16[512,256]{1,0:T(8,128)(2,1)S(1)}, bf16[512,256]{1,0:T(8,128)(2,1)S(1)}, u32[]{:S(2)}, u32[]{:S(2)}) collective-permute-start(bf16[512,256]{1,0:T(8,128)(2,1)S(1)} %collective-permute-done.25.refs_3_), channel_id=1, source_target_pairs={{8,0},{16,8},{24,16},{28,24},{20,28},{12,20},{4,12},{0,4},{9,1},{1... | collective-permute-start | bytes 786440 | tf_op jit(solution)/shard_map/ppermute | solution.py:65
  60.5 1.0 %collective-permute-start.23 = (bf16[512,256]{1,0:T(8,128)(2,1)S(1)}, bf16[512,256]{1,0:T(8,128)(2,1)S(1)}, u32[]{:S(2)}, u32[]{:S(2)}) collective-permute-start(bf16[512,256]{1,0:T(8,128)(2,1)S(1)} %collective-permute-done.21.refs_2_), channel_id=1, source_target_pairs={{0,8},{8,16},{16,24},{24,28},{28,20},{20,12},{12,4},{4,0},{1,9},{9... | collective-permute-start | bytes 786440 | tf_op jit(solution)/shard_map/ppermute | solution.py:65
  61.5 4.5 %collective-permute-done.26.refs_5_ = bf16[512,256]{1,0:T(8,128)(2,1)S(1)} collective-permute-done((bf16[512,256]{1,0:T(8,128)(2,1)S(1)}, bf16[512,256]{1,0:T(8,128)(2,1)S(1)}, u32[]{:S(2)}, u32[]{:S(2)}) %collective-permute-start.26) | collective-permute-done | bytes 262176 | tf_op jit(solution)/shard_map/ppermute | solution.py:65
  66.0 1.0 %collective-permute-start.27 = (bf16[256,256]{1,0:T(8,128)(2,1)S(1)}, bf16[256,256]{1,0:T(8,128)(2,1)S(1)}, u32[]{:S(2)}, u32[]{:S(2)}) collective-permute-start(bf16[256,256]{1,0:T(8,128)(2,1)S(1)} %slice.19), channel_id=1, source_target_pairs={{8,0},{16,8},{24,16},{28,24},{20,28},{12,20},{4,12},{0,4},{9,1},{1... | collective-permute-start | bytes 393224 | tf_op jit(solution)/shard_map/ppermute | solution.py:65
  67.1 1.1 %collective-permute-start.24 = (bf16[256,256]{1,0:T(8,128)(2,1)S(1)}, bf16[256,256]{1,0:T(8,128)(2,1)S(1)}, u32[]{:S(2)}, u32[]{:S(2)}) collective-permute-start(bf16[256,256]{1,0:T(8,128)(2,1)S(1)} %slice.18), channel_id=1, source_target_pairs={{0,8},{8,16},{16,24},{24,28},{28,20},{20,12},{12,4},{4,0},{1,9},{9... | collective-permute-start | bytes 393224 | tf_op jit(solution)/shard_map/ppermute | solution.py:65
  68.2 4.0 %dense.3.refs_3_ = bf16[128,128,128]{2,1,0:T(8,128)(2,1)} custom-call(s32[128]{0:T(128)S(1)} %get-tuple-element.60.refs_0_, bf16[512,1024]{1,0:T(8,128)(2,1)S(1)} %get-tuple-element.46.refs_12_.refs_1_.left_ref, bf16[512,256]{1,0:T(8,128)(2,1)S(1)} %collective-permute-done.21.refs_2_, bf16[512,256]{1,0:T(8,128)(2,1)S(1)} %collective-permute-done.25.refs_3_, ...), custom_call_target="tpu_custom_call" | custom-call | bytes 5000000 | tf_op jit(solution)/shard_map/dense/pallas_call | solution.py:333
  72.2 2.5 %last.1 = bf16[128,128,128]{2,1,0:T(8,128)(2,1)} custom-call(s32[128]{0:T(128)S(1)} %get-tuple-element.56.slots_ref, s32[128]{0:T(128)S(1)} %get-tuple-element.55.places_ref, s32[1]{0:T(128)} %bitcast.4.count_ref, bf16[512,1024]{1,0:T(8,128)(2,1)S(1)} %get-tuple-element.46.refs_12_.refs_1_.left_ref, ...), custom_call_target="tpu_custom_call", output_to_operand_aliasing={{}: (7, {})} | custom-call | bytes 3000000 | tf_op jit(solution)/shard_map/last/pallas_call | solution.py:373
  (52 shorter events, 0.7 us)
Async XLA Ops:
  0.6 9.5 %collective-permute-start.1 = (bf16[128,1024]{1,0:T(8,128)(2,1)}, bf16[128,1024]{1,0:T(8,128)(2,1)S(1)}, u32[]{:S(2)}, u32[]{:S(2)}) collective-permute-start(bf16[128,1024]{1,0:T(8,128)(2,1)} %panel_ref.1), channel_id=1, source_target_pairs={{0,2},{1,3},{2,0},{3,1},{4,6},{5,7},{6,4},{7,5},{8,10},{9,11},{10,... | collective-permute-start | bytes 786440 | tf_op jit(solution)/shard_map/ppermute | solution.py:36
  3.6 7.6 %collective-permute-start = (bf16[128,1024]{1,0:T(8,128)(2,1)}, bf16[128,1024]{1,0:T(8,128)(2,1)S(1)}, u32[]{:S(2)}, u32[]{:S(2)}) collective-permute-start(bf16[128,1024]{1,0:T(8,128)(2,1)} %panel_ref.1), channel_id=1, source_target_pairs={{0,1},{1,0},{2,3},{3,2},{4,5},{5,4},{6,7},{7,6},{8,9},{9,8},{10,11... | collective-permute-start | bytes 786440 | tf_op jit(solution)/shard_map/ppermute | solution.py:36
  3.6 1.0 %copy-start = (bf16[128,1024]{1,0:T(8,128)(2,1)S(1)}, bf16[128,1024]{1,0:T(8,128)(2,1)}, u32[]{:S(2)}) copy-start(bf16[128,1024]{1,0:T(8,128)(2,1)} %panel_ref.1) | copy-start | bytes 786436
  4.6 0.7 copy-start.1
  5.3 16.3 %copy-start.4 = (s32[1,1,128]{2,1,0:T(1,128)S(1)}, s32[1,1,128]{2,1,0:T(1,128)}, u32[]{:S(2)}) copy-start(s32[1,1,128]{2,1,0:T(1,128)} %param.20) | copy-start | bytes 1540
  5.3 16.3 %copy-start.5 = (s32[1,1,128]{2,1,0:T(1,128)S(1)}, s32[1,1,128]{2,1,0:T(1,128)}, u32[]{:S(2)}) copy-start(s32[1,1,128]{2,1,0:T(1,128)} %param.21) | copy-start | bytes 1540
  5.3 17.9 %copy-start.3 = (bf16[128,1024]{1,0:T(8,128)(2,1)S(1)}, bf16[128,1024]{1,0:T(8,128)(2,1)}, u32[]{:S(2)}) copy-start(bf16[128,1024]{1,0:T(8,128)(2,1)} %param.12) | copy-start | bytes 786436
  5.3 17.9 %copy-start.2 = (bf16[512,512]{1,0:T(8,128)(2,1)S(1)}, bf16[512,512]{1,0:T(8,128)(2,1)}, u32[]{:S(2)}) copy-start(bf16[512,512]{1,0:T(8,128)(2,1)} %param.14) | copy-start | bytes 1572868
  5.3 18.0 %copy-start.6 = (s32[1,1,128]{2,1,0:T(1,128)S(1)}, s32[1,1,128]{2,1,0:T(1,128)}, u32[]{:S(2)}) copy-start(s32[1,1,128]{2,1,0:T(1,128)} %param.18) | copy-start | bytes 1540
  5.3 18.0 %copy-start.7 = (s32[1,1,128]{2,1,0:T(1,128)S(1)}, s32[1,1,128]{2,1,0:T(1,128)}, u32[]{:S(2)}) copy-start(s32[1,1,128]{2,1,0:T(1,128)} %param.19) | copy-start | bytes 1540
  5.3 18.0 %copy-start.8 = (s32[8]{0:T(128)S(1)}, s32[8]{0:T(128)}, u32[]{:S(2)}) copy-start(s32[8]{0:T(128)} %param.16) | copy-start | bytes 100
  5.9 9.7 %collective-permute-start.3 = (bf16[128,512]{1,0:T(8,128)(2,1)S(1)}, bf16[128,512]{1,0:T(8,128)(2,1)S(1)}, u32[]{:S(2)}, u32[]{:S(2)}) collective-permute-start(bf16[128,512]{1,0:T(8,128)(2,1)S(1)} %bridge_columns.1), channel_id=1, source_target_pairs={{0,16},{4,20},{8,24},{12,28},{16,0},{20,4},{24,8},{28,12},{1,17},{... | collective-permute-start | bytes 393224 | tf_op jit(solution)/shard_map/ppermute | solution.py:36
  10.2 1.5 %collective-permute-start.2 = (bf16[128,1024]{1,0:T(8,128)(2,1)S(1)}, bf16[128,1024]{1,0:T(8,128)(2,1)S(1)}, u32[]{:S(2)}, u32[]{:S(2)}) collective-permute-start(bf16[128,1024]{1,0:T(8,128)(2,1)S(1)} %collective-permute-done.1.refs_3_), channel_id=1, source_target_pairs={{0,1},{1,0},{2,3},{3,2},{4,5},{5,4},{6,7},{7,6},{8,9},{9,8},{10,11... | collective-permute-start | bytes 786440 | tf_op jit(solution)/shard_map/ppermute | solution.py:36
  15.6 6.0 %collective-permute-start.4 = (bf16[128,512]{1,0:T(8,128)(2,1)S(1)}, bf16[128,512]{1,0:T(8,128)(2,1)S(1)}, u32[]{:S(2)}, u32[]{:S(2)}) collective-permute-start(bf16[128,512]{1,0:T(8,128)(2,1)S(1)} %add.151), channel_id=1, source_target_pairs={{0,8},{4,12},{8,0},{12,4},{16,24},{20,28},{24,16},{28,20},{1,9},{5... | collective-permute-start | bytes 393224 | tf_op jit(solution)/shard_map/ppermute | solution.py:36
  16.4 8.2 %collective-permute-start.12 = (bf16[128,1024]{1,0:T(8,128)(2,1)}, bf16[128,1024]{1,0:T(8,128)(2,1)S(1)}, u32[]{:S(2)}, u32[]{:S(2)}) collective-permute-start(bf16[128,1024]{1,0:T(8,128)(2,1)} %param.12), channel_id=1, source_target_pairs={{0,2},{1,3},{2,0},{3,1},{4,6},{5,7},{6,4},{7,5},{8,10},{9,11},{10,... | collective-permute-start | bytes 786440 | tf_op jit(solution)/shard_map/ppermute | solution.py:36
  16.9 17.9 %collective-permute-start.11 = (bf16[128,1024]{1,0:T(8,128)(2,1)}, bf16[128,1024]{1,0:T(8,128)(2,1)S(1)}, u32[]{:S(2)}, u32[]{:S(2)}) collective-permute-start(bf16[128,1024]{1,0:T(8,128)(2,1)} %param.12), channel_id=1, source_target_pairs={{0,1},{1,0},{2,3},{3,2},{4,5},{5,4},{6,7},{7,6},{8,9},{9,8},{10,11... | collective-permute-start | bytes 786440 | tf_op jit(solution)/shard_map/ppermute | solution.py:36
  16.9 9.5 %collective-permute-start.7 = (bf16[512,256]{1,0:T(8,128)(2,1)S(1)}, bf16[512,256]{1,0:T(8,128)(2,1)S(1)}, u32[]{:S(2)}, u32[]{:S(2)}) collective-permute-start(bf16[512,256]{1,0:T(8,128)(2,1)S(1)} %get-tuple-element.30.refs_3_), channel_id=1, source_target_pairs={{8,0},{16,8},{24,16},{28,24},{20,28},{12,20},{4,12},{0,4},{9,1},{1... | collective-permute-start | bytes 786440 | tf_op jit(solution)/shard_map/ppermute | solution.py:65
  18.4 9.1 %collective-permute-start.6 = (bf16[512,256]{1,0:T(8,128)(2,1)S(1)}, bf16[512,256]{1,0:T(8,128)(2,1)S(1)}, u32[]{:S(2)}, u32[]{:S(2)}) collective-permute-start(bf16[512,256]{1,0:T(8,128)(2,1)S(1)} %get-tuple-element.30.refs_3_), channel_id=1, source_target_pairs={{0,8},{8,16},{16,24},{24,28},{28,20},{20,12},{12,4},{4,0},{1,9},{9... | collective-permute-start | bytes 786440 | tf_op jit(solution)/shard_map/ppermute | solution.py:65
  22.4 7.3 %collective-permute-start.5 = (bf16[128,512]{1,0:T(8,128)(2,1)S(1)}, bf16[128,512]{1,0:T(8,128)(2,1)S(1)}, u32[]{:S(2)}, u32[]{:S(2)}) collective-permute-start(bf16[128,512]{1,0:T(8,128)(2,1)S(1)} %add.152), channel_id=1, source_target_pairs={{0,4},{4,0},{8,12},{12,8},{16,20},{20,16},{24,28},{28,24},{1,5},{5... | collective-permute-start | bytes 393224 | tf_op jit(solution)/shard_map/ppermute | solution.py:36
  24.6 12.7 %collective-permute-start.13 = (bf16[128,1024]{1,0:T(8,128)(2,1)S(1)}, bf16[128,1024]{1,0:T(8,128)(2,1)S(1)}, u32[]{:S(2)}, u32[]{:S(2)}) collective-permute-start(bf16[128,1024]{1,0:T(8,128)(2,1)S(1)} %collective-permute-done.12.refs_10_.refs_6_), channel_id=1, source_target_pairs={{0,1},{1,0},{2,3},{3,2},{4,5},{5,4},{6,7},{7,6},{8,9},{9,8},{10,11... | collective-permute-start | bytes 786440 | tf_op jit(solution)/shard_map/ppermute | solution.py:36
  26.4 8.9 %collective-permute-start.15 = (bf16[512,256]{1,0:T(8,128)(2,1)S(1)}, bf16[512,256]{1,0:T(8,128)(2,1)S(1)}, u32[]{:S(2)}, u32[]{:S(2)}) collective-permute-start(bf16[512,256]{1,0:T(8,128)(2,1)S(1)} %collective-permute-done.7.refs_5_), channel_id=1, source_target_pairs={{8,0},{16,8},{24,16},{28,24},{20,28},{12,20},{4,12},{0,4},{9,1},{1... | collective-permute-start | bytes 786440 | tf_op jit(solution)/shard_map/ppermute | solution.py:65
  27.6 8.4 %collective-permute-start.14 = (bf16[512,256]{1,0:T(8,128)(2,1)S(1)}, bf16[512,256]{1,0:T(8,128)(2,1)S(1)}, u32[]{:S(2)}, u32[]{:S(2)}) collective-permute-start(bf16[512,256]{1,0:T(8,128)(2,1)S(1)} %collective-permute-done.6.refs_4_), channel_id=1, source_target_pairs={{0,8},{8,16},{16,24},{24,28},{28,20},{20,12},{12,4},{4,0},{1,9},{9... | collective-permute-start | bytes 786440 | tf_op jit(solution)/shard_map/ppermute | solution.py:65
  29.7 5.0 %collective-permute-start.9 = (bf16[128,512]{1,0:T(8,128)(2,1)S(1)}, bf16[128,512]{1,0:T(8,128)(2,1)S(1)}, u32[]{:S(2)}, u32[]{:S(2)}) collective-permute-start(bf16[128,512]{1,0:T(8,128)(2,1)S(1)} %add.167.refs_4_), channel_id=1, source_target_pairs={{0,2},{1,3},{2,0},{3,1},{4,6},{5,7},{6,4},{7,5},{8,10},{9,11},{10,... | collective-permute-start | bytes 393224 | tf_op jit(solution)/shard_map/ppermute | solution.py:36
  34.8 2.6 %collective-permute-start.8 = (bf16[128,512]{1,0:T(8,128)(2,1)S(1)}, bf16[128,512]{1,0:T(8,128)(2,1)S(1)}, u32[]{:S(2)}, u32[]{:S(2)}) collective-permute-start(bf16[128,512]{1,0:T(8,128)(2,1)S(1)} %add.167.refs_4_), channel_id=1, source_target_pairs={{0,1},{1,0},{2,3},{3,2},{4,5},{5,4},{6,7},{7,6},{8,9},{9,8},{10,11... | collective-permute-start | bytes 393224 | tf_op jit(solution)/shard_map/ppermute | solution.py:36
  34.8 2.6 %collective-permute-start.10 = (bf16[128,512]{1,0:T(8,128)(2,1)S(1)}, bf16[128,512]{1,0:T(8,128)(2,1)S(1)}, u32[]{:S(2)}, u32[]{:S(2)}) collective-permute-start(bf16[128,512]{1,0:T(8,128)(2,1)S(1)} %collective-permute-done.9.refs_6_), channel_id=1, source_target_pairs={{0,1},{1,0},{2,3},{3,2},{4,5},{5,4},{6,7},{7,6},{8,9},{9,8},{10,11... | collective-permute-start | bytes 393224 | tf_op jit(solution)/shard_map/ppermute | solution.py:36
  35.3 9.2 %collective-permute-start.19 = (bf16[512,256]{1,0:T(8,128)(2,1)S(1)}, bf16[512,256]{1,0:T(8,128)(2,1)S(1)}, u32[]{:S(2)}, u32[]{:S(2)}) collective-permute-start(bf16[512,256]{1,0:T(8,128)(2,1)S(1)} %collective-permute-done.15.refs_7_), channel_id=1, source_target_pairs={{8,0},{16,8},{24,16},{28,24},{20,28},{12,20},{4,12},{0,4},{9,1},{1... | collective-permute-start | bytes 786440 | tf_op jit(solution)/shard_map/ppermute | solution.py:65
  35.9 9.2 %collective-permute-start.17 = (bf16[512,256]{1,0:T(8,128)(2,1)S(1)}, bf16[512,256]{1,0:T(8,128)(2,1)S(1)}, u32[]{:S(2)}, u32[]{:S(2)}) collective-permute-start(bf16[512,256]{1,0:T(8,128)(2,1)S(1)} %collective-permute-done.14.refs_6_), channel_id=1, source_target_pairs={{0,8},{8,16},{16,24},{24,28},{28,20},{20,12},{12,4},{4,0},{1,9},{9... | collective-permute-start | bytes 786440 | tf_op jit(solution)/shard_map/ppermute | solution.py:65
  39.1 11.0 %collective-permute-start.22 = (bf16[512,256]{1,0:T(8,128)(2,1)S(1)}, bf16[512,256]{1,0:T(8,128)(2,1)S(1)}, u32[]{:S(2)}, u32[]{:S(2)}) collective-permute-start(bf16[512,256]{1,0:T(8,128)(2,1)S(1)} %get-tuple-element.48.refs_13_), channel_id=1, source_target_pairs={{8,0},{16,8},{24,16},{28,24},{20,28},{12,20},{4,12},{0,4},{9,1},{1... | collective-permute-start | bytes 786440 | tf_op jit(solution)/shard_map/ppermute | solution.py:65
  39.8 13.6 %collective-permute-start.16 = (bf16[512,256]{1,0:T(8,128)(2,1)S(1)}, bf16[512,256]{1,0:T(8,128)(2,1)S(1)}, u32[]{:S(2)}, u32[]{:S(2)}) collective-permute-start(bf16[512,256]{1,0:T(8,128)(2,1)S(1)} %get-tuple-element.48.refs_13_), channel_id=1, source_target_pairs={{0,8},{8,16},{16,24},{24,28},{28,20},{20,12},{12,4},{4,0},{1,9},{9... | collective-permute-start | bytes 786440 | tf_op jit(solution)/shard_map/ppermute | solution.py:65
  44.5 7.5 %collective-permute-start.20 = (bf16[256,256]{1,0:T(8,128)(2,1)S(1)}, bf16[256,256]{1,0:T(8,128)(2,1)S(1)}, u32[]{:S(2)}, u32[]{:S(2)}) collective-permute-start(bf16[256,256]{1,0:T(8,128)(2,1)S(1)} %slice.17), channel_id=1, source_target_pairs={{8,0},{16,8},{24,16},{28,24},{20,28},{12,20},{4,12},{0,4},{9,1},{1... | collective-permute-start | bytes 393224 | tf_op jit(solution)/shard_map/ppermute | solution.py:65
  45.2 7.2 %collective-permute-start.18 = (bf16[256,256]{1,0:T(8,128)(2,1)S(1)}, bf16[256,256]{1,0:T(8,128)(2,1)S(1)}, u32[]{:S(2)}, u32[]{:S(2)}) collective-permute-start(bf16[256,256]{1,0:T(8,128)(2,1)S(1)} %slice.16), channel_id=1, source_target_pairs={{0,8},{8,16},{16,24},{24,28},{28,20},{20,12},{12,4},{4,0},{1,9},{9... | collective-permute-start | bytes 393224 | tf_op jit(solution)/shard_map/ppermute | solution.py:65
  52.4 7.1 %collective-permute-start.25 = (bf16[512,256]{1,0:T(8,128)(2,1)S(1)}, bf16[512,256]{1,0:T(8,128)(2,1)S(1)}, u32[]{:S(2)}, u32[]{:S(2)}) collective-permute-start(bf16[512,256]{1,0:T(8,128)(2,1)S(1)} %collective-permute-done.22.refs_15_), channel_id=1, source_target_pairs={{8,0},{16,8},{24,16},{28,24},{20,28},{12,20},{4,12},{0,4},{9,1},{1... | collective-permute-start | bytes 786440 | tf_op jit(solution)/shard_map/ppermute | solution.py:65
  53.4 7.1 %collective-permute-start.21 = (bf16[512,256]{1,0:T(8,128)(2,1)S(1)}, bf16[512,256]{1,0:T(8,128)(2,1)S(1)}, u32[]{:S(2)}, u32[]{:S(2)}) collective-permute-start(bf16[512,256]{1,0:T(8,128)(2,1)S(1)} %collective-permute-done.16.refs_14_), channel_id=1, source_target_pairs={{0,8},{8,16},{16,24},{24,28},{28,20},{20,12},{12,4},{4,0},{1,9},{9... | collective-permute-start | bytes 786440 | tf_op jit(solution)/shard_map/ppermute | solution.py:65
  59.5 6.6 %collective-permute-start.26 = (bf16[512,256]{1,0:T(8,128)(2,1)S(1)}, bf16[512,256]{1,0:T(8,128)(2,1)S(1)}, u32[]{:S(2)}, u32[]{:S(2)}) collective-permute-start(bf16[512,256]{1,0:T(8,128)(2,1)S(1)} %collective-permute-done.25.refs_3_), channel_id=1, source_target_pairs={{8,0},{16,8},{24,16},{28,24},{20,28},{12,20},{4,12},{0,4},{9,1},{1... | collective-permute-start | bytes 786440 | tf_op jit(solution)/shard_map/ppermute | solution.py:65
  60.5 6.6 %collective-permute-start.23 = (bf16[512,256]{1,0:T(8,128)(2,1)S(1)}, bf16[512,256]{1,0:T(8,128)(2,1)S(1)}, u32[]{:S(2)}, u32[]{:S(2)}) collective-permute-start(bf16[512,256]{1,0:T(8,128)(2,1)S(1)} %collective-permute-done.21.refs_2_), channel_id=1, source_target_pairs={{0,8},{8,16},{16,24},{24,28},{28,20},{20,12},{12,4},{4,0},{1,9},{9... | collective-permute-start | bytes 786440 | tf_op jit(solution)/shard_map/ppermute | solution.py:65
  66.0 6.2 %collective-permute-start.27 = (bf16[256,256]{1,0:T(8,128)(2,1)S(1)}, bf16[256,256]{1,0:T(8,128)(2,1)S(1)}, u32[]{:S(2)}, u32[]{:S(2)}) collective-permute-start(bf16[256,256]{1,0:T(8,128)(2,1)S(1)} %slice.19), channel_id=1, source_target_pairs={{8,0},{16,8},{24,16},{28,24},{20,28},{12,20},{4,12},{0,4},{9,1},{1... | collective-permute-start | bytes 393224 | tf_op jit(solution)/shard_map/ppermute | solution.py:65
  67.1 5.1 %collective-permute-start.24 = (bf16[256,256]{1,0:T(8,128)(2,1)S(1)}, bf16[256,256]{1,0:T(8,128)(2,1)S(1)}, u32[]{:S(2)}, u32[]{:S(2)}) collective-permute-start(bf16[256,256]{1,0:T(8,128)(2,1)S(1)} %slice.18), channel_id=1, source_target_pairs={{0,8},{8,16},{16,24},{24,28},{28,20},{20,12},{12,4},{4,0},{1,9},{9... | collective-permute-start | bytes 393224 | tf_op jit(solution)/shard_map/ppermute | solution.py:65
